TPU v7x, 256 devices: a whole 4x4x8 slice. The times are simulated.
256 devices in a mesh: sec: 64 (over z, x, core), pair: 4 (over y).
Axes of the slice: x: 4, y: 4, z: 8, core: 2. Of those that a mesh axis runs over, the one named last changes fastest.
Arguments:
- psi_start: float32 [64, 16, 128, 128], P('sec', 'pair'), may hold values from -6 to 6
- left_env: float32 [6, 64, 128, 128], P(None, 'sec')
- right_env: float32 [6, 16, 128, 128], P(None, 'pair')
- mpo_coef: float32 [6, 16, 16], replicated, may hold values from -0.625 to 0.625
- mpo_pattern: int32 [6, 16, 16], replicated, may hold values 0 or 1
- sector_shift: int32 [6], replicated, may hold values from -1 to 1, as said below
- block_rows: int32 [64], P('sec'), may hold values from 64 to 128, as said below
Outputs:
- state: float32 [64, 16, 128, 128], P('sec', 'pair')
- energies: float32 [4], replicated
Inputs may be any that keep to these rules, and one draw needn't show every extreme that they name: `sector_shift`: each of -1, 0 and 1 occurs at least once. `block_rows`: some sector has all 128 rows.
All inputs are finite; a program needn't handle non-finite values.
Results may differ from a plain program's by a relative error of at most 0.0013.
Values sent between devices are 32-bit elements; how exact they have to be, the bound alone decides.
No kernel may reach another device: no remote copies, remote signals or barrier semaphores. Data moves between devices by JAX's collectives and lax.ppermute only.
A program may use at most 192 MiB of HBM per device.

v0:
```python
import functools

import jax
import jax.numpy as jnp
from jax import lax
from jax.experimental import pallas as pl
from jax.experimental.pallas import tpu as pltpu
from jax.sharding import PartitionSpec as P

ITERS = 4
TERMS = 6
LOCAL = 4
GROUPS = 4
B = 128
PACK = LOCAL * B + 8

f32 = jnp.float32
bf16 = jnp.bfloat16
VM = pl.BlockSpec(memory_space=pltpu.VMEM)
SM = pl.BlockSpec(memory_space=pltpu.SMEM)
ANY = pl.BlockSpec(memory_space=pl.ANY)
PARAMS = pltpu.CompilerParams(vmem_limit_bytes=24 * 1024 * 1024)


def halves(x):
    high = x.astype(bf16)
    return high, (x - high.astype(f32)).astype(bf16)


def eye_mask():
    return lax.broadcasted_iota(jnp.int32, (B, B), 0) == lax.broadcasted_iota(jnp.int32, (B, B), 1)


def row_mask(rows):
    return (lax.broadcasted_iota(jnp.int32, (B, B), 0) < rows[0]).astype(f32)


def mask_kernel(rows, psi, state):
    keep = row_mask(rows)
    for p in range(LOCAL):
        state[p] = psi[p] * keep


def outer(left_lines, right_lines):
    return lax.dot_general(
        left_lines, right_lines, (((0,), (0,)), ((), ())),
        precision=lax.Precision.HIGHEST, preferred_element_type=f32)


def split_kernel(group, shift, rows, weights, left, right, left2, right2, diag, left_diag, right_diag):
    keep = row_mask(rows)
    eye = eye_mask()
    pad = jnp.zeros((8 - TERMS, B), f32)
    lines = []
    for k in range(TERMS):
        block = left[k] * keep
        left2[k] = jnp.concatenate(halves(block), axis=1)
        chosen = jnp.where(shift[k] == 0, 1.0, 0.0).astype(f32)
        lines.append(jnp.sum(jnp.where(eye, block, 0.0), axis=0, keepdims=True) * chosen)
    left_diag[...] = jnp.concatenate(lines + [pad], axis=0)
    lines = [[] for _ in range(LOCAL)]
    for k in range(TERMS):
        for q in range(LOCAL):
            block = right[k, q]
            right2[k, q] = jnp.concatenate(halves(jnp.transpose(block)), axis=1)
            p = group[0] * LOCAL + q
            scale = weights[k * 256 + p * 16 + p]
            lines[q].append(jnp.sum(jnp.where(eye, block, 0.0), axis=0, keepdims=True) * scale)
    for q in range(LOCAL):
        right_diag[q] = jnp.concatenate(lines[q] + [pad], axis=0)
        diag[q] = outer(left_diag[...], right_diag[q])


def mix(group, weights, z, target, out, chunks):
    height = B // chunks

    def part(start, width, at):
        first = target * LOCAL + start
        acc = [None] * width
        for k in range(TERMS):
            for q in range(LOCAL):
                block = z[k * LOCAL + q, at, :]
                for j in range(width):
                    term = weights[k * 256 + (first + j) * 16 + group[0] * LOCAL + q] * block
                    acc[j] = term if acc[j] is None else acc[j] + term
        for j in range(width):
            out[start + j, at, :] = acc[j]

    def rows(r, carry):
        part(0, LOCAL, pl.ds(pl.multiple_of(r * height, height), height))
        return carry

    if chunks > 1:
        lax.fori_loop(0, chunks, rows, 0)
    else:
        for half in range(2):
            part(2 * half, 2, slice(None))


def terms_kernel(group, sector, shift, weights, own, by_chip, by_core, left2, right2, z, far, vec2):
    odd = lax.rem(sector[0], 2)
    for p in range(LOCAL):
        vec2[1, p] = jnp.concatenate(halves(own[p]), axis=1)
        vec2[2 - 2 * odd, p] = jnp.concatenate(halves(by_core[p]), axis=1)
        vec2[2 * odd, p] = jnp.concatenate(halves(by_chip[p]), axis=1)
    for k in range(TERMS):
        source = shift[k] + 1
        lhs = left2[k]
        for q in range(LOCAL):
            r = right2[k, q]
            x = jnp.dot(vec2[source, q], jnp.concatenate([r, r], axis=0), preferred_element_type=f32)
            xh, xl = halves(x[:, :B] + x[:, B:])
            both = jnp.concatenate([xh, xl], axis=1)
            y = jnp.dot(lhs, jnp.concatenate([both, both], axis=0), preferred_element_type=f32)
            z[k * LOCAL + q] = y[:, :B] + y[:, B:]
    mix(group, weights, z, group[0] ^ 2, far, 1)


def direct_kernel(group, sector, weights, z, direct):
    mix(group, weights, z, group[0] ^ (1 + 2 * lax.rem(sector[0], 2)), direct, 2)


def relayed_kernel(group, sector, weights, z, after, relayed):
    mix(group, weights, z, group[0] ^ (3 - 2 * lax.rem(sector[0], 2)), relayed, 4)


def relay_kernel(relayed, far, out):
    for p in range(LOCAL):
        out[p] = relayed[p] + far[p]


def own_kernel(group, weights, z, own):
    mix(group, weights, z, group[0], own, 4)


def lane(row, j):
    at = lax.broadcasted_iota(jnp.int32, row.shape, 1) == j
    return jnp.sum(jnp.where(at, row, 0.0), axis=1, keepdims=True)


def put_lanes(values):
    at = lax.broadcasted_iota(jnp.int32, (1, B), 1)
    row = jnp.zeros((1, B), f32)
    for j, v in enumerate(values):
        row = jnp.where(at == j, v, row)
    return row


def lowest_root(lead, middle, const):
    root = jnp.sqrt(middle * middle - 4.0 * lead * const)
    return jnp.where(middle > 0, (-middle - root) / (2.0 * lead), 2.0 * const / (root - middle))


def ritz(sums, rayleigh, length):
    s_ic, c_i, curvature, correlation, spread = sums
    cross = 0.5 * (s_ic + c_i)
    lead = length * spread - correlation * correlation
    middle = -(length * curvature + spread * rayleigh - 2.0 * correlation * cross)
    const = rayleigh * curvature - cross * cross
    lowest = lowest_root(lead, middle, const)
    keep = curvature - lowest * spread
    add = lowest * correlation - cross
    norm = keep * keep * length + 2.0 * keep * add * correlation + add * add * spread
    factor = 1.0 / jnp.sqrt(norm)
    keep, add = keep * factor, add * factor
    rayleigh = keep * keep * rayleigh + 2.0 * keep * add * cross + add * add * curvature
    length = keep * keep * length + 2.0 * keep * add * correlation + add * add * spread
    return lowest, keep, add, rayleigh, length


def totals(stats, count, n):
    row = jnp.sum(stats[...], axis=0, keepdims=True) * (1.0 / count)
    return [lane(row, j) for j in range(n)]


def correct(state, image, diag, theta):
    return (image - theta * state) / jnp.maximum(jnp.abs(diag - theta), 1.0)


def start_kernel(count, stats, s0, s1, s2, pack0, pack1, pack2, diag0, right_diag,
                 i0, i1, i2, diag1, diag2, c0, c1, c2, carry):
    rayleigh, length = totals(stats, count, 2)
    theta = rayleigh / length
    for pack, diag in ((pack1, diag1), (pack2, diag2)):
        for p in range(LOCAL):
            diag[p] = outer(pack[LOCAL * B:PACK, :], right_diag[p])
    for s, pack, i, diag, c in ((s0, pack0, i0, diag0, c0), (s1, pack1, i1, diag1, c1), (s2, pack2, i2, diag2, c2)):
        for p in range(LOCAL):
            block = pack[p * B:(p + 1) * B, :]
            i[p] = block
            c[p] = correct(s[p], block, diag[p], theta)
    carry[...] = jnp.broadcast_to(put_lanes([rayleigh, length]), (8, B))


def next_kernel(count, step, keeps, stats, carry_in, *refs):
    sums = totals(stats, count, 5)
    old = carry_in[0:1, :]
    lowest, keep, add, rayleigh, length = ritz(sums, lane(old, 0), lane(old, 1))
    theta = rayleigh / length
    for n in range(3):
        state, image, corr, diag, more = refs[n:15:3]
        for p in range(LOCAL):
            s = keep * state[p] + add * corr[p]
            i = keep * image[p] + add * more[p]
            refs[15 + n][p] = correct(s, i, diag[p], theta)
            if n < keeps:
                refs[18 + n][p] = s
                refs[18 + keeps + n][p] = i
    energies = [lane(old, 2 + j) for j in range(step)] + [lowest]
    refs[-1][...] = jnp.broadcast_to(put_lanes([rayleigh, length] + energies), (8, B))


def last_kernel(count, stats, carry_in, state, corr, state_out, energies):
    sums = totals(stats, count, 5)
    old = carry_in[0:1, :]
    lowest, keep, add, _, _ = ritz(sums, lane(old, 0), lane(old, 1))
    for p in range(LOCAL):
        state_out[p] = keep * state[p] + add * corr[p]
    for j, v in enumerate([lane(old, 2 + j) for j in range(ITERS - 1)] + [lowest]):
        energies[j] = v[0, 0]


def sum_all(block):
    return jnp.sum(jnp.sum(block, axis=0, keepdims=True), axis=1, keepdims=True)


def first_stats_kernel(own, direct, relayed, state, left_diag, pack, stats):
    a, b = jnp.zeros((B, B), f32), jnp.zeros((B, B), f32)
    for p in range(LOCAL):
        i = own[p] + (direct[p] + relayed[p])
        s = state[p]
        pack[p * B:(p + 1) * B, :] = i
        a = a + s * i
        b = b + s * s
    pack[LOCAL * B:PACK, :] = left_diag[...]
    stats[...] = jnp.broadcast_to(put_lanes([sum_all(a), sum_all(b)]), stats.shape)


def stats_kernel(own, direct, relayed, state, corr, image, *outs):
    acc = [jnp.zeros((B, B), f32) for _ in range(5)]
    for p in range(LOCAL):
        ic = own[p] + (direct[p] + relayed[p])
        s, c, i = state[p], corr[p], image[p]
        if len(outs) > 1:
            outs[0][p] = ic
        for j, v in enumerate((s * ic, c * i, c * ic, s * c, c * c)):
            acc[j] = acc[j] + v
    outs[-1][...] = jnp.broadcast_to(put_lanes([sum_all(a) for a in acc]), outs[-1].shape)


def arr(*shape, dtype=f32):
    return jax.ShapeDtypeStruct(shape, dtype)


BLOCK = arr(LOCAL, B, B)
TERM_BLOCKS = arr(TERMS * LOCAL, B, B)


def call(kernel, name, in_specs, outs, scratch=(), out_specs=None, flops=0):
    moved = sum(o.size * o.dtype.itemsize for o in outs)
    return pl.pallas_call(
        kernel,
        out_shape=outs,
        in_specs=in_specs,
        out_specs=out_specs or [VM] * len(outs),
        scratch_shapes=list(scratch),
        compiler_params=PARAMS,
        cost_estimate=pl.CostEstimate(flops=flops, bytes_accessed=2 * moved, transcendentals=0),
        name=name,
    )


def swap(x, even, odd):
    n = lax.axis_size("sec")
    perm = [(s * GROUPS + g, s * GROUPS + (g ^ (odd if s % 2 else even))) for s in range(n) for g in range(GROUPS)]
    return lax.ppermute(x, ("sec", "pair"), perm)


def neighbours(x):
    n = lax.axis_size("sec")
    by_chip = lax.ppermute(x, "sec", [(i, i + 1 if i % 2 else i - 1) for i in range(1, n - 1)])
    by_core = lax.ppermute(x, "sec", [(i, i ^ 1) for i in range(n)])
    return by_chip, by_core


def exchange(stats, devices):
    got = lax.all_to_all(stats.reshape(devices, 1, B), ("sec", "pair"), 0, 0)
    return got.reshape(devices, B)


def on_device(psi_start, left_env, right_env, mpo_coef, mpo_pattern, sector_shift, block_rows):
    devices = lax.axis_size("sec") * lax.axis_size("pair")
    count = float(psi_start.size * devices)
    psi = psi_start.reshape(LOCAL, B, B)
    left = left_env.reshape(TERMS, B, B)
    group = lax.axis_index("pair").astype(jnp.int32).reshape(1)
    sector = lax.axis_index("sec").astype(jnp.int32).reshape(1)
    weights = (mpo_coef * mpo_pattern.astype(f32)).reshape(-1)
    stats_shape = arr(devices, B)
    carry_shape = arr(8, B)

    def shares(vectors, left2, right2):
        z, far = call(
            terms_kernel, "terms", [SM] * 4 + [VM] * 5, [TERM_BLOCKS, BLOCK],
            [pltpu.VMEM((3, LOCAL, B, 2 * B), bf16)],
        )(group, sector, sector_shift, weights, *vectors, left2, right2)
        far = swap(far, 1, 3)
        (direct,) = call(direct_kernel, "direct", [SM] * 3 + [VM], [BLOCK])(group, sector, weights, z)
        (relayed,) = call(relayed_kernel, "relayed", [SM] * 3 + [VM, ANY], [BLOCK])(group, sector, weights, z, direct)
        direct = swap(direct, 1, 3)
        (relayed,) = call(relay_kernel, "relay", [VM] * 2, [BLOCK])(relayed, far)
        (own,) = call(own_kernel, "own", [SM, SM, VM], [BLOCK])(group, weights, z)
        return own, direct, swap(relayed, 3, 1)

    (state,) = call(mask_kernel, "mask", [SM, VM], [BLOCK])(block_rows, psi)
    states = (state, *neighbours(state))
    left2, right2, diag, left_diag, right_diag = call(
        split_kernel, "split", [SM] * 4 + [VM] * 2,
        [arr(TERMS, B, 2 * B, dtype=bf16), arr(TERMS, LOCAL, B, 2 * B, dtype=bf16), BLOCK, arr(8, B), arr(LOCAL, 8, B)],
    )(group, sector_shift, block_rows, weights, left, right_env)

    parts = shares(states, left2, right2)
    pack, stats = call(first_stats_kernel, "first_stats", [VM] * 5, [arr(PACK, B), stats_shape])(
        *parts, state, left_diag)
    packs = (pack, *neighbours(pack))
    *out, carry = call(
        lambda *refs: start_kernel(count, *refs), "start", [VM] * 9, [BLOCK] * 8 + [carry_shape]
    )(exchange(stats, devices), *states, *packs, diag, right_diag)
    images, diags, corrs = out[:3], (diag, *out[3:5]), out[5:8]

    for step in range(ITERS):
        parts = shares(corrs, left2, right2)
        outs = [BLOCK, stats_shape] if step < ITERS - 1 else [stats_shape]
        *image_corr, stats = call(stats_kernel, "stats", [VM] * 6, outs)(*parts, states[0], corrs[0], images[0])
        got = exchange(stats, devices)
        if step < ITERS - 1:
            more = (*image_corr, *neighbours(*image_corr))
            keeps = 3 if step < ITERS - 2 else 1
            *out, carry = call(
                functools.partial(next_kernel, count, step, keeps), "next", [VM] * 17,
                [BLOCK] * (3 + 2 * keeps) + [carry_shape],
            )(got, carry, *states, *images, *corrs, *diags, *more)
            corrs, states, images = out[:3], out[3:3 + keeps], out[3 + keeps:]

    state, energies = call(
        lambda *refs: last_kernel(count, *refs), "last", [VM] * 4, [BLOCK, arr(ITERS)], out_specs=[VM, SM]
    )(got, carry, states[0], corrs[0])
    return state.reshape(psi_start.shape), energies


def solution(mesh):
    in_specs = (
        P("sec", "pair", None, None),
        P(None, "sec", None, None),
        P(None, "pair", None, None),
        P(),
        P(),
        P(),
        P("sec"),
    )
    out_specs = (P("sec", "pair", None, None), P())
    return jax.shard_map(
        on_device, mesh=mesh, in_specs=in_specs, out_specs=out_specs, check_vma=False
    )
```

profile of v0, /device:TPU:1, one launch (start us, length us, event | category | flops | bytes accessed | tf_op | source)
XLA Modules:
  0.0 213.6 jit_solution(1749372070088214014)
XLA Ops:
  2.3 3.3 %collective-permute-start.1 = (f32[4,128,128]{2,1,0:T(8,128)S(1)}, f32[4,128,128]{2,1,0:T(8,128)S(1)}, u32[]{:S(2)}, u32[]{:S(2)}) collective-permute-start(f32[4,128,128]{2,1,0:T(8,128)S(1)} %mask.1.own.state.refs_1_.refs_0_), channel_id=1, source_target_pairs={{0,4},{4,0},{8,12},{12,8},{16,20},{20,16},{24,28},{28,24},{32,36},... | collective-permute-start | bytes 786440 | tf_op jit(solution)/shard_map/ppermute | solution.py:282
  5.6 1.9 collective-permute-start
  13.3 2.0 terms.5
  23.1 4.6 %collective-permute-done.2.direct = f32[4,128,128]{2,1,0:T(8,128)S(1)} collective-permute-done((f32[4,128,128]{2,1,0:T(8,128)S(1)}, f32[4,128,128]{2,1,0:T(8,128)S(1)}, u32[]{:S(2)}, u32[]{:S(2)}) %collective-permute-start.2) | collective-permute-done | bytes 262176 | tf_op jit(solution)/shard_map/ppermute | solution.py:276
  29.6 3.3 %collective-permute-start.5 = (f32[520,128]{1,0:T(8,128)S(1)}, f32[520,128]{1,0:T(8,128)S(1)}, u32[]{:S(2)}, u32[]{:S(2)}) collective-permute-start(f32[520,128]{1,0:T(8,128)S(1)} %get-tuple-element.68.refs_4_), channel_id=1, source_target_pairs={{4,8},{8,4},{12,16},{16,12},{20,24},{24,20},{28,32},{32,28},{36,40... | collective-permute-start | bytes 798728 | tf_op jit(solution)/shard_map/ppermute | solution.py:281
  32.9 26.8 %all_to_all.25 = f32[256,1,128]{2,1,0:T(1,128)S(1)} all-to-all(f32[256,1,128]{2,1,0:T(1,128)S(1)} %bitcast.33), channel_id=1, replica_groups=mesh['sec'=64,'pair'=4] {'sec','pair'}, dimensions={0} | all-to-all | bytes 262144 | tf_op jit(solution)/shard_map/all_to_all | solution.py:287
  60.4 2.0 terms.6
  65.8 1.8 collective-permute-start.7
  70.2 2.1 collective-permute-done.7.direct
  72.3 2.5 %collective-permute-done.9.relayed = f32[4,128,128]{2,1,0:T(8,128)S(1)} collective-permute-done((f32[4,128,128]{2,1,0:T(8,128)S(1)}, f32[4,128,128]{2,1,0:T(8,128)S(1)}, u32[]{:S(2)}, u32[]{:S(2)}) %collective-permute-start.9) | collective-permute-done | bytes 262176 | tf_op jit(solution)/shard_map/ppermute | solution.py:276
  75.0 2.6 %collective-permute-start.11 = (f32[4,128,128]{2,1,0:T(8,128)S(1)}, f32[4,128,128]{2,1,0:T(8,128)S(1)}, u32[]{:S(2)}, u32[]{:S(2)}) collective-permute-start(f32[4,128,128]{2,1,0:T(8,128)S(1)} %get-tuple-element.83.refs_12_), channel_id=1, source_target_pairs={{0,4},{4,0},{8,12},{12,8},{16,20},{20,16},{24,28},{28,24},{32,36},... | collective-permute-start | bytes 786440 | tf_op jit(solution)/shard_map/ppermute | solution.py:282
  77.6 2.3 %collective-permute-start.10 = (f32[4,128,128]{2,1,0:T(8,128)S(1)}, f32[4,128,128]{2,1,0:T(8,128)S(1)}, u32[]{:S(2)}, u32[]{:S(2)}) collective-permute-start(f32[4,128,128]{2,1,0:T(8,128)S(1)} %get-tuple-element.83.refs_12_), channel_id=1, source_target_pairs={{4,8},{8,4},{12,16},{16,12},{20,24},{24,20},{28,32},{32,28},{36,40... | collective-permute-start | bytes 786440 | tf_op jit(solution)/shard_map/ppermute | solution.py:281
  79.9 19.1 %all_to_all.26 = f32[256,1,128]{2,1,0:T(1,128)S(1)} all-to-all(f32[256,1,128]{2,1,0:T(1,128)S(1)} %bitcast.34), channel_id=1, replica_groups=mesh['sec'=64,'pair'=4] {'sec','pair'}, dimensions={0} | all-to-all | bytes 262144 | tf_op jit(solution)/shard_map/all_to_all | solution.py:287
  99.6 2.0 terms.7
  105.0 1.8 collective-permute-start.12
  109.4 2.1 collective-permute-done.12.direct
  111.5 2.5 %collective-permute-done.14.relayed = f32[4,128,128]{2,1,0:T(8,128)S(1)} collective-permute-done((f32[4,128,128]{2,1,0:T(8,128)S(1)}, f32[4,128,128]{2,1,0:T(8,128)S(1)}, u32[]{:S(2)}, u32[]{:S(2)}) %collective-permute-start.14) | collective-permute-done | bytes 262176 | tf_op jit(solution)/shard_map/ppermute | solution.py:276
  114.3 2.6 %collective-permute-start.16 = (f32[4,128,128]{2,1,0:T(8,128)S(1)}, f32[4,128,128]{2,1,0:T(8,128)S(1)}, u32[]{:S(2)}, u32[]{:S(2)}) collective-permute-start(f32[4,128,128]{2,1,0:T(8,128)S(1)} %get-tuple-element.97.refs_12_), channel_id=1, source_target_pairs={{0,4},{4,0},{8,12},{12,8},{16,20},{20,16},{24,28},{28,24},{32,36},... | collective-permute-start | bytes 786440 | tf_op jit(solution)/shard_map/ppermute | solution.py:282
  116.8 2.1 collective-permute-start.15
  118.9 19.1 %all_to_all.27 = f32[256,1,128]{2,1,0:T(1,128)S(1)} all-to-all(f32[256,1,128]{2,1,0:T(1,128)S(1)} %bitcast.35), channel_id=1, replica_groups=mesh['sec'=64,'pair'=4] {'sec','pair'}, dimensions={0} | all-to-all | bytes 262144 | tf_op jit(solution)/shard_map/all_to_all | solution.py:287
  138.6 2.0 terms.8
  144.0 1.8 collective-permute-start.17
  148.4 2.1 collective-permute-done.17.direct
  150.5 2.5 %collective-permute-done.19.relayed = f32[4,128,128]{2,1,0:T(8,128)S(1)} collective-permute-done((f32[4,128,128]{2,1,0:T(8,128)S(1)}, f32[4,128,128]{2,1,0:T(8,128)S(1)}, u32[]{:S(2)}, u32[]{:S(2)}) %collective-permute-start.19) | collective-permute-done | bytes 262176 | tf_op jit(solution)/shard_map/ppermute | solution.py:276
  153.3 2.8 %collective-permute-start.21 = (f32[4,128,128]{2,1,0:T(8,128)S(1)}, f32[4,128,128]{2,1,0:T(8,128)S(1)}, u32[]{:S(2)}, u32[]{:S(2)}) collective-permute-start(f32[4,128,128]{2,1,0:T(8,128)S(1)} %get-tuple-element.111.refs_12_), channel_id=1, source_target_pairs={{0,4},{4,0},{8,12},{12,8},{16,20},{20,16},{24,28},{28,24},{32,36},... | collective-permute-start | bytes 786440 | tf_op jit(solution)/shard_map/ppermute | solution.py:282
  156.1 2.1 collective-permute-start.20
  158.2 19.1 %all_to_all.28 = f32[256,1,128]{2,1,0:T(1,128)S(1)} all-to-all(f32[256,1,128]{2,1,0:T(1,128)S(1)} %bitcast.36), channel_id=1, replica_groups=mesh['sec'=64,'pair'=4] {'sec','pair'}, dimensions={0} | all-to-all | bytes 262144 | tf_op jit(solution)/shard_map/all_to_all | solution.py:287
  177.8 2.0 terms.9
  183.2 1.8 collective-permute-start.22
  187.6 2.1 collective-permute-done.22.direct
  189.7 2.5 %collective-permute-done.24.relayed = f32[4,128,128]{2,1,0:T(8,128)S(1)} collective-permute-done((f32[4,128,128]{2,1,0:T(8,128)S(1)}, f32[4,128,128]{2,1,0:T(8,128)S(1)}, u32[]{:S(2)}, u32[]{:S(2)}) %collective-permute-start.24) | collective-permute-done | bytes 262176 | tf_op jit(solution)/shard_map/ppermute | solution.py:276
  192.5 20.1 %all_to_all.29 = f32[256,1,128]{2,1,0:T(1,128)S(1)} all-to-all(f32[256,1,128]{2,1,0:T(1,128)S(1)} %bitcast.29), channel_id=1, replica_groups=mesh['sec'=64,'pair'=4] {'sec','pair'}, dimensions={0} | all-to-all | bytes 262144 | tf_op jit(solution)/shard_map/all_to_all | solution.py:287
  (72 shorter events, 45.0 us)
Async XLA Ops:
  1.3 1.0 copy-start.2
  2.3 10.5 %collective-permute-start.1 = (f32[4,128,128]{2,1,0:T(8,128)S(1)}, f32[4,128,128]{2,1,0:T(8,128)S(1)}, u32[]{:S(2)}, u32[]{:S(2)}) collective-permute-start(f32[4,128,128]{2,1,0:T(8,128)S(1)} %mask.1.own.state.refs_1_.refs_0_), channel_id=1, source_target_pairs={{0,4},{4,0},{8,12},{12,8},{16,20},{20,16},{24,28},{28,24},{32,36},... | collective-permute-start | bytes 786440 | tf_op jit(solution)/shard_map/ppermute | solution.py:282
  5.6 7.7 %collective-permute-start = (f32[4,128,128]{2,1,0:T(8,128)S(1)}, f32[4,128,128]{2,1,0:T(8,128)S(1)}, u32[]{:S(2)}, u32[]{:S(2)}) collective-permute-start(f32[4,128,128]{2,1,0:T(8,128)S(1)} %mask.1.own.state.refs_1_.refs_0_), channel_id=1, source_target_pairs={{4,8},{8,4},{12,16},{16,12},{20,24},{24,20},{28,32},{32,28},{36,40... | collective-permute-start | bytes 786440 | tf_op jit(solution)/shard_map/ppermute | solution.py:281
  8.4 1.4 copy-start
  9.8 1.0 copy-start.1
  10.8 0.7 copy-start.3
  15.2 6.5 %collective-permute-start.3 = (f32[4,128,128]{2,1,0:T(8,128)S(1)}, f32[4,128,128]{2,1,0:T(8,128)S(1)}, u32[]{:S(2)}, u32[]{:S(2)}) collective-permute-start(f32[4,128,128]{2,1,0:T(8,128)S(1)} %get-tuple-element.65), channel_id=1, source_target_pairs={{0,1},{1,0},{2,3},{3,2},{4,7},{5,6},{6,5},{7,4},{8,9},{9,8},{10,11... | collective-permute-start | bytes 786440 | tf_op jit(solution)/shard_map/ppermute | solution.py:276
  19.3 8.3 %collective-permute-start.2 = (f32[4,128,128]{2,1,0:T(8,128)S(1)}, f32[4,128,128]{2,1,0:T(8,128)S(1)}, u32[]{:S(2)}, u32[]{:S(2)}) collective-permute-start(f32[4,128,128]{2,1,0:T(8,128)S(1)} %direct.5.after), channel_id=1, source_target_pairs={{0,1},{1,0},{2,3},{3,2},{4,7},{5,6},{6,5},{7,4},{8,9},{9,8},{10,11... | collective-permute-start | bytes 786440 | tf_op jit(solution)/shard_map/ppermute | solution.py:276
  21.8 5.8 %collective-permute-start.4 = (f32[4,128,128]{2,1,0:T(8,128)S(1)}, f32[4,128,128]{2,1,0:T(8,128)S(1)}, u32[]{:S(2)}, u32[]{:S(2)}) collective-permute-start(f32[4,128,128]{2,1,0:T(8,128)S(1)} %relay.5), channel_id=1, source_target_pairs={{0,3},{1,2},{2,1},{3,0},{4,5},{5,4},{6,7},{7,6},{8,11},{9,10},{10,... | collective-permute-start | bytes 786440 | tf_op jit(solution)/shard_map/ppermute | solution.py:276
  27.6 32.8 %copy-start.4 = (s32[6]{0:T(128)S(1)}, s32[6]{0:T(128)}, u32[]{:S(2)}) copy-start(s32[6]{0:T(128)} %shift.11) | copy-start | bytes 76
  27.8 31.8 %collective-permute-start.6 = (f32[520,128]{1,0:T(8,128)S(1)}, f32[520,128]{1,0:T(8,128)S(1)}, u32[]{:S(2)}, u32[]{:S(2)}) collective-permute-start(f32[520,128]{1,0:T(8,128)S(1)} %get-tuple-element.68.refs_4_), channel_id=1, source_target_pairs={{0,4},{4,0},{8,12},{12,8},{16,20},{20,16},{24,28},{28,24},{32,36},... | collective-permute-start | bytes 798728 | tf_op jit(solution)/shard_map/ppermute | solution.py:282
  29.6 30.1 %collective-permute-start.5 = (f32[520,128]{1,0:T(8,128)S(1)}, f32[520,128]{1,0:T(8,128)S(1)}, u32[]{:S(2)}, u32[]{:S(2)}) collective-permute-start(f32[520,128]{1,0:T(8,128)S(1)} %get-tuple-element.68.refs_4_), channel_id=1, source_target_pairs={{4,8},{8,4},{12,16},{16,12},{20,24},{24,20},{28,32},{32,28},{36,40... | collective-permute-start | bytes 798728 | tf_op jit(solution)/shard_map/ppermute | solution.py:281
  62.4 6.5 %collective-permute-start.8 = (f32[4,128,128]{2,1,0:T(8,128)S(1)}, f32[4,128,128]{2,1,0:T(8,128)S(1)}, u32[]{:S(2)}, u32[]{:S(2)}) collective-permute-start(f32[4,128,128]{2,1,0:T(8,128)S(1)} %get-tuple-element.75), channel_id=1, source_target_pairs={{0,1},{1,0},{2,3},{3,2},{4,7},{5,6},{6,5},{7,4},{8,9},{9,8},{10,11... | collective-permute-start | bytes 786440 | tf_op jit(solution)/shard_map/ppermute | solution.py:276
  65.8 6.5 %collective-permute-start.7 = (f32[4,128,128]{2,1,0:T(8,128)S(1)}, f32[4,128,128]{2,1,0:T(8,128)S(1)}, u32[]{:S(2)}, u32[]{:S(2)}) collective-permute-start(f32[4,128,128]{2,1,0:T(8,128)S(1)} %direct.6.after), channel_id=1, source_target_pairs={{0,1},{1,0},{2,3},{3,2},{4,7},{5,6},{6,5},{7,4},{8,9},{9,8},{10,11... | collective-permute-start | bytes 786440 | tf_op jit(solution)/shard_map/ppermute | solution.py:276
  68.9 5.8 %collective-permute-start.9 = (f32[4,128,128]{2,1,0:T(8,128)S(1)}, f32[4,128,128]{2,1,0:T(8,128)S(1)}, u32[]{:S(2)}, u32[]{:S(2)}) collective-permute-start(f32[4,128,128]{2,1,0:T(8,128)S(1)} %relay.6), channel_id=1, source_target_pairs={{0,3},{1,2},{2,1},{3,0},{4,5},{5,4},{6,7},{7,6},{8,11},{9,10},{10,... | collective-permute-start | bytes 786440 | tf_op jit(solution)/shard_map/ppermute | solution.py:276
  75.0 24.0 %collective-permute-start.11 = (f32[4,128,128]{2,1,0:T(8,128)S(1)}, f32[4,128,128]{2,1,0:T(8,128)S(1)}, u32[]{:S(2)}, u32[]{:S(2)}) collective-permute-start(f32[4,128,128]{2,1,0:T(8,128)S(1)} %get-tuple-element.83.refs_12_), channel_id=1, source_target_pairs={{0,4},{4,0},{8,12},{12,8},{16,20},{20,16},{24,28},{28,24},{32,36},... | collective-permute-start | bytes 786440 | tf_op jit(solution)/shard_map/ppermute | solution.py:282
  77.6 21.4 %collective-permute-start.10 = (f32[4,128,128]{2,1,0:T(8,128)S(1)}, f32[4,128,128]{2,1,0:T(8,128)S(1)}, u32[]{:S(2)}, u32[]{:S(2)}) collective-permute-start(f32[4,128,128]{2,1,0:T(8,128)S(1)} %get-tuple-element.83.refs_12_), channel_id=1, source_target_pairs={{4,8},{8,4},{12,16},{16,12},{20,24},{24,20},{28,32},{32,28},{36,40... | collective-permute-start | bytes 786440 | tf_op jit(solution)/shard_map/ppermute | solution.py:281
  101.6 6.5 %collective-permute-start.13 = (f32[4,128,128]{2,1,0:T(8,128)S(1)}, f32[4,128,128]{2,1,0:T(8,128)S(1)}, u32[]{:S(2)}, u32[]{:S(2)}) collective-permute-start(f32[4,128,128]{2,1,0:T(8,128)S(1)} %get-tuple-element.88), channel_id=1, source_target_pairs={{0,1},{1,0},{2,3},{3,2},{4,7},{5,6},{6,5},{7,4},{8,9},{9,8},{10,11... | collective-permute-start | bytes 786440 | tf_op jit(solution)/shard_map/ppermute | solution.py:276
  105.0 6.5 %collective-permute-start.12 = (f32[4,128,128]{2,1,0:T(8,128)S(1)}, f32[4,128,128]{2,1,0:T(8,128)S(1)}, u32[]{:S(2)}, u32[]{:S(2)}) collective-permute-start(f32[4,128,128]{2,1,0:T(8,128)S(1)} %direct.7.after), channel_id=1, source_target_pairs={{0,1},{1,0},{2,3},{3,2},{4,7},{5,6},{6,5},{7,4},{8,9},{9,8},{10,11... | collective-permute-start | bytes 786440 | tf_op jit(solution)/shard_map/ppermute | solution.py:276
  108.1 5.8 %collective-permute-start.14 = (f32[4,128,128]{2,1,0:T(8,128)S(1)}, f32[4,128,128]{2,1,0:T(8,128)S(1)}, u32[]{:S(2)}, u32[]{:S(2)}) collective-permute-start(f32[4,128,128]{2,1,0:T(8,128)S(1)} %relay.7), channel_id=1, source_target_pairs={{0,3},{1,2},{2,1},{3,0},{4,5},{5,4},{6,7},{7,6},{8,11},{9,10},{10,... | collective-permute-start | bytes 786440 | tf_op jit(solution)/shard_map/ppermute | solution.py:276
  114.3 23.8 %collective-permute-start.16 = (f32[4,128,128]{2,1,0:T(8,128)S(1)}, f32[4,128,128]{2,1,0:T(8,128)S(1)}, u32[]{:S(2)}, u32[]{:S(2)}) collective-permute-start(f32[4,128,128]{2,1,0:T(8,128)S(1)} %get-tuple-element.97.refs_12_), channel_id=1, source_target_pairs={{0,4},{4,0},{8,12},{12,8},{16,20},{20,16},{24,28},{28,24},{32,36},... | collective-permute-start | bytes 786440 | tf_op jit(solution)/shard_map/ppermute | solution.py:282
  116.8 21.2 %collective-permute-start.15 = (f32[4,128,128]{2,1,0:T(8,128)S(1)}, f32[4,128,128]{2,1,0:T(8,128)S(1)}, u32[]{:S(2)}, u32[]{:S(2)}) collective-permute-start(f32[4,128,128]{2,1,0:T(8,128)S(1)} %get-tuple-element.97.refs_12_), channel_id=1, source_target_pairs={{4,8},{8,4},{12,16},{16,12},{20,24},{24,20},{28,32},{32,28},{36,40... | collective-permute-start | bytes 786440 | tf_op jit(solution)/shard_map/ppermute | solution.py:281
  140.6 6.5 %collective-permute-start.18 = (f32[4,128,128]{2,1,0:T(8,128)S(1)}, f32[4,128,128]{2,1,0:T(8,128)S(1)}, u32[]{:S(2)}, u32[]{:S(2)}) collective-permute-start(f32[4,128,128]{2,1,0:T(8,128)S(1)} %get-tuple-element.102), channel_id=1, source_target_pairs={{0,1},{1,0},{2,3},{3,2},{4,7},{5,6},{6,5},{7,4},{8,9},{9,8},{10,11... | collective-permute-start | bytes 786440 | tf_op jit(solution)/shard_map/ppermute | solution.py:276
  144.0 6.5 %collective-permute-start.17 = (f32[4,128,128]{2,1,0:T(8,128)S(1)}, f32[4,128,128]{2,1,0:T(8,128)S(1)}, u32[]{:S(2)}, u32[]{:S(2)}) collective-permute-start(f32[4,128,128]{2,1,0:T(8,128)S(1)} %direct.8.after), channel_id=1, source_target_pairs={{0,1},{1,0},{2,3},{3,2},{4,7},{5,6},{6,5},{7,4},{8,9},{9,8},{10,11... | collective-permute-start | bytes 786440 | tf_op jit(solution)/shard_map/ppermute | solution.py:276
  147.2 5.8 %collective-permute-start.19 = (f32[4,128,128]{2,1,0:T(8,128)S(1)}, f32[4,128,128]{2,1,0:T(8,128)S(1)}, u32[]{:S(2)}, u32[]{:S(2)}) collective-permute-start(f32[4,128,128]{2,1,0:T(8,128)S(1)} %relay.8), channel_id=1, source_target_pairs={{0,3},{1,2},{2,1},{3,0},{4,5},{5,4},{6,7},{7,6},{8,11},{9,10},{10,... | collective-permute-start | bytes 786440 | tf_op jit(solution)/shard_map/ppermute | solution.py:276
  153.3 24.0 %collective-permute-start.21 = (f32[4,128,128]{2,1,0:T(8,128)S(1)}, f32[4,128,128]{2,1,0:T(8,128)S(1)}, u32[]{:S(2)}, u32[]{:S(2)}) collective-permute-start(f32[4,128,128]{2,1,0:T(8,128)S(1)} %get-tuple-element.111.refs_12_), channel_id=1, source_target_pairs={{0,4},{4,0},{8,12},{12,8},{16,20},{20,16},{24,28},{28,24},{32,36},... | collective-permute-start | bytes 786440 | tf_op jit(solution)/shard_map/ppermute | solution.py:282
  156.1 21.2 %collective-permute-start.20 = (f32[4,128,128]{2,1,0:T(8,128)S(1)}, f32[4,128,128]{2,1,0:T(8,128)S(1)}, u32[]{:S(2)}, u32[]{:S(2)}) collective-permute-start(f32[4,128,128]{2,1,0:T(8,128)S(1)} %get-tuple-element.111.refs_12_), channel_id=1, source_target_pairs={{4,8},{8,4},{12,16},{16,12},{20,24},{24,20},{28,32},{32,28},{36,40... | collective-permute-start | bytes 786440 | tf_op jit(solution)/shard_map/ppermute | solution.py:281
  179.8 6.5 %collective-permute-start.23 = (f32[4,128,128]{2,1,0:T(8,128)S(1)}, f32[4,128,128]{2,1,0:T(8,128)S(1)}, u32[]{:S(2)}, u32[]{:S(2)}) collective-permute-start(f32[4,128,128]{2,1,0:T(8,128)S(1)} %get-tuple-element.116), channel_id=1, source_target_pairs={{0,1},{1,0},{2,3},{3,2},{4,7},{5,6},{6,5},{7,4},{8,9},{9,8},{10,11... | collective-permute-start | bytes 786440 | tf_op jit(solution)/shard_map/ppermute | solution.py:276
  183.2 6.5 %collective-permute-start.22 = (f32[4,128,128]{2,1,0:T(8,128)S(1)}, f32[4,128,128]{2,1,0:T(8,128)S(1)}, u32[]{:S(2)}, u32[]{:S(2)}) collective-permute-start(f32[4,128,128]{2,1,0:T(8,128)S(1)} %direct.9.after), channel_id=1, source_target_pairs={{0,1},{1,0},{2,3},{3,2},{4,7},{5,6},{6,5},{7,4},{8,9},{9,8},{10,11... | collective-permute-start | bytes 786440 | tf_op jit(solution)/shard_map/ppermute | solution.py:276
  186.4 5.8 %collective-permute-start.24 = (f32[4,128,128]{2,1,0:T(8,128)S(1)}, f32[4,128,128]{2,1,0:T(8,128)S(1)}, u32[]{:S(2)}, u32[]{:S(2)}) collective-permute-start(f32[4,128,128]{2,1,0:T(8,128)S(1)} %relay.9), channel_id=1, source_target_pairs={{0,3},{1,2},{2,1},{3,0},{4,5},{5,4},{6,7},{7,6},{8,11},{9,10},{10,... | collective-permute-start | bytes 786440 | tf_op jit(solution)/shard_map/ppermute | solution.py:276
where the time goes:
time: 214 us
  blocking collectives  104 us (49%)
  starting transfers between devices  39.4 us (18%)
  Pallas kernels  33.2 us (16%)
  waiting for transfers between devices  30.2 us (14%)
  local copies, waits for them, and re-layouts  4.09 us (2%)
    all_to_all x5, blocking collectives, exchange(): got = lax.all_to_all(stats.reshape(devices, 1, B), ('sec', 'pair'), 0, 0)  104 us
    ppermute x15, waiting for transfers between devices, swap(): return lax.ppermute(x, ('sec', 'pair'), perm)  29.7 us
    ppermute x15, starting transfers between devices, swap(): return lax.ppermute(x, ('sec', 'pair'), perm)  14.7 us
    ppermute x5, starting transfers between devices, neighbours(): by_core = lax.ppermute(x, 'sec', [(i, i ^ 1) for i in range(n)])  13 us
    ppermute x5, starting transfers between devices, neighbours(): lax.ppermute(x, 'sec', [(i, i + 1 if i % 2 else i - 1) for i in range(1,...  11.7 us
    pallas_call x5, Pallas kernels, shares(): call(terms_kernel, 'terms', [SM] * 4 + [VM] * 5, [TERM_BLOCKS, BLOCK], [p...  9.85 us
    pallas_call x5, Pallas kernels, shares(): call(relayed_kernel, 'relayed', [SM] * 3 + [VM, ANY], [BLOCK])  5.87 us
    pallas_call x5, Pallas kernels, shares(): own, = call(own_kernel, 'own', [SM, SM, VM], [BLOCK])(group, weights, z)  5.87 us
  transfers between devices with their start and end apart: 25, of which 15 were waited for; matrix products, arithmetic and copies ran while one was open for 0% of the time, Pallas kernels for 9%

commit v1 on v0

--- a/solution.py
+++ b/solution.py
@@ -50,31 +50,40 @@
 def split_kernel(group, shift, rows, weights, left, right, left2, right2, diag, left_diag, right_diag):
     keep = row_mask(rows)
     eye = eye_mask()
-    pad = jnp.zeros((8 - TERMS, B), f32)
-    lines = []
-    for k in range(TERMS):
+    left_diag[...] = jnp.zeros_like(left_diag)
+
+    def left_term(k, _):
         block = left[k] * keep
         left2[k] = jnp.concatenate(halves(block), axis=1)
         chosen = jnp.where(shift[k] == 0, 1.0, 0.0).astype(f32)
-        lines.append(jnp.sum(jnp.where(eye, block, 0.0), axis=0, keepdims=True) * chosen)
-    left_diag[...] = jnp.concatenate(lines + [pad], axis=0)
-    lines = [[] for _ in range(LOCAL)]
-    for k in range(TERMS):
+        left_diag[pl.ds(k, 1), :] = jnp.sum(jnp.where(eye, block, 0.0), axis=0, keepdims=True) * chosen
+        return 0
+
+    lax.fori_loop(0, TERMS, left_term, 0)
+    right_diag[...] = jnp.zeros_like(right_diag)
+
+    def term(k, _):
         for q in range(LOCAL):
             block = right[k, q]
             right2[k, q] = jnp.concatenate(halves(jnp.transpose(block)), axis=1)
             p = group[0] * LOCAL + q
             scale = weights[k * 256 + p * 16 + p]
-            lines[q].append(jnp.sum(jnp.where(eye, block, 0.0), axis=0, keepdims=True) * scale)
-    for q in range(LOCAL):
-        right_diag[q] = jnp.concatenate(lines[q] + [pad], axis=0)
+            right_diag[q, pl.ds(k, 1), :] = jnp.sum(jnp.where(eye, block, 0.0), axis=0, keepdims=True) * scale
+        return 0
+
+    lax.fori_loop(0, TERMS, term, 0)
+
+    def outer_block(q, _):
         diag[q] = outer(left_diag[...], right_diag[q])
+        return 0
+
+    lax.fori_loop(0, LOCAL, outer_block, 0)
 
 
 def mix(group, weights, z, target, out, chunks):
     height = B // chunks
 
-    def part(start, width, at):
+    def part(start, width, at, out, place):
         first = target * LOCAL + start
         acc = [None] * width
         for k in range(TERMS):
@@ -84,20 +93,20 @@
                     term = weights[k * 256 + (first + j) * 16 + group[0] * LOCAL + q] * block
                     acc[j] = term if acc[j] is None else acc[j] + term
         for j in range(width):
-            out[start + j, at, :] = acc[j]
+            out[place + j, at, :] = acc[j]
 
     def rows(r, carry):
-        part(0, LOCAL, pl.ds(pl.multiple_of(r * height, height), height))
+        part(0, LOCAL, pl.ds(pl.multiple_of(r * height, height), height), out, 0)
         return carry
 
     if chunks > 1:
         lax.fori_loop(0, chunks, rows, 0)
     else:
         for half in range(2):
-            part(2 * half, 2, slice(None))
-
-
-def terms_kernel(group, sector, shift, weights, own, by_chip, by_core, left2, right2, z, far, vec2):
+            part(2 * half, 2, slice(None), out[half], 0)
+
+
+def terms_kernel(group, sector, shift, weights, own, by_chip, by_core, left2, right2, z, far_a, far_b, vec2):
     odd = lax.rem(sector[0], 2)
     for p in range(LOCAL):
         vec2[1, p] = jnp.concatenate(halves(own[p]), axis=1)
@@ -113,20 +122,21 @@
             both = jnp.concatenate([xh, xl], axis=1)
             y = jnp.dot(lhs, jnp.concatenate([both, both], axis=0), preferred_element_type=f32)
             z[k * LOCAL + q] = y[:, :B] + y[:, B:]
-    mix(group, weights, z, group[0] ^ 2, far, 1)
+    mix(group, weights, z, group[0] ^ 2, (far_a, far_b), 1)
 
 
 def direct_kernel(group, sector, weights, z, direct):
-    mix(group, weights, z, group[0] ^ (1 + 2 * lax.rem(sector[0], 2)), direct, 2)
+    mix(group, weights, z, group[0] ^ (1 + 2 * lax.rem(sector[0], 2)), direct, 4)
 
 
 def relayed_kernel(group, sector, weights, z, after, relayed):
     mix(group, weights, z, group[0] ^ (3 - 2 * lax.rem(sector[0], 2)), relayed, 4)
 
 
-def relay_kernel(relayed, far, out):
-    for p in range(LOCAL):
-        out[p] = relayed[p] + far[p]
+def relay_kernel(relayed, far_a, far_b, out_a, out_b):
+    for j in range(2):
+        out_a[j] = relayed[j] + far_a[j]
+        out_b[j] = relayed[2 + j] + far_b[j]
 
 
 def own_kernel(group, weights, z, own):
@@ -181,14 +191,18 @@
                  i0, i1, i2, diag1, diag2, c0, c1, c2, carry):
     rayleigh, length = totals(stats, count, 2)
     theta = rayleigh / length
-    for pack, diag in ((pack1, diag1), (pack2, diag2)):
-        for p in range(LOCAL):
-            diag[p] = outer(pack[LOCAL * B:PACK, :], right_diag[p])
-    for s, pack, i, diag, c in ((s0, pack0, i0, diag0, c0), (s1, pack1, i1, diag1, c1), (s2, pack2, i2, diag2, c2)):
-        for p in range(LOCAL):
-            block = pack[p * B:(p + 1) * B, :]
-            i[p] = block
-            c[p] = correct(s[p], block, diag[p], theta)
+    blocks = ((s0, pack0, i0, diag0, c0), (s1, pack1, i1, diag1, c1), (s2, pack2, i2, diag2, c2))
+
+    def block(p, _):
+        for n, (s, pack, i, diag, c) in enumerate(blocks):
+            if n:
+                diag[p] = outer(pack[LOCAL * B:PACK, :], right_diag[p])
+            image = pack[pl.ds(pl.multiple_of(p * B, B), B), :]
+            i[p] = image
+            c[p] = correct(s[p], image, diag[p], theta)
+        return 0
+
+    lax.fori_loop(0, LOCAL, block, 0)
     carry[...] = jnp.broadcast_to(put_lanes([rayleigh, length]), (8, B))
 
 
@@ -199,13 +213,16 @@
     theta = rayleigh / length
     for n in range(3):
         state, image, corr, diag, more = refs[n:15:3]
-        for p in range(LOCAL):
+        def body(p, _):
             s = keep * state[p] + add * corr[p]
             i = keep * image[p] + add * more[p]
             refs[15 + n][p] = correct(s, i, diag[p], theta)
             if n < keeps:
                 refs[18 + n][p] = s
                 refs[18 + keeps + n][p] = i
+            return 0
+
+        lax.fori_loop(0, LOCAL, body, 0)
     energies = [lane(old, 2 + j) for j in range(step)] + [lowest]
     refs[-1][...] = jnp.broadcast_to(put_lanes([rayleigh, length] + energies), (8, B))
 
@@ -224,10 +241,10 @@
     return jnp.sum(jnp.sum(block, axis=0, keepdims=True), axis=1, keepdims=True)
 
 
-def first_stats_kernel(own, direct, relayed, state, left_diag, pack, stats):
+def first_stats_kernel(own, direct, relayed_a, relayed_b, state, left_diag, pack, stats):
     a, b = jnp.zeros((B, B), f32), jnp.zeros((B, B), f32)
     for p in range(LOCAL):
-        i = own[p] + (direct[p] + relayed[p])
+        i = own[p] + (direct[p] + (relayed_a, relayed_b)[p // 2][p % 2])
         s = state[p]
         pack[p * B:(p + 1) * B, :] = i
         a = a + s * i
@@ -236,10 +253,10 @@
     stats[...] = jnp.broadcast_to(put_lanes([sum_all(a), sum_all(b)]), stats.shape)
 
 
-def stats_kernel(own, direct, relayed, state, corr, image, *outs):
+def stats_kernel(own, direct, relayed_a, relayed_b, state, corr, image, *outs):
     acc = [jnp.zeros((B, B), f32) for _ in range(5)]
     for p in range(LOCAL):
-        ic = own[p] + (direct[p] + relayed[p])
+        ic = own[p] + (direct[p] + (relayed_a, relayed_b)[p // 2][p % 2])
         s, c, i = state[p], corr[p], image[p]
         if len(outs) > 1:
             outs[0][p] = ic
@@ -253,6 +270,7 @@
 
 
 BLOCK = arr(LOCAL, B, B)
+HALF = arr(LOCAL // 2, B, B)
 TERM_BLOCKS = arr(TERMS * LOCAL, B, B)
 
 
@@ -300,17 +318,17 @@
     carry_shape = arr(8, B)
 
     def shares(vectors, left2, right2):
-        z, far = call(
-            terms_kernel, "terms", [SM] * 4 + [VM] * 5, [TERM_BLOCKS, BLOCK],
+        z, *far = call(
+            terms_kernel, "terms", [SM] * 4 + [VM] * 5, [TERM_BLOCKS, HALF, HALF],
             [pltpu.VMEM((3, LOCAL, B, 2 * B), bf16)],
         )(group, sector, sector_shift, weights, *vectors, left2, right2)
-        far = swap(far, 1, 3)
+        far = [swap(x, 1, 3) for x in far]
         (direct,) = call(direct_kernel, "direct", [SM] * 3 + [VM], [BLOCK])(group, sector, weights, z)
         (relayed,) = call(relayed_kernel, "relayed", [SM] * 3 + [VM, ANY], [BLOCK])(group, sector, weights, z, direct)
         direct = swap(direct, 1, 3)
-        (relayed,) = call(relay_kernel, "relay", [VM] * 2, [BLOCK])(relayed, far)
+        relayed = call(relay_kernel, "relay", [VM] * 3, [HALF] * 2)(relayed, *far)
         (own,) = call(own_kernel, "own", [SM, SM, VM], [BLOCK])(group, weights, z)
-        return own, direct, swap(relayed, 3, 1)
+        return own, direct, *(swap(x, 3, 1) for x in relayed)
 
     (state,) = call(mask_kernel, "mask", [SM, VM], [BLOCK])(block_rows, psi)
     states = (state, *neighbours(state))
@@ -320,7 +338,7 @@
     )(group, sector_shift, block_rows, weights, left, right_env)
 
     parts = shares(states, left2, right2)
-    pack, stats = call(first_stats_kernel, "first_stats", [VM] * 5, [arr(PACK, B), stats_shape])(
+    pack, stats = call(first_stats_kernel, "first_stats", [VM] * 6, [arr(PACK, B), stats_shape])(
         *parts, state, left_diag)
     packs = (pack, *neighbours(pack))
     *out, carry = call(
@@ -331,7 +349,7 @@
     for step in range(ITERS):
         parts = shares(corrs, left2, right2)
         outs = [BLOCK, stats_shape] if step < ITERS - 1 else [stats_shape]
-        *image_corr, stats = call(stats_kernel, "stats", [VM] * 6, outs)(*parts, states[0], corrs[0], images[0])
+        *image_corr, stats = call(stats_kernel, "stats", [VM] * 7, outs)(*parts, states[0], corrs[0], images[0])
         got = exchange(stats, devices)
         if step < ITERS - 1:
             more = (*image_corr, *neighbours(*image_corr))

time: 214 us -> 220 us (1.028)
  waiting for transfers between devices: 30.2 us -> 18.6 us
  starting transfers between devices: 39.4 us -> 50.9 us
  blocking collectives: 104 us -> 107 us
  Pallas kernels: 33.2 us -> 36 us
    ppermute x15 -> x25, starting transfers between devices: 14.7 us -> 28.3 us  [swap(): return lax.ppermute(x, ('sec', 'pair'), perm)]
    ppermute x15 -> x25, waiting for transfers between devices: 29.7 us -> 18.6 us  [swap(): return lax.ppermute(x, ('sec', 'pair'), perm)]
    all_to_all x5, blocking collectives: 104 us -> 107 us  [exchange(): got = lax.all_to_all(stats.reshape(devices, 1, B), ('sec', 'pair'), 0, 0)]
    ppermute x5, starting transfers between devices: 13 us -> 10.5 us  [neighbours(): by_core = lax.ppermute(x, 'sec', [(i, i ^ 1) for i in range(n)])]
  transfers between devices with their start and end apart: 25 -> 35, of which waited for: 15 -> 16; matrix products, arithmetic and copies ran while one was open for 0% -> 0% of each run, Pallas kernels for 9% -> 9%
where the time goes in v1:
time: 220 us; the launch traced here: 219 us
  blocking collectives  107 us (49%)
  starting transfers between devices  50.9 us (23%)
  Pallas kernels  36 us (16%)
  waiting for transfers between devices  18.6 us (8%)
  local copies, waits for them, and re-layouts  4.09 us (2%)
    all_to_all x5, blocking collectives, exchange(): got = lax.all_to_all(stats.reshape(devices, 1, B), ('sec', 'pair'), 0, 0)  107 us
    ppermute x25, starting transfers between devices, swap(): return lax.ppermute(x, ('sec', 'pair'), perm)  28.3 us
    ppermute x25, waiting for transfers between devices, swap(): return lax.ppermute(x, ('sec', 'pair'), perm)  18.6 us
    ppermute x5, starting transfers between devices, neighbours(): lax.ppermute(x, 'sec', [(i, i + 1 if i % 2 else i - 1) for i in range(1,...  12.1 us
    ppermute x5, starting transfers between devices, neighbours(): by_core = lax.ppermute(x, 'sec', [(i, i ^ 1) for i in range(n)])  10.5 us
    pallas_call x5, Pallas kernels, shares(): call(terms_kernel, 'terms', [SM] * 4 + [VM] * 5, [TERM_BLOCKS, HALF, HALF...  9.85 us
    pallas_call x5, Pallas kernels, shares(): call(relayed_kernel, 'relayed', [SM] * 3 + [VM, ANY], [BLOCK])  5.85 us
    pallas_call x5, Pallas kernels, shares(): call(direct_kernel, 'direct', [SM] * 3 + [VM], [BLOCK])  5.85 us
  transfers between devices with their start and end apart: 35, of which 16 were waited for; matrix products, arithmetic and copies ran while one was open for 0% of the time, Pallas kernels for 9%

profile of v1, /device:TPU:1, one launch (start us, length us, event | category | flops | bytes accessed | tf_op | source)
XLA Modules:
  0.0 219.0 jit_solution(18073103118388044409)
XLA Ops:
  2.3 3.3 %collective-permute-start.1 = (f32[4,128,128]{2,1,0:T(8,128)S(1)}, f32[4,128,128]{2,1,0:T(8,128)S(1)}, u32[]{:S(2)}, u32[]{:S(2)}) collective-permute-start(f32[4,128,128]{2,1,0:T(8,128)S(1)} %mask.1.own.state.refs_1_.refs_0_), channel_id=1, source_target_pairs={{0,4},{4,0},{8,12},{12,8},{16,20},{20,16},{24,28},{28,24},{32,36},... | collective-permute-start | bytes 786440 | tf_op jit(solution)/shard_map/ppermute | solution.py:300
  5.6 1.9 collective-permute-start
  11.5 2.7 %split.1 = (bf16[6,128,256]{2,1,0:T(8,128)(2,1)S(1)}, bf16[6,4,128,256]{3,2,1,0:T(8,128)(2,1)S(1)}, f32[4,128,128]{2,1,0:T(8,128)S(1)}, f32[8,128]{1,0:T(8,128)S(1)}, f32[4,8,128]{2,1,0:T(8,128)S(1)}) custom-call(s32[1]{0:T(128)} %bitcast.group, s32[6]{0:T(128)S(1)} %copy-done.3, s32[1]{0:T(128)S(6)} %copy.14.rows, f32[1536]{0:T(1024)S(1)} %reshape.53.weights, ...), custom_call_target="tpu_custom_call" | custom-call | bytes 4497408 | tf_op jit(solution)/shard_map/split/pallas_call | solution.py:335
  14.2 2.0 terms.5
  16.2 2.2 %collective-permute-start.3 = (f32[2,128,128]{2,1,0:T(8,128)S(1)}, f32[2,128,128]{2,1,0:T(8,128)S(1)}, u32[]{:S(2)}, u32[]{:S(2)}) collective-permute-start(f32[2,128,128]{2,1,0:T(8,128)S(1)} %get-tuple-element.80), channel_id=1, source_target_pairs={{0,1},{1,0},{2,3},{3,2},{4,7},{5,6},{6,5},{7,4},{8,9},{9,8},{10,11... | collective-permute-start | bytes 393224 | tf_op jit(solution)/shard_map/ppermute | solution.py:294
  20.1 2.2 %collective-permute-start.2 = (f32[4,128,128]{2,1,0:T(8,128)S(1)}, f32[4,128,128]{2,1,0:T(8,128)S(1)}, u32[]{:S(2)}, u32[]{:S(2)}) collective-permute-start(f32[4,128,128]{2,1,0:T(8,128)S(1)} %direct.5.after), channel_id=1, source_target_pairs={{0,1},{1,0},{2,3},{3,2},{4,7},{5,6},{6,5},{7,4},{8,9},{9,8},{10,11... | collective-permute-start | bytes 786440 | tf_op jit(solution)/shard_map/ppermute | solution.py:294
  30.4 3.9 %collective-permute-start.7 = (f32[520,128]{1,0:T(8,128)S(1)}, f32[520,128]{1,0:T(8,128)S(1)}, u32[]{:S(2)}, u32[]{:S(2)}) collective-permute-start(f32[520,128]{1,0:T(8,128)S(1)} %get-tuple-element.86.refs_4_), channel_id=1, source_target_pairs={{4,8},{8,4},{12,16},{16,12},{20,24},{24,20},{28,32},{32,28},{36,40... | collective-permute-start | bytes 798728 | tf_op jit(solution)/shard_map/ppermute | solution.py:299
  34.2 26.7 %all_to_all.25 = f32[256,1,128]{2,1,0:T(1,128)S(1)} all-to-all(f32[256,1,128]{2,1,0:T(1,128)S(1)} %bitcast.33), channel_id=1, replica_groups=mesh['sec'=64,'pair'=4] {'sec','pair'}, dimensions={0} | all-to-all | bytes 262144 | tf_op jit(solution)/shard_map/all_to_all | solution.py:305
  61.0 1.5 start.1
  62.5 2.0 terms.6
  65.6 1.7 collective-permute-start.11
  73.8 1.9 collective-permute-done.12.relayed_a
  75.7 1.7 collective-permute-done.13.relayed_b
  77.6 2.1 collective-permute-start.15
  79.7 2.1 collective-permute-start.14
  81.9 20.1 %all_to_all.26 = f32[256,1,128]{2,1,0:T(1,128)S(1)} all-to-all(f32[256,1,128]{2,1,0:T(1,128)S(1)} %bitcast.34), channel_id=1, replica_groups=mesh['sec'=64,'pair'=4] {'sec','pair'}, dimensions={0} | all-to-all | bytes 262144 | tf_op jit(solution)/shard_map/all_to_all | solution.py:305
  102.7 2.0 terms.7
  105.7 1.7 collective-permute-start.18
  113.9 1.9 collective-permute-done.19.relayed_a
  115.8 1.7 collective-permute-done.20.relayed_b
  117.8 2.1 collective-permute-start.22
  119.9 2.1 collective-permute-start.21
  122.0 20.1 %all_to_all.27 = f32[256,1,128]{2,1,0:T(1,128)S(1)} all-to-all(f32[256,1,128]{2,1,0:T(1,128)S(1)} %bitcast.35), channel_id=1, replica_groups=mesh['sec'=64,'pair'=4] {'sec','pair'}, dimensions={0} | all-to-all | bytes 262144 | tf_op jit(solution)/shard_map/all_to_all | solution.py:305
  142.9 2.0 terms.8
  145.9 1.7 collective-permute-start.25
  158.2 1.9 collective-permute-start.29
  160.1 2.1 collective-permute-start.28
  162.2 20.1 %all_to_all.28 = f32[256,1,128]{2,1,0:T(1,128)S(1)} all-to-all(f32[256,1,128]{2,1,0:T(1,128)S(1)} %bitcast.36), channel_id=1, replica_groups=mesh['sec'=64,'pair'=4] {'sec','pair'}, dimensions={0} | all-to-all | bytes 262144 | tf_op jit(solution)/shard_map/all_to_all | solution.py:305
  183.1 2.0 terms.9
  186.1 1.7 collective-permute-start.32
  196.2 1.7 collective-permute-done.34.relayed_b
  198.2 19.8 %all_to_all.29 = f32[256,1,128]{2,1,0:T(1,128)S(1)} all-to-all(f32[256,1,128]{2,1,0:T(1,128)S(1)} %bitcast.29), channel_id=1, replica_groups=mesh['sec'=64,'pair'=4] {'sec','pair'}, dimensions={0} | all-to-all | bytes 262144 | tf_op jit(solution)/shard_map/all_to_all | solution.py:305
  (92 shorter events, 54.8 us)
Async XLA Ops:
  2.3 11.9 %collective-permute-start.1 = (f32[4,128,128]{2,1,0:T(8,128)S(1)}, f32[4,128,128]{2,1,0:T(8,128)S(1)}, u32[]{:S(2)}, u32[]{:S(2)}) collective-permute-start(f32[4,128,128]{2,1,0:T(8,128)S(1)} %mask.1.own.state.refs_1_.refs_0_), channel_id=1, source_target_pairs={{0,4},{4,0},{8,12},{12,8},{16,20},{20,16},{24,28},{28,24},{32,36},... | collective-permute-start | bytes 786440 | tf_op jit(solution)/shard_map/ppermute | solution.py:300
  5.6 8.6 %collective-permute-start = (f32[4,128,128]{2,1,0:T(8,128)S(1)}, f32[4,128,128]{2,1,0:T(8,128)S(1)}, u32[]{:S(2)}, u32[]{:S(2)}) collective-permute-start(f32[4,128,128]{2,1,0:T(8,128)S(1)} %mask.1.own.state.refs_1_.refs_0_), channel_id=1, source_target_pairs={{4,8},{8,4},{12,16},{16,12},{20,24},{24,20},{28,32},{32,28},{36,40... | collective-permute-start | bytes 786440 | tf_op jit(solution)/shard_map/ppermute | solution.py:299
  16.2 7.3 %collective-permute-start.3 = (f32[2,128,128]{2,1,0:T(8,128)S(1)}, f32[2,128,128]{2,1,0:T(8,128)S(1)}, u32[]{:S(2)}, u32[]{:S(2)}) collective-permute-start(f32[2,128,128]{2,1,0:T(8,128)S(1)} %get-tuple-element.80), channel_id=1, source_target_pairs={{0,1},{1,0},{2,3},{3,2},{4,7},{5,6},{6,5},{7,4},{8,9},{9,8},{10,11... | collective-permute-start | bytes 393224 | tf_op jit(solution)/shard_map/ppermute | solution.py:294
  18.4 5.1 %collective-permute-start.4 = (f32[2,128,128]{2,1,0:T(8,128)S(1)}, f32[2,128,128]{2,1,0:T(8,128)S(1)}, u32[]{:S(2)}, u32[]{:S(2)}) collective-permute-start(f32[2,128,128]{2,1,0:T(8,128)S(1)} %get-tuple-element.81), channel_id=1, source_target_pairs={{0,1},{1,0},{2,3},{3,2},{4,7},{5,6},{6,5},{7,4},{8,9},{9,8},{10,11... | collective-permute-start | bytes 393224 | tf_op jit(solution)/shard_map/ppermute | solution.py:294
  20.1 9.0 %collective-permute-start.2 = (f32[4,128,128]{2,1,0:T(8,128)S(1)}, f32[4,128,128]{2,1,0:T(8,128)S(1)}, u32[]{:S(2)}, u32[]{:S(2)}) collective-permute-start(f32[4,128,128]{2,1,0:T(8,128)S(1)} %direct.5.after), channel_id=1, source_target_pairs={{0,1},{1,0},{2,3},{3,2},{4,7},{5,6},{6,5},{7,4},{8,9},{9,8},{10,11... | collective-permute-start | bytes 786440 | tf_op jit(solution)/shard_map/ppermute | solution.py:294
  23.6 5.5 %collective-permute-start.6 = (f32[2,128,128]{2,1,0:T(8,128)S(1)}, f32[2,128,128]{2,1,0:T(8,128)S(1)}, u32[]{:S(2)}, u32[]{:S(2)}) collective-permute-start(f32[2,128,128]{2,1,0:T(8,128)S(1)} %get-tuple-element.83), channel_id=1, source_target_pairs={{0,3},{1,2},{2,1},{3,0},{4,5},{5,4},{6,7},{7,6},{8,11},{9,10},{10,... | collective-permute-start | bytes 393224 | tf_op jit(solution)/shard_map/ppermute | solution.py:294
  29.3 31.7 %collective-permute-start.8 = (f32[520,128]{1,0:T(8,128)S(1)}, f32[520,128]{1,0:T(8,128)S(1)}, u32[]{:S(2)}, u32[]{:S(2)}) collective-permute-start(f32[520,128]{1,0:T(8,128)S(1)} %get-tuple-element.86.refs_4_), channel_id=1, source_target_pairs={{0,4},{4,0},{8,12},{12,8},{16,20},{20,16},{24,28},{28,24},{32,36},... | collective-permute-start | bytes 798728 | tf_op jit(solution)/shard_map/ppermute | solution.py:300
  30.4 30.6 %collective-permute-start.7 = (f32[520,128]{1,0:T(8,128)S(1)}, f32[520,128]{1,0:T(8,128)S(1)}, u32[]{:S(2)}, u32[]{:S(2)}) collective-permute-start(f32[520,128]{1,0:T(8,128)S(1)} %get-tuple-element.86.refs_4_), channel_id=1, source_target_pairs={{4,8},{8,4},{12,16},{16,12},{20,24},{24,20},{28,32},{32,28},{36,40... | collective-permute-start | bytes 798728 | tf_op jit(solution)/shard_map/ppermute | solution.py:299
  64.5 6.2 %collective-permute-start.10 = (f32[2,128,128]{2,1,0:T(8,128)S(1)}, f32[2,128,128]{2,1,0:T(8,128)S(1)}, u32[]{:S(2)}, u32[]{:S(2)}) collective-permute-start(f32[2,128,128]{2,1,0:T(8,128)S(1)} %get-tuple-element.93), channel_id=1, source_target_pairs={{0,1},{1,0},{2,3},{3,2},{4,7},{5,6},{6,5},{7,4},{8,9},{9,8},{10,11... | collective-permute-start | bytes 393224 | tf_op jit(solution)/shard_map/ppermute | solution.py:294
  65.6 5.4 %collective-permute-start.11 = (f32[2,128,128]{2,1,0:T(8,128)S(1)}, f32[2,128,128]{2,1,0:T(8,128)S(1)}, u32[]{:S(2)}, u32[]{:S(2)}) collective-permute-start(f32[2,128,128]{2,1,0:T(8,128)S(1)} %get-tuple-element.94), channel_id=1, source_target_pairs={{0,1},{1,0},{2,3},{3,2},{4,7},{5,6},{6,5},{7,4},{8,9},{9,8},{10,11... | collective-permute-start | bytes 393224 | tf_op jit(solution)/shard_map/ppermute | solution.py:294
  68.4 8.9 %collective-permute-start.9 = (f32[4,128,128]{2,1,0:T(8,128)S(1)}, f32[4,128,128]{2,1,0:T(8,128)S(1)}, u32[]{:S(2)}, u32[]{:S(2)}) collective-permute-start(f32[4,128,128]{2,1,0:T(8,128)S(1)} %direct.6.after), channel_id=1, source_target_pairs={{0,1},{1,0},{2,3},{3,2},{4,7},{5,6},{6,5},{7,4},{8,9},{9,8},{10,11... | collective-permute-start | bytes 786440 | tf_op jit(solution)/shard_map/ppermute | solution.py:294
  71.1 4.6 %collective-permute-start.12 = (f32[2,128,128]{2,1,0:T(8,128)S(1)}, f32[2,128,128]{2,1,0:T(8,128)S(1)}, u32[]{:S(2)}, u32[]{:S(2)}) collective-permute-start(f32[2,128,128]{2,1,0:T(8,128)S(1)} %get-tuple-element.95), channel_id=1, source_target_pairs={{0,3},{1,2},{2,1},{3,0},{4,5},{5,4},{6,7},{7,6},{8,11},{9,10},{10,... | collective-permute-start | bytes 393224 | tf_op jit(solution)/shard_map/ppermute | solution.py:294
  71.2 6.2 %collective-permute-start.13 = (f32[2,128,128]{2,1,0:T(8,128)S(1)}, f32[2,128,128]{2,1,0:T(8,128)S(1)}, u32[]{:S(2)}, u32[]{:S(2)}) collective-permute-start(f32[2,128,128]{2,1,0:T(8,128)S(1)} %get-tuple-element.96), channel_id=1, source_target_pairs={{0,3},{1,2},{2,1},{3,0},{4,5},{5,4},{6,7},{7,6},{8,11},{9,10},{10,... | collective-permute-start | bytes 393224 | tf_op jit(solution)/shard_map/ppermute | solution.py:294
  77.6 24.4 %collective-permute-start.15 = (f32[4,128,128]{2,1,0:T(8,128)S(1)}, f32[4,128,128]{2,1,0:T(8,128)S(1)}, u32[]{:S(2)}, u32[]{:S(2)}) collective-permute-start(f32[4,128,128]{2,1,0:T(8,128)S(1)} %get-tuple-element.104.refs_12_), channel_id=1, source_target_pairs={{0,4},{4,0},{8,12},{12,8},{16,20},{20,16},{24,28},{28,24},{32,36},... | collective-permute-start | bytes 786440 | tf_op jit(solution)/shard_map/ppermute | solution.py:300
  79.7 22.3 %collective-permute-start.14 = (f32[4,128,128]{2,1,0:T(8,128)S(1)}, f32[4,128,128]{2,1,0:T(8,128)S(1)}, u32[]{:S(2)}, u32[]{:S(2)}) collective-permute-start(f32[4,128,128]{2,1,0:T(8,128)S(1)} %get-tuple-element.104.refs_12_), channel_id=1, source_target_pairs={{4,8},{8,4},{12,16},{16,12},{20,24},{24,20},{28,32},{32,28},{36,40... | collective-permute-start | bytes 786440 | tf_op jit(solution)/shard_map/ppermute | solution.py:299
  104.6 6.2 %collective-permute-start.17 = (f32[2,128,128]{2,1,0:T(8,128)S(1)}, f32[2,128,128]{2,1,0:T(8,128)S(1)}, u32[]{:S(2)}, u32[]{:S(2)}) collective-permute-start(f32[2,128,128]{2,1,0:T(8,128)S(1)} %get-tuple-element.109), channel_id=1, source_target_pairs={{0,1},{1,0},{2,3},{3,2},{4,7},{5,6},{6,5},{7,4},{8,9},{9,8},{10,11... | collective-permute-start | bytes 393224 | tf_op jit(solution)/shard_map/ppermute | solution.py:294
  105.7 5.4 %collective-permute-start.18 = (f32[2,128,128]{2,1,0:T(8,128)S(1)}, f32[2,128,128]{2,1,0:T(8,128)S(1)}, u32[]{:S(2)}, u32[]{:S(2)}) collective-permute-start(f32[2,128,128]{2,1,0:T(8,128)S(1)} %get-tuple-element.110), channel_id=1, source_target_pairs={{0,1},{1,0},{2,3},{3,2},{4,7},{5,6},{6,5},{7,4},{8,9},{9,8},{10,11... | collective-permute-start | bytes 393224 | tf_op jit(solution)/shard_map/ppermute | solution.py:294
  108.6 8.9 %collective-permute-start.16 = (f32[4,128,128]{2,1,0:T(8,128)S(1)}, f32[4,128,128]{2,1,0:T(8,128)S(1)}, u32[]{:S(2)}, u32[]{:S(2)}) collective-permute-start(f32[4,128,128]{2,1,0:T(8,128)S(1)} %direct.7.after), channel_id=1, source_target_pairs={{0,1},{1,0},{2,3},{3,2},{4,7},{5,6},{6,5},{7,4},{8,9},{9,8},{10,11... | collective-permute-start | bytes 786440 | tf_op jit(solution)/shard_map/ppermute | solution.py:294
  111.3 6.2 %collective-permute-start.20 = (f32[2,128,128]{2,1,0:T(8,128)S(1)}, f32[2,128,128]{2,1,0:T(8,128)S(1)}, u32[]{:S(2)}, u32[]{:S(2)}) collective-permute-start(f32[2,128,128]{2,1,0:T(8,128)S(1)} %get-tuple-element.112), channel_id=1, source_target_pairs={{0,3},{1,2},{2,1},{3,0},{4,5},{5,4},{6,7},{7,6},{8,11},{9,10},{10,... | collective-permute-start | bytes 393224 | tf_op jit(solution)/shard_map/ppermute | solution.py:294
  117.8 24.4 %collective-permute-start.22 = (f32[4,128,128]{2,1,0:T(8,128)S(1)}, f32[4,128,128]{2,1,0:T(8,128)S(1)}, u32[]{:S(2)}, u32[]{:S(2)}) collective-permute-start(f32[4,128,128]{2,1,0:T(8,128)S(1)} %get-tuple-element.121.refs_12_), channel_id=1, source_target_pairs={{0,4},{4,0},{8,12},{12,8},{16,20},{20,16},{24,28},{28,24},{32,36},... | collective-permute-start | bytes 786440 | tf_op jit(solution)/shard_map/ppermute | solution.py:300
  119.9 22.3 %collective-permute-start.21 = (f32[4,128,128]{2,1,0:T(8,128)S(1)}, f32[4,128,128]{2,1,0:T(8,128)S(1)}, u32[]{:S(2)}, u32[]{:S(2)}) collective-permute-start(f32[4,128,128]{2,1,0:T(8,128)S(1)} %get-tuple-element.121.refs_12_), channel_id=1, source_target_pairs={{4,8},{8,4},{12,16},{16,12},{20,24},{24,20},{28,32},{32,28},{36,40... | collective-permute-start | bytes 786440 | tf_op jit(solution)/shard_map/ppermute | solution.py:299
  144.9 6.4 %collective-permute-start.24 = (f32[2,128,128]{2,1,0:T(8,128)S(1)}, f32[2,128,128]{2,1,0:T(8,128)S(1)}, u32[]{:S(2)}, u32[]{:S(2)}) collective-permute-start(f32[2,128,128]{2,1,0:T(8,128)S(1)} %get-tuple-element.126), channel_id=1, source_target_pairs={{0,1},{1,0},{2,3},{3,2},{4,7},{5,6},{6,5},{7,4},{8,9},{9,8},{10,11... | collective-permute-start | bytes 393224 | tf_op jit(solution)/shard_map/ppermute | solution.py:294
  145.9 5.4 %collective-permute-start.25 = (f32[2,128,128]{2,1,0:T(8,128)S(1)}, f32[2,128,128]{2,1,0:T(8,128)S(1)}, u32[]{:S(2)}, u32[]{:S(2)}) collective-permute-start(f32[2,128,128]{2,1,0:T(8,128)S(1)} %get-tuple-element.127), channel_id=1, source_target_pairs={{0,1},{1,0},{2,3},{3,2},{4,7},{5,6},{6,5},{7,4},{8,9},{9,8},{10,11... | collective-permute-start | bytes 393224 | tf_op jit(solution)/shard_map/ppermute | solution.py:294
  148.8 6.7 %collective-permute-start.23 = (f32[4,128,128]{2,1,0:T(8,128)S(1)}, f32[4,128,128]{2,1,0:T(8,128)S(1)}, u32[]{:S(2)}, u32[]{:S(2)}) collective-permute-start(f32[4,128,128]{2,1,0:T(8,128)S(1)} %direct.8.after), channel_id=1, source_target_pairs={{0,1},{1,0},{2,3},{3,2},{4,7},{5,6},{6,5},{7,4},{8,9},{9,8},{10,11... | collective-permute-start | bytes 786440 | tf_op jit(solution)/shard_map/ppermute | solution.py:294
  151.4 5.1 %collective-permute-start.26 = (f32[2,128,128]{2,1,0:T(8,128)S(1)}, f32[2,128,128]{2,1,0:T(8,128)S(1)}, u32[]{:S(2)}, u32[]{:S(2)}) collective-permute-start(f32[2,128,128]{2,1,0:T(8,128)S(1)} %get-tuple-element.128), channel_id=1, source_target_pairs={{0,3},{1,2},{2,1},{3,0},{4,5},{5,4},{6,7},{7,6},{8,11},{9,10},{10,... | collective-permute-start | bytes 393224 | tf_op jit(solution)/shard_map/ppermute | solution.py:294
  151.5 6.4 %collective-permute-start.27 = (f32[2,128,128]{2,1,0:T(8,128)S(1)}, f32[2,128,128]{2,1,0:T(8,128)S(1)}, u32[]{:S(2)}, u32[]{:S(2)}) collective-permute-start(f32[2,128,128]{2,1,0:T(8,128)S(1)} %get-tuple-element.129), channel_id=1, source_target_pairs={{0,3},{1,2},{2,1},{3,0},{4,5},{5,4},{6,7},{7,6},{8,11},{9,10},{10,... | collective-permute-start | bytes 393224 | tf_op jit(solution)/shard_map/ppermute | solution.py:294
  158.2 24.1 %collective-permute-start.29 = (f32[4,128,128]{2,1,0:T(8,128)S(1)}, f32[4,128,128]{2,1,0:T(8,128)S(1)}, u32[]{:S(2)}, u32[]{:S(2)}) collective-permute-start(f32[4,128,128]{2,1,0:T(8,128)S(1)} %get-tuple-element.138.refs_12_), channel_id=1, source_target_pairs={{0,4},{4,0},{8,12},{12,8},{16,20},{20,16},{24,28},{28,24},{32,36},... | collective-permute-start | bytes 786440 | tf_op jit(solution)/shard_map/ppermute | solution.py:300
  160.1 22.3 %collective-permute-start.28 = (f32[4,128,128]{2,1,0:T(8,128)S(1)}, f32[4,128,128]{2,1,0:T(8,128)S(1)}, u32[]{:S(2)}, u32[]{:S(2)}) collective-permute-start(f32[4,128,128]{2,1,0:T(8,128)S(1)} %get-tuple-element.138.refs_12_), channel_id=1, source_target_pairs={{4,8},{8,4},{12,16},{16,12},{20,24},{24,20},{28,32},{32,28},{36,40... | collective-permute-start | bytes 786440 | tf_op jit(solution)/shard_map/ppermute | solution.py:299
  185.0 6.2 %collective-permute-start.31 = (f32[2,128,128]{2,1,0:T(8,128)S(1)}, f32[2,128,128]{2,1,0:T(8,128)S(1)}, u32[]{:S(2)}, u32[]{:S(2)}) collective-permute-start(f32[2,128,128]{2,1,0:T(8,128)S(1)} %get-tuple-element.143), channel_id=1, source_target_pairs={{0,1},{1,0},{2,3},{3,2},{4,7},{5,6},{6,5},{7,4},{8,9},{9,8},{10,11... | collective-permute-start | bytes 393224 | tf_op jit(solution)/shard_map/ppermute | solution.py:294
  186.1 5.4 %collective-permute-start.32 = (f32[2,128,128]{2,1,0:T(8,128)S(1)}, f32[2,128,128]{2,1,0:T(8,128)S(1)}, u32[]{:S(2)}, u32[]{:S(2)}) collective-permute-start(f32[2,128,128]{2,1,0:T(8,128)S(1)} %get-tuple-element.144), channel_id=1, source_target_pairs={{0,1},{1,0},{2,3},{3,2},{4,7},{5,6},{6,5},{7,4},{8,9},{9,8},{10,11... | collective-permute-start | bytes 393224 | tf_op jit(solution)/shard_map/ppermute | solution.py:294
  189.0 6.5 %collective-permute-start.30 = (f32[4,128,128]{2,1,0:T(8,128)S(1)}, f32[4,128,128]{2,1,0:T(8,128)S(1)}, u32[]{:S(2)}, u32[]{:S(2)}) collective-permute-start(f32[4,128,128]{2,1,0:T(8,128)S(1)} %direct.9.after), channel_id=1, source_target_pairs={{0,1},{1,0},{2,3},{3,2},{4,7},{5,6},{6,5},{7,4},{8,9},{9,8},{10,11... | collective-permute-start | bytes 786440 | tf_op jit(solution)/shard_map/ppermute | solution.py:294
  191.7 6.2 %collective-permute-start.34 = (f32[2,128,128]{2,1,0:T(8,128)S(1)}, f32[2,128,128]{2,1,0:T(8,128)S(1)}, u32[]{:S(2)}, u32[]{:S(2)}) collective-permute-start(f32[2,128,128]{2,1,0:T(8,128)S(1)} %get-tuple-element.146), channel_id=1, source_target_pairs={{0,3},{1,2},{2,1},{3,0},{4,5},{5,4},{6,7},{7,6},{8,11},{9,10},{10,... | collective-permute-start | bytes 393224 | tf_op jit(solution)/shard_map/ppermute | solution.py:294
  (8 other events, 50.8 us)

commit v2 on v0

--- a/solution.py
+++ b/solution.py
@@ -74,7 +74,7 @@
 def mix(group, weights, z, target, out, chunks):
     height = B // chunks
 
-    def part(start, width, at):
+    def part(start, width, at, out, place):
         first = target * LOCAL + start
         acc = [None] * width
         for k in range(TERMS):
@@ -84,20 +84,24 @@
                     term = weights[k * 256 + (first + j) * 16 + group[0] * LOCAL + q] * block
                     acc[j] = term if acc[j] is None else acc[j] + term
         for j in range(width):
-            out[start + j, at, :] = acc[j]
+            out[place + j, at, :] = acc[j]
 
     def rows(r, carry):
-        part(0, LOCAL, pl.ds(pl.multiple_of(r * height, height), height))
+        part(0, LOCAL, pl.ds(pl.multiple_of(r * height, height), height), out, 0)
         return carry
 
     if chunks > 1:
         lax.fori_loop(0, chunks, rows, 0)
     else:
         for half in range(2):
-            part(2 * half, 2, slice(None))
-
-
-def terms_kernel(group, sector, shift, weights, own, by_chip, by_core, left2, right2, z, far, vec2):
+            if isinstance(out, tuple):
+                part(2 * half, 2, slice(None), out[half], 0)
+            else:
+                part(2 * half, 2, slice(None), out, 2 * half)
+
+
+def terms_kernel(group, sector, shift, weights, own, by_chip, by_core, left2, right2, z, *refs):
+    *far, vec2 = refs
     odd = lax.rem(sector[0], 2)
     for p in range(LOCAL):
         vec2[1, p] = jnp.concatenate(halves(own[p]), axis=1)
@@ -113,7 +117,7 @@
             both = jnp.concatenate([xh, xl], axis=1)
             y = jnp.dot(lhs, jnp.concatenate([both, both], axis=0), preferred_element_type=f32)
             z[k * LOCAL + q] = y[:, :B] + y[:, B:]
-    mix(group, weights, z, group[0] ^ 2, far, 1)
+    mix(group, weights, z, group[0] ^ 2, tuple(far) if len(far) > 1 else far[0], 1)
 
 
 def direct_kernel(group, sector, weights, z, direct):
@@ -124,9 +128,9 @@
     mix(group, weights, z, group[0] ^ (3 - 2 * lax.rem(sector[0], 2)), relayed, 4)
 
 
-def relay_kernel(relayed, far, out):
-    for p in range(LOCAL):
-        out[p] = relayed[p] + far[p]
+def relay_kernel(first, relayed, far, out):
+    for p in range(far.shape[0]):
+        out[p] = relayed[first + p] + far[p]
 
 
 def own_kernel(group, weights, z, own):
@@ -224,10 +228,15 @@
     return jnp.sum(jnp.sum(block, axis=0, keepdims=True), axis=1, keepdims=True)
 
 
+def summed(own, direct, relayed, p):
+    width = LOCAL // len(relayed)
+    return own[p] + (direct[p] + relayed[p // width][p % width])
+
+
 def first_stats_kernel(own, direct, relayed, state, left_diag, pack, stats):
     a, b = jnp.zeros((B, B), f32), jnp.zeros((B, B), f32)
     for p in range(LOCAL):
-        i = own[p] + (direct[p] + relayed[p])
+        i = summed(own, direct, (relayed,), p)
         s = state[p]
         pack[p * B:(p + 1) * B, :] = i
         a = a + s * i
@@ -236,10 +245,11 @@
     stats[...] = jnp.broadcast_to(put_lanes([sum_all(a), sum_all(b)]), stats.shape)
 
 
-def stats_kernel(own, direct, relayed, state, corr, image, *outs):
+def stats_kernel(streams, own, direct, *refs):
+    relayed, (state, corr, image), outs = refs[:streams], refs[streams:streams + 3], refs[streams + 3:]
     acc = [jnp.zeros((B, B), f32) for _ in range(5)]
     for p in range(LOCAL):
-        ic = own[p] + (direct[p] + relayed[p])
+        ic = summed(own, direct, relayed, p)
         s, c, i = state[p], corr[p], image[p]
         if len(outs) > 1:
             outs[0][p] = ic
@@ -299,18 +309,22 @@
     stats_shape = arr(devices, B)
     carry_shape = arr(8, B)
 
-    def shares(vectors, left2, right2):
-        z, far = call(
-            terms_kernel, "terms", [SM] * 4 + [VM] * 5, [TERM_BLOCKS, BLOCK],
+    def shares(vectors, left2, right2, streams):
+        width = LOCAL // streams
+        z, *far = call(
+            terms_kernel, "terms", [SM] * 4 + [VM] * 5, [TERM_BLOCKS] + [arr(width, B, B)] * streams,
             [pltpu.VMEM((3, LOCAL, B, 2 * B), bf16)],
         )(group, sector, sector_shift, weights, *vectors, left2, right2)
-        far = swap(far, 1, 3)
+        far = [swap(x, 1, 3) for x in far]
         (direct,) = call(direct_kernel, "direct", [SM] * 3 + [VM], [BLOCK])(group, sector, weights, z)
         (relayed,) = call(relayed_kernel, "relayed", [SM] * 3 + [VM, ANY], [BLOCK])(group, sector, weights, z, direct)
         direct = swap(direct, 1, 3)
-        (relayed,) = call(relay_kernel, "relay", [VM] * 2, [BLOCK])(relayed, far)
+        relayed = [
+            swap(call(functools.partial(relay_kernel, n * width), "relay", [VM] * 2, [arr(width, B, B)])(relayed, x)[0], 3, 1)
+            for n, x in enumerate(far)
+        ]
         (own,) = call(own_kernel, "own", [SM, SM, VM], [BLOCK])(group, weights, z)
-        return own, direct, swap(relayed, 3, 1)
+        return own, direct, *relayed
 
     (state,) = call(mask_kernel, "mask", [SM, VM], [BLOCK])(block_rows, psi)
     states = (state, *neighbours(state))
@@ -319,7 +333,7 @@
         [arr(TERMS, B, 2 * B, dtype=bf16), arr(TERMS, LOCAL, B, 2 * B, dtype=bf16), BLOCK, arr(8, B), arr(LOCAL, 8, B)],
     )(group, sector_shift, block_rows, weights, left, right_env)
 
-    parts = shares(states, left2, right2)
+    parts = shares(states, left2, right2, 1)
     pack, stats = call(first_stats_kernel, "first_stats", [VM] * 5, [arr(PACK, B), stats_shape])(
         *parts, state, left_diag)
     packs = (pack, *neighbours(pack))
@@ -329,9 +343,11 @@
     images, diags, corrs = out[:3], (diag, *out[3:5]), out[5:8]
 
     for step in range(ITERS):
-        parts = shares(corrs, left2, right2)
+        streams = 2 if step < ITERS - 1 else 1
+        parts = shares(corrs, left2, right2, streams)
         outs = [BLOCK, stats_shape] if step < ITERS - 1 else [stats_shape]
-        *image_corr, stats = call(stats_kernel, "stats", [VM] * 6, outs)(*parts, states[0], corrs[0], images[0])
+        *image_corr, stats = call(functools.partial(stats_kernel, streams), "stats", [VM] * (5 + streams), outs)(
+            *parts, states[0], corrs[0], images[0])
         got = exchange(stats, devices)
         if step < ITERS - 1:
             more = (*image_corr, *neighbours(*image_corr))

time: 214 us -> 217 us (1.014)
  blocking collectives: 104 us -> 107 us
  waiting for transfers between devices: 30.2 us -> 27.2 us
  starting transfers between devices: 39.4 us -> 42 us
    ppermute x15 -> x21, starting transfers between devices: 14.7 us -> 20.8 us  [swap(): return lax.ppermute(x, ('sec', 'pair'), perm)]
    ppermute x15 -> x21, waiting for transfers between devices: 29.7 us -> 26.7 us  [swap(): return lax.ppermute(x, ('sec', 'pair'), perm)]
    ppermute x5, starting transfers between devices: 13 us -> 10.1 us  [neighbours(): by_core = lax.ppermute(x, 'sec', [(i, i ^ 1) for i in range(n)])]
    all_to_all x5, blocking collectives: 104 us -> 107 us  [exchange(): got = lax.all_to_all(stats.reshape(devices, 1, B), ('sec', 'pair'), 0, 0)]
    pallas_call x14 -> x17, Pallas kernels: 11 us -> 11.1 us  [the longest x5 9.85 us: shares(): call(terms_kernel, 'terms', [SM] * 4 + [VM] * 5, [TERM_BLOCKS] + [arr(wid...]
  transfers between devices with their start and end apart: 25 -> 31, of which waited for: 15 -> 14; matrix products, arithmetic and copies ran while one was open for 0% -> 0% of each run, Pallas kernels for 9% -> 9%
where the time goes in v2:
time: 217 us; the launch traced here: 216 us
  blocking collectives  107 us (49%)
  starting transfers between devices  42 us (19%)
  Pallas kernels  33.2 us (15%)
  waiting for transfers between devices  27.2 us (13%)
  local copies, waits for them, and re-layouts  4.16 us (2%)
    all_to_all x5, blocking collectives, exchange(): got = lax.all_to_all(stats.reshape(devices, 1, B), ('sec', 'pair'), 0, 0)  107 us
    ppermute x21, waiting for transfers between devices, swap(): return lax.ppermute(x, ('sec', 'pair'), perm)  26.7 us
    ppermute x21, starting transfers between devices, swap(): return lax.ppermute(x, ('sec', 'pair'), perm)  20.8 us
    ppermute x5, starting transfers between devices, neighbours(): lax.ppermute(x, 'sec', [(i, i + 1 if i % 2 else i - 1) for i in range(1,...  11.1 us
    ppermute x5, starting transfers between devices, neighbours(): by_core = lax.ppermute(x, 'sec', [(i, i ^ 1) for i in range(n)])  10.1 us
    pallas_call x5, Pallas kernels, shares(): call(terms_kernel, 'terms', [SM] * 4 + [VM] * 5, [TERM_BLOCKS] + [arr(wid...  9.85 us
    pallas_call x5, Pallas kernels, shares(): call(relayed_kernel, 'relayed', [SM] * 3 + [VM, ANY], [BLOCK])  5.86 us
    pallas_call x5, Pallas kernels, shares(): own, = call(own_kernel, 'own', [SM, SM, VM], [BLOCK])(group, weights, z)  5.86 us
  transfers between devices with their start and end apart: 31, of which 14 were waited for; matrix products, arithmetic and copies ran while one was open for 0% of the time, Pallas kernels for 9%

profile of v2, /device:TPU:1, one launch (start us, length us, event | category | flops | bytes accessed | tf_op | source)
XLA Modules:
  0.0 216.0 jit_solution(14365993184556334598)
XLA Ops:
  2.3 3.3 %collective-permute-start.1 = (f32[4,128,128]{2,1,0:T(8,128)S(1)}, f32[4,128,128]{2,1,0:T(8,128)S(1)}, u32[]{:S(2)}, u32[]{:S(2)}) collective-permute-start(f32[4,128,128]{2,1,0:T(8,128)S(1)} %mask.1.own.state.refs_1_.refs_2_.refs_0_), channel_id=1, source_target_pairs={{0,4},{4,0},{8,12},{12,8},{16,20},{20,16},{24,28},{28,24},{32,36},... | collective-permute-start | bytes 786440 | tf_op jit(solution)/shard_map/ppermute | solution.py:292
  5.6 1.9 collective-permute-start
  8.4 1.4 copy-done
  13.3 2.0 terms.5
  15.2 1.7 collective-permute-start.3
  23.1 4.6 %collective-permute-done.2.direct = f32[4,128,128]{2,1,0:T(8,128)S(1)} collective-permute-done((f32[4,128,128]{2,1,0:T(8,128)S(1)}, f32[4,128,128]{2,1,0:T(8,128)S(1)}, u32[]{:S(2)}, u32[]{:S(2)}) %collective-permute-start.2) | collective-permute-done | bytes 262176 | tf_op jit(solution)/shard_map/ppermute | solution.py:286
  27.8 1.8 collective-permute-start.6
  29.6 3.3 %collective-permute-start.5 = (f32[520,128]{1,0:T(8,128)S(1)}, f32[520,128]{1,0:T(8,128)S(1)}, u32[]{:S(2)}, u32[]{:S(2)}) collective-permute-start(f32[520,128]{1,0:T(8,128)S(1)} %get-tuple-element.71.refs_4_), channel_id=1, source_target_pairs={{4,8},{8,4},{12,16},{16,12},{20,24},{24,20},{28,32},{32,28},{36,40... | collective-permute-start | bytes 798728 | tf_op jit(solution)/shard_map/ppermute | solution.py:291
  32.9 26.8 %all_to_all.25 = f32[256,1,128]{2,1,0:T(1,128)S(1)} all-to-all(f32[256,1,128]{2,1,0:T(1,128)S(1)} %bitcast.33), channel_id=1, replica_groups=mesh['sec'=64,'pair'=4] {'sec','pair'}, dimensions={0} | all-to-all | bytes 262144 | tf_op jit(solution)/shard_map/all_to_all | solution.py:297
  60.4 2.0 terms.6
  63.5 1.7 collective-permute-start.10
  68.9 1.5 collective-permute-start.11
  71.6 2.2 %collective-permute-done.9.refs_0_ = f32[2,128,128]{2,1,0:T(8,128)S(1)} collective-permute-done((f32[2,128,128]{2,1,0:T(8,128)S(1)}, f32[2,128,128]{2,1,0:T(8,128)S(1)}, u32[]{:S(2)}, u32[]{:S(2)}) %collective-permute-start.9) | collective-permute-done | bytes 131104 | tf_op jit(solution)/shard_map/ppermute | solution.py:286
  76.6 1.9 collective-permute-start.12
  78.5 20.3 %all_to_all.26 = f32[256,1,128]{2,1,0:T(1,128)S(1)} all-to-all(f32[256,1,128]{2,1,0:T(1,128)S(1)} %bitcast.34), channel_id=1, replica_groups=mesh['sec'=64,'pair'=4] {'sec','pair'}, dimensions={0} | all-to-all | bytes 262144 | tf_op jit(solution)/shard_map/all_to_all | solution.py:297
  99.4 2.0 terms.7
  102.5 1.7 collective-permute-start.17
  110.4 2.4 %collective-permute-done.16.refs_0_ = f32[2,128,128]{2,1,0:T(8,128)S(1)} collective-permute-done((f32[2,128,128]{2,1,0:T(8,128)S(1)}, f32[2,128,128]{2,1,0:T(8,128)S(1)}, u32[]{:S(2)}, u32[]{:S(2)}) %collective-permute-start.16) | collective-permute-done | bytes 131104 | tf_op jit(solution)/shard_map/ppermute | solution.py:286
  115.7 1.9 collective-permute-start.19
  117.6 20.1 %all_to_all.27 = f32[256,1,128]{2,1,0:T(1,128)S(1)} all-to-all(f32[256,1,128]{2,1,0:T(1,128)S(1)} %bitcast.35), channel_id=1, replica_groups=mesh['sec'=64,'pair'=4] {'sec','pair'}, dimensions={0} | all-to-all | bytes 262144 | tf_op jit(solution)/shard_map/all_to_all | solution.py:297
  138.3 2.0 terms.8
  142.7 1.8 collective-permute-start.21
  146.8 4.2 %collective-permute-done.24.far = f32[2,128,128]{2,1,0:T(8,128)S(1)} collective-permute-done((f32[2,128,128]{2,1,0:T(8,128)S(1)}, f32[2,128,128]{2,1,0:T(8,128)S(1)}, u32[]{:S(2)}, u32[]{:S(2)}) %collective-permute-start.24) | collective-permute-done | bytes 131104 | tf_op jit(solution)/shard_map/ppermute | solution.py:286
  152.4 2.6 %collective-permute-done.25.refs_1_ = f32[2,128,128]{2,1,0:T(8,128)S(1)} collective-permute-done((f32[2,128,128]{2,1,0:T(8,128)S(1)}, f32[2,128,128]{2,1,0:T(8,128)S(1)}, u32[]{:S(2)}, u32[]{:S(2)}) %collective-permute-start.25) | collective-permute-done | bytes 131104 | tf_op jit(solution)/shard_map/ppermute | solution.py:286
  155.3 2.7 %collective-permute-start.27 = (f32[4,128,128]{2,1,0:T(8,128)S(1)}, f32[4,128,128]{2,1,0:T(8,128)S(1)}, u32[]{:S(2)}, u32[]{:S(2)}) collective-permute-start(f32[4,128,128]{2,1,0:T(8,128)S(1)} %get-tuple-element.117.refs_12_), channel_id=1, source_target_pairs={{0,4},{4,0},{8,12},{12,8},{16,20},{20,16},{24,28},{28,24},{32,36},... | collective-permute-start | bytes 786440 | tf_op jit(solution)/shard_map/ppermute | solution.py:292
  157.9 2.1 collective-permute-start.26
  160.0 19.6 %all_to_all.28 = f32[256,1,128]{2,1,0:T(1,128)S(1)} all-to-all(f32[256,1,128]{2,1,0:T(1,128)S(1)} %bitcast.36), channel_id=1, replica_groups=mesh['sec'=64,'pair'=4] {'sec','pair'}, dimensions={0} | all-to-all | bytes 262144 | tf_op jit(solution)/shard_map/all_to_all | solution.py:297
  180.2 2.0 terms.9
  185.6 1.8 collective-permute-start.28
  190.0 2.1 collective-permute-done.28.direct
  192.1 2.5 %collective-permute-done.30.refs_0_ = f32[4,128,128]{2,1,0:T(8,128)S(1)} collective-permute-done((f32[4,128,128]{2,1,0:T(8,128)S(1)}, f32[4,128,128]{2,1,0:T(8,128)S(1)}, u32[]{:S(2)}, u32[]{:S(2)}) %collective-permute-start.30) | collective-permute-done | bytes 262176 | tf_op jit(solution)/shard_map/ppermute | solution.py:286
  194.9 20.1 %all_to_all.29 = f32[256,1,128]{2,1,0:T(1,128)S(1)} all-to-all(f32[256,1,128]{2,1,0:T(1,128)S(1)} %bitcast.29), channel_id=1, replica_groups=mesh['sec'=64,'pair'=4] {'sec','pair'}, dimensions={0} | all-to-all | bytes 262144 | tf_op jit(solution)/shard_map/all_to_all | solution.py:297
  (87 shorter events, 46.5 us)
Async XLA Ops:
  2.3 10.5 %collective-permute-start.1 = (f32[4,128,128]{2,1,0:T(8,128)S(1)}, f32[4,128,128]{2,1,0:T(8,128)S(1)}, u32[]{:S(2)}, u32[]{:S(2)}) collective-permute-start(f32[4,128,128]{2,1,0:T(8,128)S(1)} %mask.1.own.state.refs_1_.refs_2_.refs_0_), channel_id=1, source_target_pairs={{0,4},{4,0},{8,12},{12,8},{16,20},{20,16},{24,28},{28,24},{32,36},... | collective-permute-start | bytes 786440 | tf_op jit(solution)/shard_map/ppermute | solution.py:292
  5.6 7.7 %collective-permute-start = (f32[4,128,128]{2,1,0:T(8,128)S(1)}, f32[4,128,128]{2,1,0:T(8,128)S(1)}, u32[]{:S(2)}, u32[]{:S(2)}) collective-permute-start(f32[4,128,128]{2,1,0:T(8,128)S(1)} %mask.1.own.state.refs_1_.refs_2_.refs_0_), channel_id=1, source_target_pairs={{4,8},{8,4},{12,16},{16,12},{20,24},{24,20},{28,32},{32,28},{36,40... | collective-permute-start | bytes 786440 | tf_op jit(solution)/shard_map/ppermute | solution.py:291
  8.4 1.4 copy-start
  15.2 6.5 %collective-permute-start.3 = (f32[4,128,128]{2,1,0:T(8,128)S(1)}, f32[4,128,128]{2,1,0:T(8,128)S(1)}, u32[]{:S(2)}, u32[]{:S(2)}) collective-permute-start(f32[4,128,128]{2,1,0:T(8,128)S(1)} %get-tuple-element.68), channel_id=1, source_target_pairs={{0,1},{1,0},{2,3},{3,2},{4,7},{5,6},{6,5},{7,4},{8,9},{9,8},{10,11... | collective-permute-start | bytes 786440 | tf_op jit(solution)/shard_map/ppermute | solution.py:286
  19.3 8.3 %collective-permute-start.2 = (f32[4,128,128]{2,1,0:T(8,128)S(1)}, f32[4,128,128]{2,1,0:T(8,128)S(1)}, u32[]{:S(2)}, u32[]{:S(2)}) collective-permute-start(f32[4,128,128]{2,1,0:T(8,128)S(1)} %direct.5.after), channel_id=1, source_target_pairs={{0,1},{1,0},{2,3},{3,2},{4,7},{5,6},{6,5},{7,4},{8,9},{9,8},{10,11... | collective-permute-start | bytes 786440 | tf_op jit(solution)/shard_map/ppermute | solution.py:286
  21.8 5.8 %collective-permute-start.4 = (f32[4,128,128]{2,1,0:T(8,128)S(1)}, f32[4,128,128]{2,1,0:T(8,128)S(1)}, u32[]{:S(2)}, u32[]{:S(2)}) collective-permute-start(f32[4,128,128]{2,1,0:T(8,128)S(1)} %relay.8), channel_id=1, source_target_pairs={{0,3},{1,2},{2,1},{3,0},{4,5},{5,4},{6,7},{7,6},{8,11},{9,10},{10,... | collective-permute-start | bytes 786440 | tf_op jit(solution)/shard_map/ppermute | solution.py:286
  27.8 31.8 %collective-permute-start.6 = (f32[520,128]{1,0:T(8,128)S(1)}, f32[520,128]{1,0:T(8,128)S(1)}, u32[]{:S(2)}, u32[]{:S(2)}) collective-permute-start(f32[520,128]{1,0:T(8,128)S(1)} %get-tuple-element.71.refs_4_), channel_id=1, source_target_pairs={{0,4},{4,0},{8,12},{12,8},{16,20},{20,16},{24,28},{28,24},{32,36},... | collective-permute-start | bytes 798728 | tf_op jit(solution)/shard_map/ppermute | solution.py:292
  29.6 30.1 %collective-permute-start.5 = (f32[520,128]{1,0:T(8,128)S(1)}, f32[520,128]{1,0:T(8,128)S(1)}, u32[]{:S(2)}, u32[]{:S(2)}) collective-permute-start(f32[520,128]{1,0:T(8,128)S(1)} %get-tuple-element.71.refs_4_), channel_id=1, source_target_pairs={{4,8},{8,4},{12,16},{16,12},{20,24},{24,20},{28,32},{32,28},{36,40... | collective-permute-start | bytes 798728 | tf_op jit(solution)/shard_map/ppermute | solution.py:291
  62.4 6.1 %collective-permute-start.8 = (f32[2,128,128]{2,1,0:T(8,128)S(1)}, f32[2,128,128]{2,1,0:T(8,128)S(1)}, u32[]{:S(2)}, u32[]{:S(2)}) collective-permute-start(f32[2,128,128]{2,1,0:T(8,128)S(1)} %get-tuple-element.78), channel_id=1, source_target_pairs={{0,1},{1,0},{2,3},{3,2},{4,7},{5,6},{6,5},{7,4},{8,9},{9,8},{10,11... | collective-permute-start | bytes 393224 | tf_op jit(solution)/shard_map/ppermute | solution.py:286
  63.5 5.4 %collective-permute-start.10 = (f32[2,128,128]{2,1,0:T(8,128)S(1)}, f32[2,128,128]{2,1,0:T(8,128)S(1)}, u32[]{:S(2)}, u32[]{:S(2)}) collective-permute-start(f32[2,128,128]{2,1,0:T(8,128)S(1)} %get-tuple-element.79), channel_id=1, source_target_pairs={{0,1},{1,0},{2,3},{3,2},{4,7},{5,6},{6,5},{7,4},{8,9},{9,8},{10,11... | collective-permute-start | bytes 393224 | tf_op jit(solution)/shard_map/ppermute | solution.py:286
  66.3 8.9 %collective-permute-start.7 = (f32[4,128,128]{2,1,0:T(8,128)S(1)}, f32[4,128,128]{2,1,0:T(8,128)S(1)}, u32[]{:S(2)}, u32[]{:S(2)}) collective-permute-start(f32[4,128,128]{2,1,0:T(8,128)S(1)} %direct.6.after), channel_id=1, source_target_pairs={{0,1},{1,0},{2,3},{3,2},{4,7},{5,6},{6,5},{7,4},{8,9},{9,8},{10,11... | collective-permute-start | bytes 786440 | tf_op jit(solution)/shard_map/ppermute | solution.py:286
  68.5 5.2 %collective-permute-start.9 = (f32[2,128,128]{2,1,0:T(8,128)S(1)}, f32[2,128,128]{2,1,0:T(8,128)S(1)}, u32[]{:S(2)}, u32[]{:S(2)}) collective-permute-start(f32[2,128,128]{2,1,0:T(8,128)S(1)} %relay.9), channel_id=1, source_target_pairs={{0,3},{1,2},{2,1},{3,0},{4,5},{5,4},{6,7},{7,6},{8,11},{9,10},{10,... | collective-permute-start | bytes 393224 | tf_op jit(solution)/shard_map/ppermute | solution.py:286
  68.9 6.3 %collective-permute-start.11 = (f32[2,128,128]{2,1,0:T(8,128)S(1)}, f32[2,128,128]{2,1,0:T(8,128)S(1)}, u32[]{:S(2)}, u32[]{:S(2)}) collective-permute-start(f32[2,128,128]{2,1,0:T(8,128)S(1)} %relay.10), channel_id=1, source_target_pairs={{0,3},{1,2},{2,1},{3,0},{4,5},{5,4},{6,7},{7,6},{8,11},{9,10},{10,... | collective-permute-start | bytes 393224 | tf_op jit(solution)/shard_map/ppermute | solution.py:286
  75.5 23.4 %collective-permute-start.13 = (f32[4,128,128]{2,1,0:T(8,128)S(1)}, f32[4,128,128]{2,1,0:T(8,128)S(1)}, u32[]{:S(2)}, u32[]{:S(2)}) collective-permute-start(f32[4,128,128]{2,1,0:T(8,128)S(1)} %get-tuple-element.87.refs_12_), channel_id=1, source_target_pairs={{0,4},{4,0},{8,12},{12,8},{16,20},{20,16},{24,28},{28,24},{32,36},... | collective-permute-start | bytes 786440 | tf_op jit(solution)/shard_map/ppermute | solution.py:292
  76.6 22.2 %collective-permute-start.12 = (f32[4,128,128]{2,1,0:T(8,128)S(1)}, f32[4,128,128]{2,1,0:T(8,128)S(1)}, u32[]{:S(2)}, u32[]{:S(2)}) collective-permute-start(f32[4,128,128]{2,1,0:T(8,128)S(1)} %get-tuple-element.87.refs_12_), channel_id=1, source_target_pairs={{4,8},{8,4},{12,16},{16,12},{20,24},{24,20},{28,32},{32,28},{36,40... | collective-permute-start | bytes 786440 | tf_op jit(solution)/shard_map/ppermute | solution.py:291
  101.4 6.1 %collective-permute-start.15 = (f32[2,128,128]{2,1,0:T(8,128)S(1)}, f32[2,128,128]{2,1,0:T(8,128)S(1)}, u32[]{:S(2)}, u32[]{:S(2)}) collective-permute-start(f32[2,128,128]{2,1,0:T(8,128)S(1)} %get-tuple-element.92), channel_id=1, source_target_pairs={{0,1},{1,0},{2,3},{3,2},{4,7},{5,6},{6,5},{7,4},{8,9},{9,8},{10,11... | collective-permute-start | bytes 393224 | tf_op jit(solution)/shard_map/ppermute | solution.py:286
  102.5 5.4 %collective-permute-start.17 = (f32[2,128,128]{2,1,0:T(8,128)S(1)}, f32[2,128,128]{2,1,0:T(8,128)S(1)}, u32[]{:S(2)}, u32[]{:S(2)}) collective-permute-start(f32[2,128,128]{2,1,0:T(8,128)S(1)} %get-tuple-element.93), channel_id=1, source_target_pairs={{0,1},{1,0},{2,3},{3,2},{4,7},{5,6},{6,5},{7,4},{8,9},{9,8},{10,11... | collective-permute-start | bytes 393224 | tf_op jit(solution)/shard_map/ppermute | solution.py:286
  105.3 8.9 %collective-permute-start.14 = (f32[4,128,128]{2,1,0:T(8,128)S(1)}, f32[4,128,128]{2,1,0:T(8,128)S(1)}, u32[]{:S(2)}, u32[]{:S(2)}) collective-permute-start(f32[4,128,128]{2,1,0:T(8,128)S(1)} %direct.7.after), channel_id=1, source_target_pairs={{0,1},{1,0},{2,3},{3,2},{4,7},{5,6},{6,5},{7,4},{8,9},{9,8},{10,11... | collective-permute-start | bytes 786440 | tf_op jit(solution)/shard_map/ppermute | solution.py:286
  107.6 5.2 %collective-permute-start.16 = (f32[2,128,128]{2,1,0:T(8,128)S(1)}, f32[2,128,128]{2,1,0:T(8,128)S(1)}, u32[]{:S(2)}, u32[]{:S(2)}) collective-permute-start(f32[2,128,128]{2,1,0:T(8,128)S(1)} %relay.11), channel_id=1, source_target_pairs={{0,3},{1,2},{2,1},{3,0},{4,5},{5,4},{6,7},{7,6},{8,11},{9,10},{10,... | collective-permute-start | bytes 393224 | tf_op jit(solution)/shard_map/ppermute | solution.py:286
  107.9 6.3 %collective-permute-start.18 = (f32[2,128,128]{2,1,0:T(8,128)S(1)}, f32[2,128,128]{2,1,0:T(8,128)S(1)}, u32[]{:S(2)}, u32[]{:S(2)}) collective-permute-start(f32[2,128,128]{2,1,0:T(8,128)S(1)} %relay.12), channel_id=1, source_target_pairs={{0,3},{1,2},{2,1},{3,0},{4,5},{5,4},{6,7},{7,6},{8,11},{9,10},{10,... | collective-permute-start | bytes 393224 | tf_op jit(solution)/shard_map/ppermute | solution.py:286
  114.5 23.2 %collective-permute-start.20 = (f32[4,128,128]{2,1,0:T(8,128)S(1)}, f32[4,128,128]{2,1,0:T(8,128)S(1)}, u32[]{:S(2)}, u32[]{:S(2)}) collective-permute-start(f32[4,128,128]{2,1,0:T(8,128)S(1)} %get-tuple-element.102.refs_12_), channel_id=1, source_target_pairs={{0,4},{4,0},{8,12},{12,8},{16,20},{20,16},{24,28},{28,24},{32,36},... | collective-permute-start | bytes 786440 | tf_op jit(solution)/shard_map/ppermute | solution.py:292
  115.7 22.0 %collective-permute-start.19 = (f32[4,128,128]{2,1,0:T(8,128)S(1)}, f32[4,128,128]{2,1,0:T(8,128)S(1)}, u32[]{:S(2)}, u32[]{:S(2)}) collective-permute-start(f32[4,128,128]{2,1,0:T(8,128)S(1)} %get-tuple-element.102.refs_12_), channel_id=1, source_target_pairs={{4,8},{8,4},{12,16},{16,12},{20,24},{24,20},{28,32},{32,28},{36,40... | collective-permute-start | bytes 786440 | tf_op jit(solution)/shard_map/ppermute | solution.py:291
  140.3 6.4 %collective-permute-start.22 = (f32[2,128,128]{2,1,0:T(8,128)S(1)}, f32[2,128,128]{2,1,0:T(8,128)S(1)}, u32[]{:S(2)}, u32[]{:S(2)}) collective-permute-start(f32[2,128,128]{2,1,0:T(8,128)S(1)} %get-tuple-element.107), channel_id=1, source_target_pairs={{0,1},{1,0},{2,3},{3,2},{4,7},{5,6},{6,5},{7,4},{8,9},{9,8},{10,11... | collective-permute-start | bytes 393224 | tf_op jit(solution)/shard_map/ppermute | solution.py:286
  142.7 9.6 %collective-permute-start.21 = (f32[4,128,128]{2,1,0:T(8,128)S(1)}, f32[4,128,128]{2,1,0:T(8,128)S(1)}, u32[]{:S(2)}, u32[]{:S(2)}) collective-permute-start(f32[4,128,128]{2,1,0:T(8,128)S(1)} %direct.8.after), channel_id=1, source_target_pairs={{0,1},{1,0},{2,3},{3,2},{4,7},{5,6},{6,5},{7,4},{8,9},{9,8},{10,11... | collective-permute-start | bytes 786440 | tf_op jit(solution)/shard_map/ppermute | solution.py:286
  144.5 6.6 %collective-permute-start.24 = (f32[2,128,128]{2,1,0:T(8,128)S(1)}, f32[2,128,128]{2,1,0:T(8,128)S(1)}, u32[]{:S(2)}, u32[]{:S(2)}) collective-permute-start(f32[2,128,128]{2,1,0:T(8,128)S(1)} %get-tuple-element.108), channel_id=1, source_target_pairs={{0,1},{1,0},{2,3},{3,2},{4,7},{5,6},{6,5},{7,4},{8,9},{9,8},{10,11... | collective-permute-start | bytes 393224 | tf_op jit(solution)/shard_map/ppermute | solution.py:286
  146.7 5.7 %collective-permute-start.23 = (f32[2,128,128]{2,1,0:T(8,128)S(1)}, f32[2,128,128]{2,1,0:T(8,128)S(1)}, u32[]{:S(2)}, u32[]{:S(2)}) collective-permute-start(f32[2,128,128]{2,1,0:T(8,128)S(1)} %relay.13), channel_id=1, source_target_pairs={{0,3},{1,2},{2,1},{3,0},{4,5},{5,4},{6,7},{7,6},{8,11},{9,10},{10,... | collective-permute-start | bytes 393224 | tf_op jit(solution)/shard_map/ppermute | solution.py:286
  151.1 3.9 %collective-permute-start.25 = (f32[2,128,128]{2,1,0:T(8,128)S(1)}, f32[2,128,128]{2,1,0:T(8,128)S(1)}, u32[]{:S(2)}, u32[]{:S(2)}) collective-permute-start(f32[2,128,128]{2,1,0:T(8,128)S(1)} %relay.14), channel_id=1, source_target_pairs={{0,3},{1,2},{2,1},{3,0},{4,5},{5,4},{6,7},{7,6},{8,11},{9,10},{10,... | collective-permute-start | bytes 393224 | tf_op jit(solution)/shard_map/ppermute | solution.py:286
  155.3 24.4 %collective-permute-start.27 = (f32[4,128,128]{2,1,0:T(8,128)S(1)}, f32[4,128,128]{2,1,0:T(8,128)S(1)}, u32[]{:S(2)}, u32[]{:S(2)}) collective-permute-start(f32[4,128,128]{2,1,0:T(8,128)S(1)} %get-tuple-element.117.refs_12_), channel_id=1, source_target_pairs={{0,4},{4,0},{8,12},{12,8},{16,20},{20,16},{24,28},{28,24},{32,36},... | collective-permute-start | bytes 786440 | tf_op jit(solution)/shard_map/ppermute | solution.py:292
  157.9 21.8 %collective-permute-start.26 = (f32[4,128,128]{2,1,0:T(8,128)S(1)}, f32[4,128,128]{2,1,0:T(8,128)S(1)}, u32[]{:S(2)}, u32[]{:S(2)}) collective-permute-start(f32[4,128,128]{2,1,0:T(8,128)S(1)} %get-tuple-element.117.refs_12_), channel_id=1, source_target_pairs={{4,8},{8,4},{12,16},{16,12},{20,24},{24,20},{28,32},{32,28},{36,40... | collective-permute-start | bytes 786440 | tf_op jit(solution)/shard_map/ppermute | solution.py:291
  182.2 6.5 %collective-permute-start.29 = (f32[4,128,128]{2,1,0:T(8,128)S(1)}, f32[4,128,128]{2,1,0:T(8,128)S(1)}, u32[]{:S(2)}, u32[]{:S(2)}) collective-permute-start(f32[4,128,128]{2,1,0:T(8,128)S(1)} %get-tuple-element.122), channel_id=1, source_target_pairs={{0,1},{1,0},{2,3},{3,2},{4,7},{5,6},{6,5},{7,4},{8,9},{9,8},{10,11... | collective-permute-start | bytes 786440 | tf_op jit(solution)/shard_map/ppermute | solution.py:286
  185.6 6.5 %collective-permute-start.28 = (f32[4,128,128]{2,1,0:T(8,128)S(1)}, f32[4,128,128]{2,1,0:T(8,128)S(1)}, u32[]{:S(2)}, u32[]{:S(2)}) collective-permute-start(f32[4,128,128]{2,1,0:T(8,128)S(1)} %direct.9.after), channel_id=1, source_target_pairs={{0,1},{1,0},{2,3},{3,2},{4,7},{5,6},{6,5},{7,4},{8,9},{9,8},{10,11... | collective-permute-start | bytes 786440 | tf_op jit(solution)/shard_map/ppermute | solution.py:286
  188.7 5.8 %collective-permute-start.30 = (f32[4,128,128]{2,1,0:T(8,128)S(1)}, f32[4,128,128]{2,1,0:T(8,128)S(1)}, u32[]{:S(2)}, u32[]{:S(2)}) collective-permute-start(f32[4,128,128]{2,1,0:T(8,128)S(1)} %relay.15), channel_id=1, source_target_pairs={{0,3},{1,2},{2,1},{3,0},{4,5},{5,4},{6,7},{7,6},{8,11},{9,10},{10,... | collective-permute-start | bytes 786440 | tf_op jit(solution)/shard_map/ppermute | solution.py:286
  (4 other events, 3.3 us)

commit v3 on v0

--- a/solution.py
+++ b/solution.py
@@ -12,7 +12,8 @@
 LOCAL = 4
 GROUPS = 4
 B = 128
-PACK = LOCAL * B + 8
+PACK = LOCAL * B + 16
+THETA = 16
 
 f32 = jnp.float32
 bf16 = jnp.bfloat16
@@ -138,10 +139,10 @@
     return jnp.sum(jnp.where(at, row, 0.0), axis=1, keepdims=True)
 
 
-def put_lanes(values):
+def put_lanes(values, more=()):
     at = lax.broadcasted_iota(jnp.int32, (1, B), 1)
     row = jnp.zeros((1, B), f32)
-    for j, v in enumerate(values):
+    for j, v in [*enumerate(values), *enumerate(more, THETA)]:
         row = jnp.where(at == j, v, row)
     return row
 
@@ -177,38 +178,45 @@
     return (image - theta * state) / jnp.maximum(jnp.abs(diag - theta), 1.0)
 
 
-def start_kernel(count, stats, s0, s1, s2, pack0, pack1, pack2, diag0, right_diag,
-                 i0, i1, i2, diag1, diag2, c0, c1, c2, carry):
+def first_coefficients_kernel(count, stats, carry):
     rayleigh, length = totals(stats, count, 2)
-    theta = rayleigh / length
+    row = put_lanes([rayleigh, length], (rayleigh / length,))
+    carry[...] = jnp.broadcast_to(row, (8, B))
+
+
+def coefficients_kernel(count, step, stats, carry_in, carry):
+    sums = totals(stats, count, 5)
+    old = carry_in[0:1, :]
+    lowest, keep, add, rayleigh, length = ritz(sums, lane(old, 0), lane(old, 1))
+    energies = [lane(old, 2 + j) for j in range(step)] + [lowest]
+    row = put_lanes([rayleigh, length] + energies, (rayleigh / length, keep, add))
+    carry[...] = jnp.broadcast_to(row, (8, B))
+
+
+def start_kernel(carry, s0, s1, s2, pack0, pack1, pack2, diag0, right_diag,
+                 i0, i1, i2, diag1, diag2, c0, c1, c2):
+    theta = lane(carry[0:1, :], THETA)
     for pack, diag in ((pack1, diag1), (pack2, diag2)):
         for p in range(LOCAL):
-            diag[p] = outer(pack[LOCAL * B:PACK, :], right_diag[p])
+            diag[p] = outer(pack[LOCAL * B:PACK - 8, :], right_diag[p])
     for s, pack, i, diag, c in ((s0, pack0, i0, diag0, c0), (s1, pack1, i1, diag1, c1), (s2, pack2, i2, diag2, c2)):
         for p in range(LOCAL):
             block = pack[p * B:(p + 1) * B, :]
             i[p] = block
             c[p] = correct(s[p], block, diag[p], theta)
-    carry[...] = jnp.broadcast_to(put_lanes([rayleigh, length]), (8, B))
-
-
-def next_kernel(count, step, keeps, stats, carry_in, *refs):
-    sums = totals(stats, count, 5)
-    old = carry_in[0:1, :]
-    lowest, keep, add, rayleigh, length = ritz(sums, lane(old, 0), lane(old, 1))
-    theta = rayleigh / length
+
+
+def next_kernel(keeps, carry, *refs):
+    theta, keep, add = [lane(carry[0:1, :], THETA + j) for j in range(3)]
     for n in range(3):
         state, image, corr, diag, more = refs[n:15:3]
         for p in range(LOCAL):
             s = keep * state[p] + add * corr[p]
-            i = keep * image[p] + add * more[p]
+            i = keep * image[p] + add * more[p * B:(p + 1) * B, :]
             refs[15 + n][p] = correct(s, i, diag[p], theta)
             if n < keeps:
                 refs[18 + n][p] = s
                 refs[18 + keeps + n][p] = i
-    energies = [lane(old, 2 + j) for j in range(step)] + [lowest]
-    refs[-1][...] = jnp.broadcast_to(put_lanes([rayleigh, length] + energies), (8, B))
-
 
 def last_kernel(count, stats, carry_in, state, corr, state_out, energies):
     sums = totals(stats, count, 5)
@@ -224,7 +232,7 @@
     return jnp.sum(jnp.sum(block, axis=0, keepdims=True), axis=1, keepdims=True)
 
 
-def first_stats_kernel(own, direct, relayed, state, left_diag, pack, stats):
+def first_stats_kernel(own, direct, relayed, state, left_diag, pack):
     a, b = jnp.zeros((B, B), f32), jnp.zeros((B, B), f32)
     for p in range(LOCAL):
         i = own[p] + (direct[p] + relayed[p])
@@ -232,20 +240,31 @@
         pack[p * B:(p + 1) * B, :] = i
         a = a + s * i
         b = b + s * s
-    pack[LOCAL * B:PACK, :] = left_diag[...]
-    stats[...] = jnp.broadcast_to(put_lanes([sum_all(a), sum_all(b)]), stats.shape)
-
-
-def stats_kernel(own, direct, relayed, state, corr, image, *outs):
+    pack[LOCAL * B:PACK - 8, :] = left_diag[...]
+    pack[PACK - 8:PACK, :] = jnp.broadcast_to(put_lanes([sum_all(a), sum_all(b)]), (8, B))
+
+
+def stats_kernel(own, direct, relayed, state, corr, image, out):
+    last = out.shape[0] <= LOCAL * B
     acc = [jnp.zeros((B, B), f32) for _ in range(5)]
     for p in range(LOCAL):
         ic = own[p] + (direct[p] + relayed[p])
         s, c, i = state[p], corr[p], image[p]
-        if len(outs) > 1:
-            outs[0][p] = ic
+        if not last:
+            out[p * B:(p + 1) * B, :] = ic
         for j, v in enumerate((s * ic, c * i, c * ic, s * c, c * c)):
             acc[j] = acc[j] + v
-    outs[-1][...] = jnp.broadcast_to(put_lanes([sum_all(a) for a in acc]), outs[-1].shape)
+    row = put_lanes([sum_all(a) for a in acc])
+    if last:
+        out[...] = jnp.broadcast_to(row, out.shape)
+    else:
+        out[LOCAL * B:, :] = jnp.broadcast_to(row, (8, B))
+
+
+def cores_kernel(mine, theirs, stats):
+    at = mine.shape[0] - 8
+    row = mine[at:at + 1, :] + theirs[at:at + 1, :]
+    stats[...] = jnp.broadcast_to(row, stats.shape)
 
 
 def arr(*shape, dtype=f32):
@@ -276,16 +295,25 @@
     return lax.ppermute(x, ("sec", "pair"), perm)
 
 
-def neighbours(x):
+def from_chip(x):
     n = lax.axis_size("sec")
-    by_chip = lax.ppermute(x, "sec", [(i, i + 1 if i % 2 else i - 1) for i in range(1, n - 1)])
-    by_core = lax.ppermute(x, "sec", [(i, i ^ 1) for i in range(n)])
-    return by_chip, by_core
-
-
-def exchange(stats, devices):
-    got = lax.all_to_all(stats.reshape(devices, 1, B), ("sec", "pair"), 0, 0)
-    return got.reshape(devices, B)
+    return lax.ppermute(x, "sec", [(i, i + 1 if i % 2 else i - 1) for i in range(1, n - 1)])
+
+
+def from_core(x):
+    return lax.ppermute(x, "sec", [(i, i ^ 1) for i in range(lax.axis_size("sec"))])
+
+
+def exchange(stats):
+    return lax.all_to_all(stats.reshape(-1, 1, B), ("sec", "pair"), 0, 0).reshape(stats.shape)
+
+
+def exchange_cores(mine, theirs):
+    n = lax.axis_size("sec")
+    groups = [[s * GROUPS + g for s in range(core, n, 2) for g in range(GROUPS)] for core in range(2)]
+    (stats,) = call(cores_kernel, "cores", [VM] * 2, [arr(n // 2 * GROUPS, B)])(mine, theirs)
+    got = lax.all_to_all(stats.reshape(-1, 1, B), ("sec", "pair"), 0, 0, axis_index_groups=groups)
+    return got.reshape(stats.shape)
 
 
 def on_device(psi_start, left_env, right_env, mpo_coef, mpo_pattern, sector_shift, block_rows):
@@ -296,7 +324,6 @@
     group = lax.axis_index("pair").astype(jnp.int32).reshape(1)
     sector = lax.axis_index("sec").astype(jnp.int32).reshape(1)
     weights = (mpo_coef * mpo_pattern.astype(f32)).reshape(-1)
-    stats_shape = arr(devices, B)
     carry_shape = arr(8, B)
 
     def shares(vectors, left2, right2):
@@ -313,33 +340,37 @@
         return own, direct, swap(relayed, 3, 1)
 
     (state,) = call(mask_kernel, "mask", [SM, VM], [BLOCK])(block_rows, psi)
-    states = (state, *neighbours(state))
+    states = (state, from_chip(state), from_core(state))
     left2, right2, diag, left_diag, right_diag = call(
         split_kernel, "split", [SM] * 4 + [VM] * 2,
         [arr(TERMS, B, 2 * B, dtype=bf16), arr(TERMS, LOCAL, B, 2 * B, dtype=bf16), BLOCK, arr(8, B), arr(LOCAL, 8, B)],
     )(group, sector_shift, block_rows, weights, left, right_env)
 
     parts = shares(states, left2, right2)
-    pack, stats = call(first_stats_kernel, "first_stats", [VM] * 5, [arr(PACK, B), stats_shape])(
-        *parts, state, left_diag)
-    packs = (pack, *neighbours(pack))
-    *out, carry = call(
-        lambda *refs: start_kernel(count, *refs), "start", [VM] * 9, [BLOCK] * 8 + [carry_shape]
-    )(exchange(stats, devices), *states, *packs, diag, right_diag)
+    (pack,) = call(first_stats_kernel, "first_stats", [VM] * 5, [arr(PACK, B)])(*parts, state, left_diag)
+    core = from_core(pack)
+    got = exchange_cores(pack, core)
+    packs = (pack, from_chip(pack), core)
+    (carry,) = call(functools.partial(first_coefficients_kernel, count), "coefficients", [VM], [carry_shape])(got)
+    out = call(start_kernel, "start", [VM] * 9, [BLOCK] * 8)(carry, *states, *packs, diag, right_diag)
     images, diags, corrs = out[:3], (diag, *out[3:5]), out[5:8]
 
     for step in range(ITERS):
         parts = shares(corrs, left2, right2)
-        outs = [BLOCK, stats_shape] if step < ITERS - 1 else [stats_shape]
-        *image_corr, stats = call(stats_kernel, "stats", [VM] * 6, outs)(*parts, states[0], corrs[0], images[0])
-        got = exchange(stats, devices)
-        if step < ITERS - 1:
-            more = (*image_corr, *neighbours(*image_corr))
+        rows = LOCAL * B + 8 if step < ITERS - 1 else devices
+        (out,) = call(stats_kernel, "stats", [VM] * 6, [arr(rows, B)])(*parts, states[0], corrs[0], images[0])
+        if step == ITERS - 1:
+            got = exchange(out)
+        else:
+            core = from_core(out)
+            got = exchange_cores(out, core)
+            more = (out, from_chip(out), core)
             keeps = 3 if step < ITERS - 2 else 1
-            *out, carry = call(
-                functools.partial(next_kernel, count, step, keeps), "next", [VM] * 17,
-                [BLOCK] * (3 + 2 * keeps) + [carry_shape],
-            )(got, carry, *states, *images, *corrs, *diags, *more)
+            (carry,) = call(
+                functools.partial(coefficients_kernel, count, step), "coefficients", [VM] * 2, [carry_shape]
+            )(got, carry)
+            out = call(functools.partial(next_kernel, keeps), "next", [VM] * 16, [BLOCK] * (3 + 2 * keeps))(
+                carry, *states, *images, *corrs, *diags, *more)
             corrs, states, images = out[:3], out[3:3 + keeps], out[3 + keeps:]
 
     state, energies = call(

time: 214 us -> 213 us (level)
  blocking collectives: 104 us -> 100 us
  waiting for transfers between devices: 30.2 us -> 33.1 us
    all_to_all x5, blocking collectives: 104 us -> 100 us  [the longest x4 80.4 us: exchange_cores(): lax.all_to_all(stats.reshape(-1, 1, B), ('sec', 'pair'), 0, 0, axis_index...]
    ppermute x15, waiting for transfers between devices: 29.7 us -> 32.6 us  [swap(): return lax.ppermute(x, ('sec', 'pair'), perm)]
where the time goes in v3:
time: 213 us; the launch traced here: 212 us
  blocking collectives  100 us (47%)
  starting transfers between devices  39 us (18%)
  Pallas kernels  33.1 us (16%)
  waiting for transfers between devices  33.1 us (16%)
  local copies, waits for them, and re-layouts  4.25 us (2%)
    all_to_all x4, blocking collectives, exchange_cores(): lax.all_to_all(stats.reshape(-1, 1, B), ('sec', 'pair'), 0, 0, axis_index...  80.4 us
    ppermute x15, waiting for transfers between devices, swap(): return lax.ppermute(x, ('sec', 'pair'), perm)  32.6 us
    all_to_all x1, blocking collectives, exchange(): lax.all_to_all(stats.reshape(-1, 1, B), ('sec', 'pair'), 0, 0)  19.9 us
    ppermute x15, starting transfers between devices, swap(): return lax.ppermute(x, ('sec', 'pair'), perm)  15.1 us
    ppermute x5, starting transfers between devices, from_core(): lax.ppermute(x, 'sec', [(i, i ^ 1) for i in range(lax.axis_size('sec'))])  12.3 us
    ppermute x5, starting transfers between devices, from_chip(): lax.ppermute(x, 'sec', [(i, i + 1 if i % 2 else i - 1) for i in range(1,...  11.6 us
    pallas_call x5, Pallas kernels, shares(): call(terms_kernel, 'terms', [SM] * 4 + [VM] * 5, [TERM_BLOCKS, BLOCK], [p...  9.44 us
    pallas_call x5, Pallas kernels, shares(): call(relayed_kernel, 'relayed', [SM] * 3 + [VM, ANY], [BLOCK])  5.87 us
  transfers between devices with their start and end apart: 25, of which 15 were waited for; matrix products, arithmetic and copies ran while one was open for 0% of the time, Pallas kernels for 9%

profile of v3, /device:TPU:1, one launch (start us, length us, event | category | flops | bytes accessed | tf_op | source)
XLA Modules:
  0.0 212.3 jit_solution(9967851217533659357)
XLA Ops:
  2.3 3.3 %collective-permute-start.1 = (f32[4,128,128]{2,1,0:T(8,128)S(1)}, f32[4,128,128]{2,1,0:T(8,128)S(1)}, u32[]{:S(2)}, u32[]{:S(2)}) collective-permute-start(f32[4,128,128]{2,1,0:T(8,128)S(1)} %mask.1.own.state.s0.refs_0_), channel_id=1, source_target_pairs={{0,4},{4,0},{8,12},{12,8},{16,20},{20,16},{24,28},{28,24},{32,36},... | collective-permute-start | bytes 786440 | tf_op jit(solution)/shard_map/ppermute | solution.py:304
  5.6 1.9 collective-permute-start
  13.3 1.9 terms.5
  15.2 1.7 collective-permute-start.3
  23.0 4.6 %collective-permute-done.2.direct = f32[4,128,128]{2,1,0:T(8,128)S(1)} collective-permute-done((f32[4,128,128]{2,1,0:T(8,128)S(1)}, f32[4,128,128]{2,1,0:T(8,128)S(1)}, u32[]{:S(2)}, u32[]{:S(2)}) %collective-permute-start.2) | collective-permute-done | bytes 262176 | tf_op jit(solution)/shard_map/ppermute | solution.py:295
  27.7 1.7 collective-permute-start.5
  29.4 3.3 %collective-permute-start.6 = (f32[528,128]{1,0:T(8,128)S(1)}, f32[528,128]{1,0:T(8,128)S(1)}, u32[]{:S(2)}, u32[]{:S(2)}) collective-permute-start(f32[528,128]{1,0:T(8,128)S(1)} %first_stats.1.mine.pack0), channel_id=1, source_target_pairs={{4,8},{8,4},{12,16},{16,12},{20,24},{24,20},{28,32},{32,28},{36,40... | collective-permute-start | bytes 811016 | tf_op jit(solution)/shard_map/ppermute | solution.py:300
  32.7 26.5 %all_to_all.25 = f32[128,1,128]{2,1,0:T(1,128)S(1)} all-to-all(f32[128,1,128]{2,1,0:T(1,128)S(1)} %bitcast.29), channel_id=1, replica_groups={{0,1,2,3,8,9,10,11,16,17,18,19,24,25,26,27,32,33,34,35,40,41,42,43,48,4..., dimensions={0} | all-to-all | bytes 131072 | tf_op jit(solution)/shard_map/all_to_all | solution.py:315
  60.1 1.9 terms.6
  65.0 2.1 %collective-permute-start.7 = (f32[4,128,128]{2,1,0:T(8,128)S(1)}, f32[4,128,128]{2,1,0:T(8,128)S(1)}, u32[]{:S(2)}, u32[]{:S(2)}) collective-permute-start(f32[4,128,128]{2,1,0:T(8,128)S(1)} %direct.6.after), channel_id=1, source_target_pairs={{0,1},{1,0},{2,3},{3,2},{4,7},{5,6},{6,5},{7,4},{8,9},{9,8},{10,11... | collective-permute-start | bytes 786440 | tf_op jit(solution)/shard_map/ppermute | solution.py:295
  71.5 3.0 %collective-permute-done.9.relayed = f32[4,128,128]{2,1,0:T(8,128)S(1)} collective-permute-done((f32[4,128,128]{2,1,0:T(8,128)S(1)}, f32[4,128,128]{2,1,0:T(8,128)S(1)}, u32[]{:S(2)}, u32[]{:S(2)}) %collective-permute-start.9) | collective-permute-done | bytes 262176 | tf_op jit(solution)/shard_map/ppermute | solution.py:295
  74.8 2.5 %collective-permute-start.10 = (f32[520,128]{1,0:T(8,128)S(1)}, f32[520,128]{1,0:T(8,128)S(1)}, u32[]{:S(2)}, u32[]{:S(2)}) collective-permute-start(f32[520,128]{1,0:T(8,128)S(1)} %stats.4.mine.refs_12_), channel_id=1, source_target_pairs={{0,4},{4,0},{8,12},{12,8},{16,20},{20,16},{24,28},{28,24},{32,36},... | collective-permute-start | bytes 798728 | tf_op jit(solution)/shard_map/ppermute | solution.py:304
  77.3 2.1 collective-permute-start.11
  79.4 18.0 %all_to_all.26 = f32[128,1,128]{2,1,0:T(1,128)S(1)} all-to-all(f32[128,1,128]{2,1,0:T(1,128)S(1)} %bitcast.30), channel_id=1, replica_groups={{0,1,2,3,8,9,10,11,16,17,18,19,24,25,26,27,32,33,34,35,40,41,42,43,48,4..., dimensions={0} | all-to-all | bytes 131072 | tf_op jit(solution)/shard_map/all_to_all | solution.py:315
  98.2 1.9 terms.7
  103.1 2.2 %collective-permute-start.12 = (f32[4,128,128]{2,1,0:T(8,128)S(1)}, f32[4,128,128]{2,1,0:T(8,128)S(1)}, u32[]{:S(2)}, u32[]{:S(2)}) collective-permute-start(f32[4,128,128]{2,1,0:T(8,128)S(1)} %direct.7.after), channel_id=1, source_target_pairs={{0,1},{1,0},{2,3},{3,2},{4,7},{5,6},{6,5},{7,4},{8,9},{9,8},{10,11... | collective-permute-start | bytes 786440 | tf_op jit(solution)/shard_map/ppermute | solution.py:295
  109.6 3.8 %collective-permute-done.14.relayed = f32[4,128,128]{2,1,0:T(8,128)S(1)} collective-permute-done((f32[4,128,128]{2,1,0:T(8,128)S(1)}, f32[4,128,128]{2,1,0:T(8,128)S(1)}, u32[]{:S(2)}, u32[]{:S(2)}) %collective-permute-start.14) | collective-permute-done | bytes 262176 | tf_op jit(solution)/shard_map/ppermute | solution.py:295
  113.7 2.4 %collective-permute-start.15 = (f32[520,128]{1,0:T(8,128)S(1)}, f32[520,128]{1,0:T(8,128)S(1)}, u32[]{:S(2)}, u32[]{:S(2)}) collective-permute-start(f32[520,128]{1,0:T(8,128)S(1)} %stats.5.mine.refs_12_), channel_id=1, source_target_pairs={{0,4},{4,0},{8,12},{12,8},{16,20},{20,16},{24,28},{28,24},{32,36},... | collective-permute-start | bytes 798728 | tf_op jit(solution)/shard_map/ppermute | solution.py:304
  116.0 2.1 collective-permute-start.16
  118.2 18.0 %all_to_all.27 = f32[128,1,128]{2,1,0:T(1,128)S(1)} all-to-all(f32[128,1,128]{2,1,0:T(1,128)S(1)} %bitcast.31), channel_id=1, replica_groups={{0,1,2,3,8,9,10,11,16,17,18,19,24,25,26,27,32,33,34,35,40,41,42,43,48,4..., dimensions={0} | all-to-all | bytes 131072 | tf_op jit(solution)/shard_map/all_to_all | solution.py:315
  136.8 1.9 terms.8
  141.9 2.1 %collective-permute-start.17 = (f32[4,128,128]{2,1,0:T(8,128)S(1)}, f32[4,128,128]{2,1,0:T(8,128)S(1)}, u32[]{:S(2)}, u32[]{:S(2)}) collective-permute-start(f32[4,128,128]{2,1,0:T(8,128)S(1)} %direct.8.after), channel_id=1, source_target_pairs={{0,1},{1,0},{2,3},{3,2},{4,7},{5,6},{6,5},{7,4},{8,9},{9,8},{10,11... | collective-permute-start | bytes 786440 | tf_op jit(solution)/shard_map/ppermute | solution.py:295
  146.8 1.7 collective-permute-done.17.direct
  148.5 3.9 %collective-permute-done.19.relayed = f32[4,128,128]{2,1,0:T(8,128)S(1)} collective-permute-done((f32[4,128,128]{2,1,0:T(8,128)S(1)}, f32[4,128,128]{2,1,0:T(8,128)S(1)}, u32[]{:S(2)}, u32[]{:S(2)}) %collective-permute-start.19) | collective-permute-done | bytes 262176 | tf_op jit(solution)/shard_map/ppermute | solution.py:295
  152.6 2.4 %collective-permute-start.20 = (f32[520,128]{1,0:T(8,128)S(1)}, f32[520,128]{1,0:T(8,128)S(1)}, u32[]{:S(2)}, u32[]{:S(2)}) collective-permute-start(f32[520,128]{1,0:T(8,128)S(1)} %stats.6.mine.refs_12_), channel_id=1, source_target_pairs={{0,4},{4,0},{8,12},{12,8},{16,20},{20,16},{24,28},{28,24},{32,36},... | collective-permute-start | bytes 798728 | tf_op jit(solution)/shard_map/ppermute | solution.py:304
  155.0 2.1 collective-permute-start.21
  157.1 18.0 %all_to_all.28 = f32[128,1,128]{2,1,0:T(1,128)S(1)} all-to-all(f32[128,1,128]{2,1,0:T(1,128)S(1)} %bitcast.32), channel_id=1, replica_groups={{0,1,2,3,8,9,10,11,16,17,18,19,24,25,26,27,32,33,34,35,40,41,42,43,48,4..., dimensions={0} | all-to-all | bytes 131072 | tf_op jit(solution)/shard_map/all_to_all | solution.py:315
  175.7 1.9 terms.9
  180.6 2.1 %collective-permute-start.22 = (f32[4,128,128]{2,1,0:T(8,128)S(1)}, f32[4,128,128]{2,1,0:T(8,128)S(1)}, u32[]{:S(2)}, u32[]{:S(2)}) collective-permute-start(f32[4,128,128]{2,1,0:T(8,128)S(1)} %direct.9.after), channel_id=1, source_target_pairs={{0,1},{1,0},{2,3},{3,2},{4,7},{5,6},{6,5},{7,4},{8,9},{9,8},{10,11... | collective-permute-start | bytes 786440 | tf_op jit(solution)/shard_map/ppermute | solution.py:295
  185.4 1.7 collective-permute-done.22.direct
  187.1 3.9 %collective-permute-done.24.relayed = f32[4,128,128]{2,1,0:T(8,128)S(1)} collective-permute-done((f32[4,128,128]{2,1,0:T(8,128)S(1)}, f32[4,128,128]{2,1,0:T(8,128)S(1)}, u32[]{:S(2)}, u32[]{:S(2)}) %collective-permute-start.24) | collective-permute-done | bytes 262176 | tf_op jit(solution)/shard_map/ppermute | solution.py:295
  191.3 19.9 %all_to_all.29 = f32[256,1,128]{2,1,0:T(1,128)S(1)} all-to-all(f32[256,1,128]{2,1,0:T(1,128)S(1)} %bitcast.26), channel_id=1, replica_groups=mesh['sec'=64,'pair'=4] {'sec','pair'}, dimensions={0} | all-to-all | bytes 262144 | tf_op jit(solution)/shard_map/all_to_all | solution.py:308
  (80 shorter events, 44.0 us)
Async XLA Ops:
  1.3 1.0 copy-start.2
  2.3 10.5 %collective-permute-start.1 = (f32[4,128,128]{2,1,0:T(8,128)S(1)}, f32[4,128,128]{2,1,0:T(8,128)S(1)}, u32[]{:S(2)}, u32[]{:S(2)}) collective-permute-start(f32[4,128,128]{2,1,0:T(8,128)S(1)} %mask.1.own.state.s0.refs_0_), channel_id=1, source_target_pairs={{0,4},{4,0},{8,12},{12,8},{16,20},{20,16},{24,28},{28,24},{32,36},... | collective-permute-start | bytes 786440 | tf_op jit(solution)/shard_map/ppermute | solution.py:304
  5.6 7.7 %collective-permute-start = (f32[4,128,128]{2,1,0:T(8,128)S(1)}, f32[4,128,128]{2,1,0:T(8,128)S(1)}, u32[]{:S(2)}, u32[]{:S(2)}) collective-permute-start(f32[4,128,128]{2,1,0:T(8,128)S(1)} %mask.1.own.state.s0.refs_0_), channel_id=1, source_target_pairs={{4,8},{8,4},{12,16},{16,12},{20,24},{24,20},{28,32},{32,28},{36,40... | collective-permute-start | bytes 786440 | tf_op jit(solution)/shard_map/ppermute | solution.py:300
  8.4 1.4 copy-start
  9.8 1.0 copy-start.1
  10.8 0.7 copy-start.3
  15.2 6.5 %collective-permute-start.3 = (f32[4,128,128]{2,1,0:T(8,128)S(1)}, f32[4,128,128]{2,1,0:T(8,128)S(1)}, u32[]{:S(2)}, u32[]{:S(2)}) collective-permute-start(f32[4,128,128]{2,1,0:T(8,128)S(1)} %get-tuple-element.53), channel_id=1, source_target_pairs={{0,1},{1,0},{2,3},{3,2},{4,7},{5,6},{6,5},{7,4},{8,9},{9,8},{10,11... | collective-permute-start | bytes 786440 | tf_op jit(solution)/shard_map/ppermute | solution.py:295
  19.2 8.3 %collective-permute-start.2 = (f32[4,128,128]{2,1,0:T(8,128)S(1)}, f32[4,128,128]{2,1,0:T(8,128)S(1)}, u32[]{:S(2)}, u32[]{:S(2)}) collective-permute-start(f32[4,128,128]{2,1,0:T(8,128)S(1)} %direct.5.after), channel_id=1, source_target_pairs={{0,1},{1,0},{2,3},{3,2},{4,7},{5,6},{6,5},{7,4},{8,9},{9,8},{10,11... | collective-permute-start | bytes 786440 | tf_op jit(solution)/shard_map/ppermute | solution.py:295
  21.7 5.8 %collective-permute-start.4 = (f32[4,128,128]{2,1,0:T(8,128)S(1)}, f32[4,128,128]{2,1,0:T(8,128)S(1)}, u32[]{:S(2)}, u32[]{:S(2)}) collective-permute-start(f32[4,128,128]{2,1,0:T(8,128)S(1)} %relay.5), channel_id=1, source_target_pairs={{0,3},{1,2},{2,1},{3,0},{4,5},{5,4},{6,7},{7,6},{8,11},{9,10},{10,... | collective-permute-start | bytes 786440 | tf_op jit(solution)/shard_map/ppermute | solution.py:295
  27.7 5.0 %collective-permute-start.5 = (f32[528,128]{1,0:T(8,128)S(1)}, f32[528,128]{1,0:T(8,128)S(1)}, u32[]{:S(2)}, u32[]{:S(2)}) collective-permute-start(f32[528,128]{1,0:T(8,128)S(1)} %first_stats.1.mine.pack0), channel_id=1, source_target_pairs={{0,4},{4,0},{8,12},{12,8},{16,20},{20,16},{24,28},{28,24},{32,36},... | collective-permute-start | bytes 811016 | tf_op jit(solution)/shard_map/ppermute | solution.py:304
  29.4 29.9 %collective-permute-start.6 = (f32[528,128]{1,0:T(8,128)S(1)}, f32[528,128]{1,0:T(8,128)S(1)}, u32[]{:S(2)}, u32[]{:S(2)}) collective-permute-start(f32[528,128]{1,0:T(8,128)S(1)} %first_stats.1.mine.pack0), channel_id=1, source_target_pairs={{4,8},{8,4},{12,16},{16,12},{20,24},{24,20},{28,32},{32,28},{36,40... | collective-permute-start | bytes 811016 | tf_op jit(solution)/shard_map/ppermute | solution.py:300
  62.0 6.5 %collective-permute-start.8 = (f32[4,128,128]{2,1,0:T(8,128)S(1)}, f32[4,128,128]{2,1,0:T(8,128)S(1)}, u32[]{:S(2)}, u32[]{:S(2)}) collective-permute-start(f32[4,128,128]{2,1,0:T(8,128)S(1)} %get-tuple-element.61), channel_id=1, source_target_pairs={{0,1},{1,0},{2,3},{3,2},{4,7},{5,6},{6,5},{7,4},{8,9},{9,8},{10,11... | collective-permute-start | bytes 786440 | tf_op jit(solution)/shard_map/ppermute | solution.py:295
  65.0 6.5 %collective-permute-start.7 = (f32[4,128,128]{2,1,0:T(8,128)S(1)}, f32[4,128,128]{2,1,0:T(8,128)S(1)}, u32[]{:S(2)}, u32[]{:S(2)}) collective-permute-start(f32[4,128,128]{2,1,0:T(8,128)S(1)} %direct.6.after), channel_id=1, source_target_pairs={{0,1},{1,0},{2,3},{3,2},{4,7},{5,6},{6,5},{7,4},{8,9},{9,8},{10,11... | collective-permute-start | bytes 786440 | tf_op jit(solution)/shard_map/ppermute | solution.py:295
  68.5 6.0 %collective-permute-start.9 = (f32[4,128,128]{2,1,0:T(8,128)S(1)}, f32[4,128,128]{2,1,0:T(8,128)S(1)}, u32[]{:S(2)}, u32[]{:S(2)}) collective-permute-start(f32[4,128,128]{2,1,0:T(8,128)S(1)} %relay.6), channel_id=1, source_target_pairs={{0,3},{1,2},{2,1},{3,0},{4,5},{5,4},{6,7},{7,6},{8,11},{9,10},{10,... | collective-permute-start | bytes 786440 | tf_op jit(solution)/shard_map/ppermute | solution.py:295
  74.8 4.7 %collective-permute-start.10 = (f32[520,128]{1,0:T(8,128)S(1)}, f32[520,128]{1,0:T(8,128)S(1)}, u32[]{:S(2)}, u32[]{:S(2)}) collective-permute-start(f32[520,128]{1,0:T(8,128)S(1)} %stats.4.mine.refs_12_), channel_id=1, source_target_pairs={{0,4},{4,0},{8,12},{12,8},{16,20},{20,16},{24,28},{28,24},{32,36},... | collective-permute-start | bytes 798728 | tf_op jit(solution)/shard_map/ppermute | solution.py:304
  77.3 20.3 %collective-permute-start.11 = (f32[520,128]{1,0:T(8,128)S(1)}, f32[520,128]{1,0:T(8,128)S(1)}, u32[]{:S(2)}, u32[]{:S(2)}) collective-permute-start(f32[520,128]{1,0:T(8,128)S(1)} %stats.4.mine.refs_12_), channel_id=1, source_target_pairs={{4,8},{8,4},{12,16},{16,12},{20,24},{24,20},{28,32},{32,28},{36,40... | collective-permute-start | bytes 798728 | tf_op jit(solution)/shard_map/ppermute | solution.py:300
  97.6 0.7 copy-start.4
  100.1 6.5 %collective-permute-start.13 = (f32[4,128,128]{2,1,0:T(8,128)S(1)}, f32[4,128,128]{2,1,0:T(8,128)S(1)}, u32[]{:S(2)}, u32[]{:S(2)}) collective-permute-start(f32[4,128,128]{2,1,0:T(8,128)S(1)} %get-tuple-element.71), channel_id=1, source_target_pairs={{0,1},{1,0},{2,3},{3,2},{4,7},{5,6},{6,5},{7,4},{8,9},{9,8},{10,11... | collective-permute-start | bytes 786440 | tf_op jit(solution)/shard_map/ppermute | solution.py:295
  103.1 6.5 %collective-permute-start.12 = (f32[4,128,128]{2,1,0:T(8,128)S(1)}, f32[4,128,128]{2,1,0:T(8,128)S(1)}, u32[]{:S(2)}, u32[]{:S(2)}) collective-permute-start(f32[4,128,128]{2,1,0:T(8,128)S(1)} %direct.7.after), channel_id=1, source_target_pairs={{0,1},{1,0},{2,3},{3,2},{4,7},{5,6},{6,5},{7,4},{8,9},{9,8},{10,11... | collective-permute-start | bytes 786440 | tf_op jit(solution)/shard_map/ppermute | solution.py:295
  106.7 6.8 %collective-permute-start.14 = (f32[4,128,128]{2,1,0:T(8,128)S(1)}, f32[4,128,128]{2,1,0:T(8,128)S(1)}, u32[]{:S(2)}, u32[]{:S(2)}) collective-permute-start(f32[4,128,128]{2,1,0:T(8,128)S(1)} %relay.7), channel_id=1, source_target_pairs={{0,3},{1,2},{2,1},{3,0},{4,5},{5,4},{6,7},{7,6},{8,11},{9,10},{10,... | collective-permute-start | bytes 786440 | tf_op jit(solution)/shard_map/ppermute | solution.py:295
  113.7 4.5 %collective-permute-start.15 = (f32[520,128]{1,0:T(8,128)S(1)}, f32[520,128]{1,0:T(8,128)S(1)}, u32[]{:S(2)}, u32[]{:S(2)}) collective-permute-start(f32[520,128]{1,0:T(8,128)S(1)} %stats.5.mine.refs_12_), channel_id=1, source_target_pairs={{0,4},{4,0},{8,12},{12,8},{16,20},{20,16},{24,28},{28,24},{32,36},... | collective-permute-start | bytes 798728 | tf_op jit(solution)/shard_map/ppermute | solution.py:304
  116.0 20.3 %collective-permute-start.16 = (f32[520,128]{1,0:T(8,128)S(1)}, f32[520,128]{1,0:T(8,128)S(1)}, u32[]{:S(2)}, u32[]{:S(2)}) collective-permute-start(f32[520,128]{1,0:T(8,128)S(1)} %stats.5.mine.refs_12_), channel_id=1, source_target_pairs={{4,8},{8,4},{12,16},{16,12},{20,24},{24,20},{28,32},{32,28},{36,40... | collective-permute-start | bytes 798728 | tf_op jit(solution)/shard_map/ppermute | solution.py:300
  138.7 6.7 %collective-permute-start.18 = (f32[4,128,128]{2,1,0:T(8,128)S(1)}, f32[4,128,128]{2,1,0:T(8,128)S(1)}, u32[]{:S(2)}, u32[]{:S(2)}) collective-permute-start(f32[4,128,128]{2,1,0:T(8,128)S(1)} %get-tuple-element.82), channel_id=1, source_target_pairs={{0,1},{1,0},{2,3},{3,2},{4,7},{5,6},{6,5},{7,4},{8,9},{9,8},{10,11... | collective-permute-start | bytes 786440 | tf_op jit(solution)/shard_map/ppermute | solution.py:295
  141.9 6.5 %collective-permute-start.17 = (f32[4,128,128]{2,1,0:T(8,128)S(1)}, f32[4,128,128]{2,1,0:T(8,128)S(1)}, u32[]{:S(2)}, u32[]{:S(2)}) collective-permute-start(f32[4,128,128]{2,1,0:T(8,128)S(1)} %direct.8.after), channel_id=1, source_target_pairs={{0,1},{1,0},{2,3},{3,2},{4,7},{5,6},{6,5},{7,4},{8,9},{9,8},{10,11... | collective-permute-start | bytes 786440 | tf_op jit(solution)/shard_map/ppermute | solution.py:295
  145.5 6.9 %collective-permute-start.19 = (f32[4,128,128]{2,1,0:T(8,128)S(1)}, f32[4,128,128]{2,1,0:T(8,128)S(1)}, u32[]{:S(2)}, u32[]{:S(2)}) collective-permute-start(f32[4,128,128]{2,1,0:T(8,128)S(1)} %relay.8), channel_id=1, source_target_pairs={{0,3},{1,2},{2,1},{3,0},{4,5},{5,4},{6,7},{7,6},{8,11},{9,10},{10,... | collective-permute-start | bytes 786440 | tf_op jit(solution)/shard_map/ppermute | solution.py:295
  152.6 4.5 %collective-permute-start.20 = (f32[520,128]{1,0:T(8,128)S(1)}, f32[520,128]{1,0:T(8,128)S(1)}, u32[]{:S(2)}, u32[]{:S(2)}) collective-permute-start(f32[520,128]{1,0:T(8,128)S(1)} %stats.6.mine.refs_12_), channel_id=1, source_target_pairs={{0,4},{4,0},{8,12},{12,8},{16,20},{20,16},{24,28},{28,24},{32,36},... | collective-permute-start | bytes 798728 | tf_op jit(solution)/shard_map/ppermute | solution.py:304
  155.0 20.3 %collective-permute-start.21 = (f32[520,128]{1,0:T(8,128)S(1)}, f32[520,128]{1,0:T(8,128)S(1)}, u32[]{:S(2)}, u32[]{:S(2)}) collective-permute-start(f32[520,128]{1,0:T(8,128)S(1)} %stats.6.mine.refs_12_), channel_id=1, source_target_pairs={{4,8},{8,4},{12,16},{16,12},{20,24},{24,20},{28,32},{32,28},{36,40... | collective-permute-start | bytes 798728 | tf_op jit(solution)/shard_map/ppermute | solution.py:300
  177.6 6.5 %collective-permute-start.23 = (f32[4,128,128]{2,1,0:T(8,128)S(1)}, f32[4,128,128]{2,1,0:T(8,128)S(1)}, u32[]{:S(2)}, u32[]{:S(2)}) collective-permute-start(f32[4,128,128]{2,1,0:T(8,128)S(1)} %get-tuple-element.93), channel_id=1, source_target_pairs={{0,1},{1,0},{2,3},{3,2},{4,7},{5,6},{6,5},{7,4},{8,9},{9,8},{10,11... | collective-permute-start | bytes 786440 | tf_op jit(solution)/shard_map/ppermute | solution.py:295
  180.6 6.5 %collective-permute-start.22 = (f32[4,128,128]{2,1,0:T(8,128)S(1)}, f32[4,128,128]{2,1,0:T(8,128)S(1)}, u32[]{:S(2)}, u32[]{:S(2)}) collective-permute-start(f32[4,128,128]{2,1,0:T(8,128)S(1)} %direct.9.after), channel_id=1, source_target_pairs={{0,1},{1,0},{2,3},{3,2},{4,7},{5,6},{6,5},{7,4},{8,9},{9,8},{10,11... | collective-permute-start | bytes 786440 | tf_op jit(solution)/shard_map/ppermute | solution.py:295
  184.2 6.9 %collective-permute-start.24 = (f32[4,128,128]{2,1,0:T(8,128)S(1)}, f32[4,128,128]{2,1,0:T(8,128)S(1)}, u32[]{:S(2)}, u32[]{:S(2)}) collective-permute-start(f32[4,128,128]{2,1,0:T(8,128)S(1)} %relay.9), channel_id=1, source_target_pairs={{0,3},{1,2},{2,1},{3,0},{4,5},{5,4},{6,7},{7,6},{8,11},{9,10},{10,... | collective-permute-start | bytes 786440 | tf_op jit(solution)/shard_map/ppermute | solution.py:295

commit v4 on v3

--- a/solution.py
+++ b/solution.py
@@ -14,6 +14,7 @@
 B = 128
 PACK = LOCAL * B + 16
 THETA = 16
+SHIFTS = TERMS * 16 * 16
 
 f32 = jnp.float32
 bf16 = jnp.bfloat16
@@ -48,7 +49,7 @@
         precision=lax.Precision.HIGHEST, preferred_element_type=f32)
 
 
-def split_kernel(group, shift, rows, weights, left, right, left2, right2, diag, left_diag, right_diag):
+def split_kernel(group, rows, weights, left, right, left2, right2, diag, left_diag, right_diag):
     keep = row_mask(rows)
     eye = eye_mask()
     pad = jnp.zeros((8 - TERMS, B), f32)
@@ -56,7 +57,7 @@
     for k in range(TERMS):
         block = left[k] * keep
         left2[k] = jnp.concatenate(halves(block), axis=1)
-        chosen = jnp.where(shift[k] == 0, 1.0, 0.0).astype(f32)
+        chosen = jnp.where(weights[SHIFTS + k] == 0.0, 1.0, 0.0).astype(f32)
         lines.append(jnp.sum(jnp.where(eye, block, 0.0), axis=0, keepdims=True) * chosen)
     left_diag[...] = jnp.concatenate(lines + [pad], axis=0)
     lines = [[] for _ in range(LOCAL)]
@@ -98,14 +99,14 @@
             part(2 * half, 2, slice(None))
 
 
-def terms_kernel(group, sector, shift, weights, own, by_chip, by_core, left2, right2, z, far, vec2):
+def terms_kernel(group, sector, weights, own, by_chip, by_core, left2, right2, z, far, vec2):
     odd = lax.rem(sector[0], 2)
     for p in range(LOCAL):
         vec2[1, p] = jnp.concatenate(halves(own[p]), axis=1)
         vec2[2 - 2 * odd, p] = jnp.concatenate(halves(by_core[p]), axis=1)
         vec2[2 * odd, p] = jnp.concatenate(halves(by_chip[p]), axis=1)
     for k in range(TERMS):
-        source = shift[k] + 1
+        source = weights[SHIFTS + k].astype(jnp.int32) + 1
         lhs = left2[k]
         for q in range(LOCAL):
             r = right2[k, q]
@@ -324,13 +325,14 @@
     group = lax.axis_index("pair").astype(jnp.int32).reshape(1)
     sector = lax.axis_index("sec").astype(jnp.int32).reshape(1)
     weights = (mpo_coef * mpo_pattern.astype(f32)).reshape(-1)
+    weights = jnp.concatenate([weights, sector_shift.astype(f32)])
     carry_shape = arr(8, B)
 
     def shares(vectors, left2, right2):
         z, far = call(
-            terms_kernel, "terms", [SM] * 4 + [VM] * 5, [TERM_BLOCKS, BLOCK],
+            terms_kernel, "terms", [SM] * 3 + [VM] * 5, [TERM_BLOCKS, BLOCK],
             [pltpu.VMEM((3, LOCAL, B, 2 * B), bf16)],
-        )(group, sector, sector_shift, weights, *vectors, left2, right2)
+        )(group, sector, weights, *vectors, left2, right2)
         far = swap(far, 1, 3)
         (direct,) = call(direct_kernel, "direct", [SM] * 3 + [VM], [BLOCK])(group, sector, weights, z)
         (relayed,) = call(relayed_kernel, "relayed", [SM] * 3 + [VM, ANY], [BLOCK])(group, sector, weights, z, direct)
@@ -342,9 +344,9 @@
     (state,) = call(mask_kernel, "mask", [SM, VM], [BLOCK])(block_rows, psi)
     states = (state, from_chip(state), from_core(state))
     left2, right2, diag, left_diag, right_diag = call(
-        split_kernel, "split", [SM] * 4 + [VM] * 2,
+        split_kernel, "split", [SM] * 3 + [VM] * 2,
         [arr(TERMS, B, 2 * B, dtype=bf16), arr(TERMS, LOCAL, B, 2 * B, dtype=bf16), BLOCK, arr(8, B), arr(LOCAL, 8, B)],
-    )(group, sector_shift, block_rows, weights, left, right_env)
+    )(group, block_rows, weights, left, right_env)
 
     parts = shares(states, left2, right2)
     (pack,) = call(first_stats_kernel, "first_stats", [VM] * 5, [arr(PACK, B)])(*parts, state, left_diag)

time: 213 us -> 213 us (level)
  transfers between devices with their start and end apart: 25 -> 25, of which waited for: 15 -> 15; matrix products, arithmetic and copies ran while one was open for 0% -> 1% of each run, Pallas kernels for 9% -> 9%
where the time goes in v4:
time: 213 us; the launch traced here: 212 us
  blocking collectives  100 us (47%)
  starting transfers between devices  38.9 us (18%)
  Pallas kernels  33.1 us (16%)
  waiting for transfers between devices  33.1 us (16%)
  local copies, waits for them, and re-layouts  3.42 us (2%)
    all_to_all x4, blocking collectives, exchange_cores(): lax.all_to_all(stats.reshape(-1, 1, B), ('sec', 'pair'), 0, 0, axis_index...  80.4 us
    ppermute x15, waiting for transfers between devices, swap(): return lax.ppermute(x, ('sec', 'pair'), perm)  32.6 us
    all_to_all x1, blocking collectives, exchange(): lax.all_to_all(stats.reshape(-1, 1, B), ('sec', 'pair'), 0, 0)  19.9 us
    ppermute x15, starting transfers between devices, swap(): return lax.ppermute(x, ('sec', 'pair'), perm)  15.1 us
    ppermute x5, starting transfers between devices, from_core(): lax.ppermute(x, 'sec', [(i, i ^ 1) for i in range(lax.axis_size('sec'))])  12.3 us
    ppermute x5, starting transfers between devices, from_chip(): lax.ppermute(x, 'sec', [(i, i + 1 if i % 2 else i - 1) for i in range(1,...  11.5 us
    pallas_call x5, Pallas kernels, shares(): call(terms_kernel, 'terms', [SM] * 3 + [VM] * 5, [TERM_BLOCKS, BLOCK], [p...  9.46 us
    pallas_call x5, Pallas kernels, shares(): call(relayed_kernel, 'relayed', [SM] * 3 + [VM, ANY], [BLOCK])  5.9 us
  transfers between devices with their start and end apart: 25, of which 15 were waited for; matrix products, arithmetic and copies ran while one was open for 1% of the time, Pallas kernels for 9%

profile of v4, /device:TPU:1, one launch (start us, length us, event | category | flops | bytes accessed | tf_op | source)
XLA Modules:
  0.0 212.2 jit_solution(8358566279257262102)
XLA Ops:
  2.3 3.3 %collective-permute-start.1 = (f32[4,128,128]{2,1,0:T(8,128)S(1)}, f32[4,128,128]{2,1,0:T(8,128)S(1)}, u32[]{:S(2)}, u32[]{:S(2)}) collective-permute-start(f32[4,128,128]{2,1,0:T(8,128)S(1)} %mask.1.own.state.s0.refs_0_), channel_id=1, source_target_pairs={{0,4},{4,0},{8,12},{12,8},{16,20},{20,16},{24,28},{28,24},{32,36},... | collective-permute-start | bytes 786440 | tf_op jit(solution)/shard_map/ppermute | solution.py:305
  5.6 1.9 collective-permute-start
  13.3 1.9 terms.5
  15.2 1.7 collective-permute-start.3
  23.0 4.6 %collective-permute-done.2.direct = f32[4,128,128]{2,1,0:T(8,128)S(1)} collective-permute-done((f32[4,128,128]{2,1,0:T(8,128)S(1)}, f32[4,128,128]{2,1,0:T(8,128)S(1)}, u32[]{:S(2)}, u32[]{:S(2)}) %collective-permute-start.2) | collective-permute-done | bytes 262176 | tf_op jit(solution)/shard_map/ppermute | solution.py:296
  29.4 3.3 %collective-permute-start.6 = (f32[528,128]{1,0:T(8,128)S(1)}, f32[528,128]{1,0:T(8,128)S(1)}, u32[]{:S(2)}, u32[]{:S(2)}) collective-permute-start(f32[528,128]{1,0:T(8,128)S(1)} %first_stats.1.mine.pack0), channel_id=1, source_target_pairs={{4,8},{8,4},{12,16},{16,12},{20,24},{24,20},{28,32},{32,28},{36,40... | collective-permute-start | bytes 811016 | tf_op jit(solution)/shard_map/ppermute | solution.py:301
  32.7 26.5 %all_to_all.25 = f32[128,1,128]{2,1,0:T(1,128)S(1)} all-to-all(f32[128,1,128]{2,1,0:T(1,128)S(1)} %bitcast.29), channel_id=1, replica_groups={{0,1,2,3,8,9,10,11,16,17,18,19,24,25,26,27,32,33,34,35,40,41,42,43,48,4..., dimensions={0} | all-to-all | bytes 131072 | tf_op jit(solution)/shard_map/all_to_all | solution.py:316
  60.1 1.9 terms.6
  65.0 2.1 %collective-permute-start.7 = (f32[4,128,128]{2,1,0:T(8,128)S(1)}, f32[4,128,128]{2,1,0:T(8,128)S(1)}, u32[]{:S(2)}, u32[]{:S(2)}) collective-permute-start(f32[4,128,128]{2,1,0:T(8,128)S(1)} %direct.6.after), channel_id=1, source_target_pairs={{0,1},{1,0},{2,3},{3,2},{4,7},{5,6},{6,5},{7,4},{8,9},{9,8},{10,11... | collective-permute-start | bytes 786440 | tf_op jit(solution)/shard_map/ppermute | solution.py:296
  71.5 3.0 %collective-permute-done.9.relayed = f32[4,128,128]{2,1,0:T(8,128)S(1)} collective-permute-done((f32[4,128,128]{2,1,0:T(8,128)S(1)}, f32[4,128,128]{2,1,0:T(8,128)S(1)}, u32[]{:S(2)}, u32[]{:S(2)}) %collective-permute-start.9) | collective-permute-done | bytes 262176 | tf_op jit(solution)/shard_map/ppermute | solution.py:296
  74.8 2.5 %collective-permute-start.10 = (f32[520,128]{1,0:T(8,128)S(1)}, f32[520,128]{1,0:T(8,128)S(1)}, u32[]{:S(2)}, u32[]{:S(2)}) collective-permute-start(f32[520,128]{1,0:T(8,128)S(1)} %stats.4.mine.refs_12_), channel_id=1, source_target_pairs={{0,4},{4,0},{8,12},{12,8},{16,20},{20,16},{24,28},{28,24},{32,36},... | collective-permute-start | bytes 798728 | tf_op jit(solution)/shard_map/ppermute | solution.py:305
  77.3 2.1 collective-permute-start.11
  79.4 18.0 %all_to_all.26 = f32[128,1,128]{2,1,0:T(1,128)S(1)} all-to-all(f32[128,1,128]{2,1,0:T(1,128)S(1)} %bitcast.30), channel_id=1, replica_groups={{0,1,2,3,8,9,10,11,16,17,18,19,24,25,26,27,32,33,34,35,40,41,42,43,48,4..., dimensions={0} | all-to-all | bytes 131072 | tf_op jit(solution)/shard_map/all_to_all | solution.py:316
  98.0 1.9 terms.7
  102.9 2.2 %collective-permute-start.12 = (f32[4,128,128]{2,1,0:T(8,128)S(1)}, f32[4,128,128]{2,1,0:T(8,128)S(1)}, u32[]{:S(2)}, u32[]{:S(2)}) collective-permute-start(f32[4,128,128]{2,1,0:T(8,128)S(1)} %direct.7.after), channel_id=1, source_target_pairs={{0,1},{1,0},{2,3},{3,2},{4,7},{5,6},{6,5},{7,4},{8,9},{9,8},{10,11... | collective-permute-start | bytes 786440 | tf_op jit(solution)/shard_map/ppermute | solution.py:296
  107.8 1.7 collective-permute-done.12.direct
  109.5 3.8 %collective-permute-done.14.relayed = f32[4,128,128]{2,1,0:T(8,128)S(1)} collective-permute-done((f32[4,128,128]{2,1,0:T(8,128)S(1)}, f32[4,128,128]{2,1,0:T(8,128)S(1)}, u32[]{:S(2)}, u32[]{:S(2)}) %collective-permute-start.14) | collective-permute-done | bytes 262176 | tf_op jit(solution)/shard_map/ppermute | solution.py:296
  113.5 2.4 %collective-permute-start.15 = (f32[520,128]{1,0:T(8,128)S(1)}, f32[520,128]{1,0:T(8,128)S(1)}, u32[]{:S(2)}, u32[]{:S(2)}) collective-permute-start(f32[520,128]{1,0:T(8,128)S(1)} %stats.5.mine.refs_12_), channel_id=1, source_target_pairs={{0,4},{4,0},{8,12},{12,8},{16,20},{20,16},{24,28},{28,24},{32,36},... | collective-permute-start | bytes 798728 | tf_op jit(solution)/shard_map/ppermute | solution.py:305
  115.9 2.1 collective-permute-start.16
  118.0 18.0 %all_to_all.27 = f32[128,1,128]{2,1,0:T(1,128)S(1)} all-to-all(f32[128,1,128]{2,1,0:T(1,128)S(1)} %bitcast.31), channel_id=1, replica_groups={{0,1,2,3,8,9,10,11,16,17,18,19,24,25,26,27,32,33,34,35,40,41,42,43,48,4..., dimensions={0} | all-to-all | bytes 131072 | tf_op jit(solution)/shard_map/all_to_all | solution.py:316
  136.7 1.9 terms.8
  141.8 2.1 %collective-permute-start.17 = (f32[4,128,128]{2,1,0:T(8,128)S(1)}, f32[4,128,128]{2,1,0:T(8,128)S(1)}, u32[]{:S(2)}, u32[]{:S(2)}) collective-permute-start(f32[4,128,128]{2,1,0:T(8,128)S(1)} %direct.8.after), channel_id=1, source_target_pairs={{0,1},{1,0},{2,3},{3,2},{4,7},{5,6},{6,5},{7,4},{8,9},{9,8},{10,11... | collective-permute-start | bytes 786440 | tf_op jit(solution)/shard_map/ppermute | solution.py:296
  146.6 1.7 collective-permute-done.17.direct
  148.3 3.9 %collective-permute-done.19.relayed = f32[4,128,128]{2,1,0:T(8,128)S(1)} collective-permute-done((f32[4,128,128]{2,1,0:T(8,128)S(1)}, f32[4,128,128]{2,1,0:T(8,128)S(1)}, u32[]{:S(2)}, u32[]{:S(2)}) %collective-permute-start.19) | collective-permute-done | bytes 262176 | tf_op jit(solution)/shard_map/ppermute | solution.py:296
  152.5 2.4 %collective-permute-start.20 = (f32[520,128]{1,0:T(8,128)S(1)}, f32[520,128]{1,0:T(8,128)S(1)}, u32[]{:S(2)}, u32[]{:S(2)}) collective-permute-start(f32[520,128]{1,0:T(8,128)S(1)} %stats.6.mine.refs_12_), channel_id=1, source_target_pairs={{0,4},{4,0},{8,12},{12,8},{16,20},{20,16},{24,28},{28,24},{32,36},... | collective-permute-start | bytes 798728 | tf_op jit(solution)/shard_map/ppermute | solution.py:305
  154.8 2.1 collective-permute-start.21
  157.0 18.0 %all_to_all.28 = f32[128,1,128]{2,1,0:T(1,128)S(1)} all-to-all(f32[128,1,128]{2,1,0:T(1,128)S(1)} %bitcast.32), channel_id=1, replica_groups={{0,1,2,3,8,9,10,11,16,17,18,19,24,25,26,27,32,33,34,35,40,41,42,43,48,4..., dimensions={0} | all-to-all | bytes 131072 | tf_op jit(solution)/shard_map/all_to_all | solution.py:316
  175.6 1.9 terms.9
  180.5 2.1 %collective-permute-start.22 = (f32[4,128,128]{2,1,0:T(8,128)S(1)}, f32[4,128,128]{2,1,0:T(8,128)S(1)}, u32[]{:S(2)}, u32[]{:S(2)}) collective-permute-start(f32[4,128,128]{2,1,0:T(8,128)S(1)} %direct.9.after), channel_id=1, source_target_pairs={{0,1},{1,0},{2,3},{3,2},{4,7},{5,6},{6,5},{7,4},{8,9},{9,8},{10,11... | collective-permute-start | bytes 786440 | tf_op jit(solution)/shard_map/ppermute | solution.py:296
  185.3 1.7 collective-permute-done.22.direct
  187.0 3.9 %collective-permute-done.24.relayed = f32[4,128,128]{2,1,0:T(8,128)S(1)} collective-permute-done((f32[4,128,128]{2,1,0:T(8,128)S(1)}, f32[4,128,128]{2,1,0:T(8,128)S(1)}, u32[]{:S(2)}, u32[]{:S(2)}) %collective-permute-start.24) | collective-permute-done | bytes 262176 | tf_op jit(solution)/shard_map/ppermute | solution.py:296
  191.1 19.9 %all_to_all.29 = f32[256,1,128]{2,1,0:T(1,128)S(1)} all-to-all(f32[256,1,128]{2,1,0:T(1,128)S(1)} %bitcast.26), channel_id=1, replica_groups=mesh['sec'=64,'pair'=4] {'sec','pair'}, dimensions={0} | all-to-all | bytes 262144 | tf_op jit(solution)/shard_map/all_to_all | solution.py:309
  (78 shorter events, 43.9 us)
Async XLA Ops:
  1.3 1.0 copy-start.2
  2.3 10.5 %collective-permute-start.1 = (f32[4,128,128]{2,1,0:T(8,128)S(1)}, f32[4,128,128]{2,1,0:T(8,128)S(1)}, u32[]{:S(2)}, u32[]{:S(2)}) collective-permute-start(f32[4,128,128]{2,1,0:T(8,128)S(1)} %mask.1.own.state.s0.refs_0_), channel_id=1, source_target_pairs={{0,4},{4,0},{8,12},{12,8},{16,20},{20,16},{24,28},{28,24},{32,36},... | collective-permute-start | bytes 786440 | tf_op jit(solution)/shard_map/ppermute | solution.py:305
  5.6 7.7 %collective-permute-start = (f32[4,128,128]{2,1,0:T(8,128)S(1)}, f32[4,128,128]{2,1,0:T(8,128)S(1)}, u32[]{:S(2)}, u32[]{:S(2)}) collective-permute-start(f32[4,128,128]{2,1,0:T(8,128)S(1)} %mask.1.own.state.s0.refs_0_), channel_id=1, source_target_pairs={{4,8},{8,4},{12,16},{16,12},{20,24},{24,20},{28,32},{32,28},{36,40... | collective-permute-start | bytes 786440 | tf_op jit(solution)/shard_map/ppermute | solution.py:301
  9.1 1.4 copy-start
  10.5 1.0 copy-start.1
  15.2 6.5 %collective-permute-start.3 = (f32[4,128,128]{2,1,0:T(8,128)S(1)}, f32[4,128,128]{2,1,0:T(8,128)S(1)}, u32[]{:S(2)}, u32[]{:S(2)}) collective-permute-start(f32[4,128,128]{2,1,0:T(8,128)S(1)} %get-tuple-element.53), channel_id=1, source_target_pairs={{0,1},{1,0},{2,3},{3,2},{4,7},{5,6},{6,5},{7,4},{8,9},{9,8},{10,11... | collective-permute-start | bytes 786440 | tf_op jit(solution)/shard_map/ppermute | solution.py:296
  19.2 8.3 %collective-permute-start.2 = (f32[4,128,128]{2,1,0:T(8,128)S(1)}, f32[4,128,128]{2,1,0:T(8,128)S(1)}, u32[]{:S(2)}, u32[]{:S(2)}) collective-permute-start(f32[4,128,128]{2,1,0:T(8,128)S(1)} %direct.5.after), channel_id=1, source_target_pairs={{0,1},{1,0},{2,3},{3,2},{4,7},{5,6},{6,5},{7,4},{8,9},{9,8},{10,11... | collective-permute-start | bytes 786440 | tf_op jit(solution)/shard_map/ppermute | solution.py:296
  21.7 5.8 %collective-permute-start.4 = (f32[4,128,128]{2,1,0:T(8,128)S(1)}, f32[4,128,128]{2,1,0:T(8,128)S(1)}, u32[]{:S(2)}, u32[]{:S(2)}) collective-permute-start(f32[4,128,128]{2,1,0:T(8,128)S(1)} %relay.5), channel_id=1, source_target_pairs={{0,3},{1,2},{2,1},{3,0},{4,5},{5,4},{6,7},{7,6},{8,11},{9,10},{10,... | collective-permute-start | bytes 786440 | tf_op jit(solution)/shard_map/ppermute | solution.py:296
  27.7 5.0 %collective-permute-start.5 = (f32[528,128]{1,0:T(8,128)S(1)}, f32[528,128]{1,0:T(8,128)S(1)}, u32[]{:S(2)}, u32[]{:S(2)}) collective-permute-start(f32[528,128]{1,0:T(8,128)S(1)} %first_stats.1.mine.pack0), channel_id=1, source_target_pairs={{0,4},{4,0},{8,12},{12,8},{16,20},{20,16},{24,28},{28,24},{32,36},... | collective-permute-start | bytes 811016 | tf_op jit(solution)/shard_map/ppermute | solution.py:305
  29.4 29.9 %collective-permute-start.6 = (f32[528,128]{1,0:T(8,128)S(1)}, f32[528,128]{1,0:T(8,128)S(1)}, u32[]{:S(2)}, u32[]{:S(2)}) collective-permute-start(f32[528,128]{1,0:T(8,128)S(1)} %first_stats.1.mine.pack0), channel_id=1, source_target_pairs={{4,8},{8,4},{12,16},{16,12},{20,24},{24,20},{28,32},{32,28},{36,40... | collective-permute-start | bytes 811016 | tf_op jit(solution)/shard_map/ppermute | solution.py:301
  62.0 6.5 %collective-permute-start.8 = (f32[4,128,128]{2,1,0:T(8,128)S(1)}, f32[4,128,128]{2,1,0:T(8,128)S(1)}, u32[]{:S(2)}, u32[]{:S(2)}) collective-permute-start(f32[4,128,128]{2,1,0:T(8,128)S(1)} %get-tuple-element.61), channel_id=1, source_target_pairs={{0,1},{1,0},{2,3},{3,2},{4,7},{5,6},{6,5},{7,4},{8,9},{9,8},{10,11... | collective-permute-start | bytes 786440 | tf_op jit(solution)/shard_map/ppermute | solution.py:296
  65.0 6.5 %collective-permute-start.7 = (f32[4,128,128]{2,1,0:T(8,128)S(1)}, f32[4,128,128]{2,1,0:T(8,128)S(1)}, u32[]{:S(2)}, u32[]{:S(2)}) collective-permute-start(f32[4,128,128]{2,1,0:T(8,128)S(1)} %direct.6.after), channel_id=1, source_target_pairs={{0,1},{1,0},{2,3},{3,2},{4,7},{5,6},{6,5},{7,4},{8,9},{9,8},{10,11... | collective-permute-start | bytes 786440 | tf_op jit(solution)/shard_map/ppermute | solution.py:296
  68.5 6.0 %collective-permute-start.9 = (f32[4,128,128]{2,1,0:T(8,128)S(1)}, f32[4,128,128]{2,1,0:T(8,128)S(1)}, u32[]{:S(2)}, u32[]{:S(2)}) collective-permute-start(f32[4,128,128]{2,1,0:T(8,128)S(1)} %relay.6), channel_id=1, source_target_pairs={{0,3},{1,2},{2,1},{3,0},{4,5},{5,4},{6,7},{7,6},{8,11},{9,10},{10,... | collective-permute-start | bytes 786440 | tf_op jit(solution)/shard_map/ppermute | solution.py:296
  74.8 4.6 %collective-permute-start.10 = (f32[520,128]{1,0:T(8,128)S(1)}, f32[520,128]{1,0:T(8,128)S(1)}, u32[]{:S(2)}, u32[]{:S(2)}) collective-permute-start(f32[520,128]{1,0:T(8,128)S(1)} %stats.4.mine.refs_12_), channel_id=1, source_target_pairs={{0,4},{4,0},{8,12},{12,8},{16,20},{20,16},{24,28},{28,24},{32,36},... | collective-permute-start | bytes 798728 | tf_op jit(solution)/shard_map/ppermute | solution.py:305
  77.3 20.3 %collective-permute-start.11 = (f32[520,128]{1,0:T(8,128)S(1)}, f32[520,128]{1,0:T(8,128)S(1)}, u32[]{:S(2)}, u32[]{:S(2)}) collective-permute-start(f32[520,128]{1,0:T(8,128)S(1)} %stats.4.mine.refs_12_), channel_id=1, source_target_pairs={{4,8},{8,4},{12,16},{16,12},{20,24},{24,20},{28,32},{32,28},{36,40... | collective-permute-start | bytes 798728 | tf_op jit(solution)/shard_map/ppermute | solution.py:301
  99.9 6.5 %collective-permute-start.13 = (f32[4,128,128]{2,1,0:T(8,128)S(1)}, f32[4,128,128]{2,1,0:T(8,128)S(1)}, u32[]{:S(2)}, u32[]{:S(2)}) collective-permute-start(f32[4,128,128]{2,1,0:T(8,128)S(1)} %get-tuple-element.71), channel_id=1, source_target_pairs={{0,1},{1,0},{2,3},{3,2},{4,7},{5,6},{6,5},{7,4},{8,9},{9,8},{10,11... | collective-permute-start | bytes 786440 | tf_op jit(solution)/shard_map/ppermute | solution.py:296
  102.9 6.5 %collective-permute-start.12 = (f32[4,128,128]{2,1,0:T(8,128)S(1)}, f32[4,128,128]{2,1,0:T(8,128)S(1)}, u32[]{:S(2)}, u32[]{:S(2)}) collective-permute-start(f32[4,128,128]{2,1,0:T(8,128)S(1)} %direct.7.after), channel_id=1, source_target_pairs={{0,1},{1,0},{2,3},{3,2},{4,7},{5,6},{6,5},{7,4},{8,9},{9,8},{10,11... | collective-permute-start | bytes 786440 | tf_op jit(solution)/shard_map/ppermute | solution.py:296
  106.5 6.8 %collective-permute-start.14 = (f32[4,128,128]{2,1,0:T(8,128)S(1)}, f32[4,128,128]{2,1,0:T(8,128)S(1)}, u32[]{:S(2)}, u32[]{:S(2)}) collective-permute-start(f32[4,128,128]{2,1,0:T(8,128)S(1)} %relay.7), channel_id=1, source_target_pairs={{0,3},{1,2},{2,1},{3,0},{4,5},{5,4},{6,7},{7,6},{8,11},{9,10},{10,... | collective-permute-start | bytes 786440 | tf_op jit(solution)/shard_map/ppermute | solution.py:296
  113.5 4.5 %collective-permute-start.15 = (f32[520,128]{1,0:T(8,128)S(1)}, f32[520,128]{1,0:T(8,128)S(1)}, u32[]{:S(2)}, u32[]{:S(2)}) collective-permute-start(f32[520,128]{1,0:T(8,128)S(1)} %stats.5.mine.refs_12_), channel_id=1, source_target_pairs={{0,4},{4,0},{8,12},{12,8},{16,20},{20,16},{24,28},{28,24},{32,36},... | collective-permute-start | bytes 798728 | tf_op jit(solution)/shard_map/ppermute | solution.py:305
  115.9 20.3 %collective-permute-start.16 = (f32[520,128]{1,0:T(8,128)S(1)}, f32[520,128]{1,0:T(8,128)S(1)}, u32[]{:S(2)}, u32[]{:S(2)}) collective-permute-start(f32[520,128]{1,0:T(8,128)S(1)} %stats.5.mine.refs_12_), channel_id=1, source_target_pairs={{4,8},{8,4},{12,16},{16,12},{20,24},{24,20},{28,32},{32,28},{36,40... | collective-permute-start | bytes 798728 | tf_op jit(solution)/shard_map/ppermute | solution.py:301
  138.6 6.7 %collective-permute-start.18 = (f32[4,128,128]{2,1,0:T(8,128)S(1)}, f32[4,128,128]{2,1,0:T(8,128)S(1)}, u32[]{:S(2)}, u32[]{:S(2)}) collective-permute-start(f32[4,128,128]{2,1,0:T(8,128)S(1)} %get-tuple-element.82), channel_id=1, source_target_pairs={{0,1},{1,0},{2,3},{3,2},{4,7},{5,6},{6,5},{7,4},{8,9},{9,8},{10,11... | collective-permute-start | bytes 786440 | tf_op jit(solution)/shard_map/ppermute | solution.py:296
  141.8 6.5 %collective-permute-start.17 = (f32[4,128,128]{2,1,0:T(8,128)S(1)}, f32[4,128,128]{2,1,0:T(8,128)S(1)}, u32[]{:S(2)}, u32[]{:S(2)}) collective-permute-start(f32[4,128,128]{2,1,0:T(8,128)S(1)} %direct.8.after), channel_id=1, source_target_pairs={{0,1},{1,0},{2,3},{3,2},{4,7},{5,6},{6,5},{7,4},{8,9},{9,8},{10,11... | collective-permute-start | bytes 786440 | tf_op jit(solution)/shard_map/ppermute | solution.py:296
  145.3 6.9 %collective-permute-start.19 = (f32[4,128,128]{2,1,0:T(8,128)S(1)}, f32[4,128,128]{2,1,0:T(8,128)S(1)}, u32[]{:S(2)}, u32[]{:S(2)}) collective-permute-start(f32[4,128,128]{2,1,0:T(8,128)S(1)} %relay.8), channel_id=1, source_target_pairs={{0,3},{1,2},{2,1},{3,0},{4,5},{5,4},{6,7},{7,6},{8,11},{9,10},{10,... | collective-permute-start | bytes 786440 | tf_op jit(solution)/shard_map/ppermute | solution.py:296
  152.5 4.5 %collective-permute-start.20 = (f32[520,128]{1,0:T(8,128)S(1)}, f32[520,128]{1,0:T(8,128)S(1)}, u32[]{:S(2)}, u32[]{:S(2)}) collective-permute-start(f32[520,128]{1,0:T(8,128)S(1)} %stats.6.mine.refs_12_), channel_id=1, source_target_pairs={{0,4},{4,0},{8,12},{12,8},{16,20},{20,16},{24,28},{28,24},{32,36},... | collective-permute-start | bytes 798728 | tf_op jit(solution)/shard_map/ppermute | solution.py:305
  154.8 20.3 %collective-permute-start.21 = (f32[520,128]{1,0:T(8,128)S(1)}, f32[520,128]{1,0:T(8,128)S(1)}, u32[]{:S(2)}, u32[]{:S(2)}) collective-permute-start(f32[520,128]{1,0:T(8,128)S(1)} %stats.6.mine.refs_12_), channel_id=1, source_target_pairs={{4,8},{8,4},{12,16},{16,12},{20,24},{24,20},{28,32},{32,28},{36,40... | collective-permute-start | bytes 798728 | tf_op jit(solution)/shard_map/ppermute | solution.py:301
  177.5 6.5 %collective-permute-start.23 = (f32[4,128,128]{2,1,0:T(8,128)S(1)}, f32[4,128,128]{2,1,0:T(8,128)S(1)}, u32[]{:S(2)}, u32[]{:S(2)}) collective-permute-start(f32[4,128,128]{2,1,0:T(8,128)S(1)} %get-tuple-element.93), channel_id=1, source_target_pairs={{0,1},{1,0},{2,3},{3,2},{4,7},{5,6},{6,5},{7,4},{8,9},{9,8},{10,11... | collective-permute-start | bytes 786440 | tf_op jit(solution)/shard_map/ppermute | solution.py:296
  180.5 6.5 %collective-permute-start.22 = (f32[4,128,128]{2,1,0:T(8,128)S(1)}, f32[4,128,128]{2,1,0:T(8,128)S(1)}, u32[]{:S(2)}, u32[]{:S(2)}) collective-permute-start(f32[4,128,128]{2,1,0:T(8,128)S(1)} %direct.9.after), channel_id=1, source_target_pairs={{0,1},{1,0},{2,3},{3,2},{4,7},{5,6},{6,5},{7,4},{8,9},{9,8},{10,11... | collective-permute-start | bytes 786440 | tf_op jit(solution)/shard_map/ppermute | solution.py:296
  184.0 6.9 %collective-permute-start.24 = (f32[4,128,128]{2,1,0:T(8,128)S(1)}, f32[4,128,128]{2,1,0:T(8,128)S(1)}, u32[]{:S(2)}, u32[]{:S(2)}) collective-permute-start(f32[4,128,128]{2,1,0:T(8,128)S(1)} %relay.9), channel_id=1, source_target_pairs={{0,3},{1,2},{2,1},{3,0},{4,5},{5,4},{6,7},{7,6},{8,11},{9,10},{10,... | collective-permute-start | bytes 786440 | tf_op jit(solution)/shard_map/ppermute | solution.py:296

commit v5 on v4

--- a/solution.py
+++ b/solution.py
@@ -305,10 +305,6 @@
     return lax.ppermute(x, "sec", [(i, i ^ 1) for i in range(lax.axis_size("sec"))])
 
 
-def exchange(stats):
-    return lax.all_to_all(stats.reshape(-1, 1, B), ("sec", "pair"), 0, 0).reshape(stats.shape)
-
-
 def exchange_cores(mine, theirs):
     n = lax.axis_size("sec")
     groups = [[s * GROUPS + g for s in range(core, n, 2) for g in range(GROUPS)] for core in range(2)]
@@ -359,13 +355,11 @@
 
     for step in range(ITERS):
         parts = shares(corrs, left2, right2)
-        rows = LOCAL * B + 8 if step < ITERS - 1 else devices
+        rows = LOCAL * B + 8 if step < ITERS - 1 else 8
         (out,) = call(stats_kernel, "stats", [VM] * 6, [arr(rows, B)])(*parts, states[0], corrs[0], images[0])
-        if step == ITERS - 1:
-            got = exchange(out)
-        else:
-            core = from_core(out)
-            got = exchange_cores(out, core)
+        core = from_core(out)
+        got = exchange_cores(out, core)
+        if step < ITERS - 1:
             more = (out, from_chip(out), core)
             keeps = 3 if step < ITERS - 2 else 1
             (carry,) = call(

time: 213 us -> 212 us (level)
  blocking collectives: 100 us -> 96.6 us
  starting transfers between devices: 38.9 us -> 41.3 us
    all_to_all x1 -> x0, blocking collectives: 19.9 us -> none  [exchange(): lax.all_to_all(stats.reshape(-1, 1, B), ('sec', 'pair'), 0, 0)]
    all_to_all x4 -> x5, blocking collectives: 80.4 us -> 96.6 us  [exchange_cores(): lax.all_to_all(stats.reshape(-1, 1, B), ('sec', 'pair'), 0, 0, axis_index...]
    ppermute x5 -> x6, starting transfers between devices: 12.3 us -> 14.6 us  [from_core(): lax.ppermute(x, 'sec', [(i, i ^ 1) for i in range(lax.axis_size('sec'))])]
  transfers between devices with their start and end apart: 25 -> 26, of which waited for: 15 -> 16; matrix products, arithmetic and copies ran while one was open for 1% -> 1% of each run, Pallas kernels for 9% -> 9%
where the time goes in v5:
time: 212 us
  blocking collectives  96.6 us (46%)
  starting transfers between devices  41.3 us (19%)
  waiting for transfers between devices  33.9 us (16%)
  Pallas kernels  33.1 us (16%)
  local copies, waits for them, and re-layouts  3.42 us (2%)
    all_to_all x5, blocking collectives, exchange_cores(): lax.all_to_all(stats.reshape(-1, 1, B), ('sec', 'pair'), 0, 0, axis_index...  96.6 us
    ppermute x15, waiting for transfers between devices, swap(): return lax.ppermute(x, ('sec', 'pair'), perm)  32.6 us
    ppermute x15, starting transfers between devices, swap(): return lax.ppermute(x, ('sec', 'pair'), perm)  15.1 us
    ppermute x6, starting transfers between devices, from_core(): lax.ppermute(x, 'sec', [(i, i ^ 1) for i in range(lax.axis_size('sec'))])  14.6 us
    ppermute x5, starting transfers between devices, from_chip(): lax.ppermute(x, 'sec', [(i, i + 1 if i % 2 else i - 1) for i in range(1,...  11.5 us
    pallas_call x5, Pallas kernels, shares(): call(terms_kernel, 'terms', [SM] * 3 + [VM] * 5, [TERM_BLOCKS, BLOCK], [p...  9.46 us
    pallas_call x5, Pallas kernels, shares(): call(relayed_kernel, 'relayed', [SM] * 3 + [VM, ANY], [BLOCK])  5.9 us
    pallas_call x5, Pallas kernels, shares(): own, = call(own_kernel, 'own', [SM, SM, VM], [BLOCK])(group, weights, z)  5.89 us
  transfers between devices with their start and end apart: 26, of which 16 were waited for; matrix products, arithmetic and copies ran while one was open for 1% of the time, Pallas kernels for 9%

profile of v5, /device:TPU:1, one launch (start us, length us, event | category | flops | bytes accessed | tf_op | source)
XLA Modules:
  0.0 211.7 jit_solution(17173482510448541901)
XLA Ops:
  2.3 3.3 %collective-permute-start.1 = (f32[4,128,128]{2,1,0:T(8,128)S(1)}, f32[4,128,128]{2,1,0:T(8,128)S(1)}, u32[]{:S(2)}, u32[]{:S(2)}) collective-permute-start(f32[4,128,128]{2,1,0:T(8,128)S(1)} %mask.1.own.state.s0.refs_0_), channel_id=1, source_target_pairs={{0,4},{4,0},{8,12},{12,8},{16,20},{20,16},{24,28},{28,24},{32,36},... | collective-permute-start | bytes 786440 | tf_op jit(solution)/shard_map/ppermute | solution.py:305
  5.6 1.9 collective-permute-start
  13.3 1.9 terms.5
  15.2 1.7 collective-permute-start.3
  23.0 4.6 %collective-permute-done.2.direct = f32[4,128,128]{2,1,0:T(8,128)S(1)} collective-permute-done((f32[4,128,128]{2,1,0:T(8,128)S(1)}, f32[4,128,128]{2,1,0:T(8,128)S(1)}, u32[]{:S(2)}, u32[]{:S(2)}) %collective-permute-start.2) | collective-permute-done | bytes 262176 | tf_op jit(solution)/shard_map/ppermute | solution.py:296
  29.4 3.3 %collective-permute-start.6 = (f32[528,128]{1,0:T(8,128)S(1)}, f32[528,128]{1,0:T(8,128)S(1)}, u32[]{:S(2)}, u32[]{:S(2)}) collective-permute-start(f32[528,128]{1,0:T(8,128)S(1)} %first_stats.1.mine.pack0), channel_id=1, source_target_pairs={{4,8},{8,4},{12,16},{16,12},{20,24},{24,20},{28,32},{32,28},{36,40... | collective-permute-start | bytes 811016 | tf_op jit(solution)/shard_map/ppermute | solution.py:301
  32.7 26.5 %all_to_all.25 = f32[128,1,128]{2,1,0:T(1,128)S(1)} all-to-all(f32[128,1,128]{2,1,0:T(1,128)S(1)} %bitcast.28), channel_id=1, replica_groups={{0,1,2,3,8,9,10,11,16,17,18,19,24,25,26,27,32,33,34,35,40,41,42,43,48,4..., dimensions={0} | all-to-all | bytes 131072 | tf_op jit(solution)/shard_map/all_to_all | solution.py:312
  60.1 1.9 terms.6
  65.0 2.1 %collective-permute-start.7 = (f32[4,128,128]{2,1,0:T(8,128)S(1)}, f32[4,128,128]{2,1,0:T(8,128)S(1)}, u32[]{:S(2)}, u32[]{:S(2)}) collective-permute-start(f32[4,128,128]{2,1,0:T(8,128)S(1)} %direct.6.after), channel_id=1, source_target_pairs={{0,1},{1,0},{2,3},{3,2},{4,7},{5,6},{6,5},{7,4},{8,9},{9,8},{10,11... | collective-permute-start | bytes 786440 | tf_op jit(solution)/shard_map/ppermute | solution.py:296
  71.5 3.0 %collective-permute-done.9.relayed = f32[4,128,128]{2,1,0:T(8,128)S(1)} collective-permute-done((f32[4,128,128]{2,1,0:T(8,128)S(1)}, f32[4,128,128]{2,1,0:T(8,128)S(1)}, u32[]{:S(2)}, u32[]{:S(2)}) %collective-permute-start.9) | collective-permute-done | bytes 262176 | tf_op jit(solution)/shard_map/ppermute | solution.py:296
  74.8 2.5 %collective-permute-start.10 = (f32[520,128]{1,0:T(8,128)S(1)}, f32[520,128]{1,0:T(8,128)S(1)}, u32[]{:S(2)}, u32[]{:S(2)}) collective-permute-start(f32[520,128]{1,0:T(8,128)S(1)} %stats.4.mine.refs_12_), channel_id=1, source_target_pairs={{0,4},{4,0},{8,12},{12,8},{16,20},{20,16},{24,28},{28,24},{32,36},... | collective-permute-start | bytes 798728 | tf_op jit(solution)/shard_map/ppermute | solution.py:305
  77.3 2.1 collective-permute-start.11
  79.4 18.0 %all_to_all.26 = f32[128,1,128]{2,1,0:T(1,128)S(1)} all-to-all(f32[128,1,128]{2,1,0:T(1,128)S(1)} %bitcast.29), channel_id=1, replica_groups={{0,1,2,3,8,9,10,11,16,17,18,19,24,25,26,27,32,33,34,35,40,41,42,43,48,4..., dimensions={0} | all-to-all | bytes 131072 | tf_op jit(solution)/shard_map/all_to_all | solution.py:312
  98.0 1.9 terms.7
  102.9 2.2 %collective-permute-start.12 = (f32[4,128,128]{2,1,0:T(8,128)S(1)}, f32[4,128,128]{2,1,0:T(8,128)S(1)}, u32[]{:S(2)}, u32[]{:S(2)}) collective-permute-start(f32[4,128,128]{2,1,0:T(8,128)S(1)} %direct.7.after), channel_id=1, source_target_pairs={{0,1},{1,0},{2,3},{3,2},{4,7},{5,6},{6,5},{7,4},{8,9},{9,8},{10,11... | collective-permute-start | bytes 786440 | tf_op jit(solution)/shard_map/ppermute | solution.py:296
  109.5 3.8 %collective-permute-done.14.relayed = f32[4,128,128]{2,1,0:T(8,128)S(1)} collective-permute-done((f32[4,128,128]{2,1,0:T(8,128)S(1)}, f32[4,128,128]{2,1,0:T(8,128)S(1)}, u32[]{:S(2)}, u32[]{:S(2)}) %collective-permute-start.14) | collective-permute-done | bytes 262176 | tf_op jit(solution)/shard_map/ppermute | solution.py:296
  113.5 2.4 %collective-permute-start.15 = (f32[520,128]{1,0:T(8,128)S(1)}, f32[520,128]{1,0:T(8,128)S(1)}, u32[]{:S(2)}, u32[]{:S(2)}) collective-permute-start(f32[520,128]{1,0:T(8,128)S(1)} %stats.5.mine.refs_12_), channel_id=1, source_target_pairs={{0,4},{4,0},{8,12},{12,8},{16,20},{20,16},{24,28},{28,24},{32,36},... | collective-permute-start | bytes 798728 | tf_op jit(solution)/shard_map/ppermute | solution.py:305
  115.9 2.1 %collective-permute-start.16 = (f32[520,128]{1,0:T(8,128)S(1)}, f32[520,128]{1,0:T(8,128)S(1)}, u32[]{:S(2)}, u32[]{:S(2)}) collective-permute-start(f32[520,128]{1,0:T(8,128)S(1)} %stats.5.mine.refs_12_), channel_id=1, source_target_pairs={{4,8},{8,4},{12,16},{16,12},{20,24},{24,20},{28,32},{32,28},{36,40... | collective-permute-start | bytes 798728 | tf_op jit(solution)/shard_map/ppermute | solution.py:301
  118.0 18.0 %all_to_all.27 = f32[128,1,128]{2,1,0:T(1,128)S(1)} all-to-all(f32[128,1,128]{2,1,0:T(1,128)S(1)} %bitcast.30), channel_id=1, replica_groups={{0,1,2,3,8,9,10,11,16,17,18,19,24,25,26,27,32,33,34,35,40,41,42,43,48,4..., dimensions={0} | all-to-all | bytes 131072 | tf_op jit(solution)/shard_map/all_to_all | solution.py:312
  136.7 1.9 terms.8
  141.8 2.1 %collective-permute-start.17 = (f32[4,128,128]{2,1,0:T(8,128)S(1)}, f32[4,128,128]{2,1,0:T(8,128)S(1)}, u32[]{:S(2)}, u32[]{:S(2)}) collective-permute-start(f32[4,128,128]{2,1,0:T(8,128)S(1)} %direct.8.after), channel_id=1, source_target_pairs={{0,1},{1,0},{2,3},{3,2},{4,7},{5,6},{6,5},{7,4},{8,9},{9,8},{10,11... | collective-permute-start | bytes 786440 | tf_op jit(solution)/shard_map/ppermute | solution.py:296
  146.6 1.7 collective-permute-done.17.direct
  148.3 3.9 %collective-permute-done.19.relayed = f32[4,128,128]{2,1,0:T(8,128)S(1)} collective-permute-done((f32[4,128,128]{2,1,0:T(8,128)S(1)}, f32[4,128,128]{2,1,0:T(8,128)S(1)}, u32[]{:S(2)}, u32[]{:S(2)}) %collective-permute-start.19) | collective-permute-done | bytes 262176 | tf_op jit(solution)/shard_map/ppermute | solution.py:296
  152.5 2.4 %collective-permute-start.20 = (f32[520,128]{1,0:T(8,128)S(1)}, f32[520,128]{1,0:T(8,128)S(1)}, u32[]{:S(2)}, u32[]{:S(2)}) collective-permute-start(f32[520,128]{1,0:T(8,128)S(1)} %stats.6.mine.refs_12_), channel_id=1, source_target_pairs={{0,4},{4,0},{8,12},{12,8},{16,20},{20,16},{24,28},{28,24},{32,36},... | collective-permute-start | bytes 798728 | tf_op jit(solution)/shard_map/ppermute | solution.py:305
  154.8 2.1 %collective-permute-start.21 = (f32[520,128]{1,0:T(8,128)S(1)}, f32[520,128]{1,0:T(8,128)S(1)}, u32[]{:S(2)}, u32[]{:S(2)}) collective-permute-start(f32[520,128]{1,0:T(8,128)S(1)} %stats.6.mine.refs_12_), channel_id=1, source_target_pairs={{4,8},{8,4},{12,16},{16,12},{20,24},{24,20},{28,32},{32,28},{36,40... | collective-permute-start | bytes 798728 | tf_op jit(solution)/shard_map/ppermute | solution.py:301
  157.0 18.0 %all_to_all.28 = f32[128,1,128]{2,1,0:T(1,128)S(1)} all-to-all(f32[128,1,128]{2,1,0:T(1,128)S(1)} %bitcast.31), channel_id=1, replica_groups={{0,1,2,3,8,9,10,11,16,17,18,19,24,25,26,27,32,33,34,35,40,41,42,43,48,4..., dimensions={0} | all-to-all | bytes 131072 | tf_op jit(solution)/shard_map/all_to_all | solution.py:312
  175.6 1.9 terms.9
  180.5 2.1 %collective-permute-start.22 = (f32[4,128,128]{2,1,0:T(8,128)S(1)}, f32[4,128,128]{2,1,0:T(8,128)S(1)}, u32[]{:S(2)}, u32[]{:S(2)}) collective-permute-start(f32[4,128,128]{2,1,0:T(8,128)S(1)} %direct.9.after), channel_id=1, source_target_pairs={{0,1},{1,0},{2,3},{3,2},{4,7},{5,6},{6,5},{7,4},{8,9},{9,8},{10,11... | collective-permute-start | bytes 786440 | tf_op jit(solution)/shard_map/ppermute | solution.py:296
  185.3 1.7 collective-permute-done.22.direct
  187.0 3.9 %collective-permute-done.24.relayed = f32[4,128,128]{2,1,0:T(8,128)S(1)} collective-permute-done((f32[4,128,128]{2,1,0:T(8,128)S(1)}, f32[4,128,128]{2,1,0:T(8,128)S(1)}, u32[]{:S(2)}, u32[]{:S(2)}) %collective-permute-start.24) | collective-permute-done | bytes 262176 | tf_op jit(solution)/shard_map/ppermute | solution.py:296
  191.1 2.4 %collective-permute-start.25 = (f32[8,128]{1,0:T(8,128)S(1)}, f32[8,128]{1,0:T(8,128)S(1)}, u32[]{:S(2)}, u32[]{:S(2)}) collective-permute-start(f32[8,128]{1,0:T(8,128)S(1)} %stats.7.mine), channel_id=1, source_target_pairs={{0,4},{4,0},{8,12},{12,8},{16,20},{20,16},{24,28},{28,24},{32,36},... | collective-permute-start | bytes 12296 | tf_op jit(solution)/shard_map/ppermute | solution.py:305
  194.3 16.2 %all_to_all.29 = f32[128,1,128]{2,1,0:T(1,128)S(1)} all-to-all(f32[128,1,128]{2,1,0:T(1,128)S(1)} %bitcast.35), channel_id=1, replica_groups={{0,1,2,3,8,9,10,11,16,17,18,19,24,25,26,27,32,33,34,35,40,41,42,43,48,4..., dimensions={0} | all-to-all | bytes 131072 | tf_op jit(solution)/shard_map/all_to_all | solution.py:312
  (81 shorter events, 46.4 us)
Async XLA Ops:
  1.3 1.0 copy-start.2
  2.3 10.5 %collective-permute-start.1 = (f32[4,128,128]{2,1,0:T(8,128)S(1)}, f32[4,128,128]{2,1,0:T(8,128)S(1)}, u32[]{:S(2)}, u32[]{:S(2)}) collective-permute-start(f32[4,128,128]{2,1,0:T(8,128)S(1)} %mask.1.own.state.s0.refs_0_), channel_id=1, source_target_pairs={{0,4},{4,0},{8,12},{12,8},{16,20},{20,16},{24,28},{28,24},{32,36},... | collective-permute-start | bytes 786440 | tf_op jit(solution)/shard_map/ppermute | solution.py:305
  5.6 7.7 %collective-permute-start = (f32[4,128,128]{2,1,0:T(8,128)S(1)}, f32[4,128,128]{2,1,0:T(8,128)S(1)}, u32[]{:S(2)}, u32[]{:S(2)}) collective-permute-start(f32[4,128,128]{2,1,0:T(8,128)S(1)} %mask.1.own.state.s0.refs_0_), channel_id=1, source_target_pairs={{4,8},{8,4},{12,16},{16,12},{20,24},{24,20},{28,32},{32,28},{36,40... | collective-permute-start | bytes 786440 | tf_op jit(solution)/shard_map/ppermute | solution.py:301
  9.1 1.4 copy-start
  10.5 1.0 copy-start.1
  15.2 6.5 %collective-permute-start.3 = (f32[4,128,128]{2,1,0:T(8,128)S(1)}, f32[4,128,128]{2,1,0:T(8,128)S(1)}, u32[]{:S(2)}, u32[]{:S(2)}) collective-permute-start(f32[4,128,128]{2,1,0:T(8,128)S(1)} %get-tuple-element.53), channel_id=1, source_target_pairs={{0,1},{1,0},{2,3},{3,2},{4,7},{5,6},{6,5},{7,4},{8,9},{9,8},{10,11... | collective-permute-start | bytes 786440 | tf_op jit(solution)/shard_map/ppermute | solution.py:296
  19.2 8.3 %collective-permute-start.2 = (f32[4,128,128]{2,1,0:T(8,128)S(1)}, f32[4,128,128]{2,1,0:T(8,128)S(1)}, u32[]{:S(2)}, u32[]{:S(2)}) collective-permute-start(f32[4,128,128]{2,1,0:T(8,128)S(1)} %direct.5.after), channel_id=1, source_target_pairs={{0,1},{1,0},{2,3},{3,2},{4,7},{5,6},{6,5},{7,4},{8,9},{9,8},{10,11... | collective-permute-start | bytes 786440 | tf_op jit(solution)/shard_map/ppermute | solution.py:296
  21.7 5.8 %collective-permute-start.4 = (f32[4,128,128]{2,1,0:T(8,128)S(1)}, f32[4,128,128]{2,1,0:T(8,128)S(1)}, u32[]{:S(2)}, u32[]{:S(2)}) collective-permute-start(f32[4,128,128]{2,1,0:T(8,128)S(1)} %relay.5), channel_id=1, source_target_pairs={{0,3},{1,2},{2,1},{3,0},{4,5},{5,4},{6,7},{7,6},{8,11},{9,10},{10,... | collective-permute-start | bytes 786440 | tf_op jit(solution)/shard_map/ppermute | solution.py:296
  27.7 5.0 %collective-permute-start.5 = (f32[528,128]{1,0:T(8,128)S(1)}, f32[528,128]{1,0:T(8,128)S(1)}, u32[]{:S(2)}, u32[]{:S(2)}) collective-permute-start(f32[528,128]{1,0:T(8,128)S(1)} %first_stats.1.mine.pack0), channel_id=1, source_target_pairs={{0,4},{4,0},{8,12},{12,8},{16,20},{20,16},{24,28},{28,24},{32,36},... | collective-permute-start | bytes 811016 | tf_op jit(solution)/shard_map/ppermute | solution.py:305
  29.4 29.9 %collective-permute-start.6 = (f32[528,128]{1,0:T(8,128)S(1)}, f32[528,128]{1,0:T(8,128)S(1)}, u32[]{:S(2)}, u32[]{:S(2)}) collective-permute-start(f32[528,128]{1,0:T(8,128)S(1)} %first_stats.1.mine.pack0), channel_id=1, source_target_pairs={{4,8},{8,4},{12,16},{16,12},{20,24},{24,20},{28,32},{32,28},{36,40... | collective-permute-start | bytes 811016 | tf_op jit(solution)/shard_map/ppermute | solution.py:301
  62.0 6.5 %collective-permute-start.8 = (f32[4,128,128]{2,1,0:T(8,128)S(1)}, f32[4,128,128]{2,1,0:T(8,128)S(1)}, u32[]{:S(2)}, u32[]{:S(2)}) collective-permute-start(f32[4,128,128]{2,1,0:T(8,128)S(1)} %get-tuple-element.61), channel_id=1, source_target_pairs={{0,1},{1,0},{2,3},{3,2},{4,7},{5,6},{6,5},{7,4},{8,9},{9,8},{10,11... | collective-permute-start | bytes 786440 | tf_op jit(solution)/shard_map/ppermute | solution.py:296
  65.0 6.5 %collective-permute-start.7 = (f32[4,128,128]{2,1,0:T(8,128)S(1)}, f32[4,128,128]{2,1,0:T(8,128)S(1)}, u32[]{:S(2)}, u32[]{:S(2)}) collective-permute-start(f32[4,128,128]{2,1,0:T(8,128)S(1)} %direct.6.after), channel_id=1, source_target_pairs={{0,1},{1,0},{2,3},{3,2},{4,7},{5,6},{6,5},{7,4},{8,9},{9,8},{10,11... | collective-permute-start | bytes 786440 | tf_op jit(solution)/shard_map/ppermute | solution.py:296
  68.5 6.0 %collective-permute-start.9 = (f32[4,128,128]{2,1,0:T(8,128)S(1)}, f32[4,128,128]{2,1,0:T(8,128)S(1)}, u32[]{:S(2)}, u32[]{:S(2)}) collective-permute-start(f32[4,128,128]{2,1,0:T(8,128)S(1)} %relay.6), channel_id=1, source_target_pairs={{0,3},{1,2},{2,1},{3,0},{4,5},{5,4},{6,7},{7,6},{8,11},{9,10},{10,... | collective-permute-start | bytes 786440 | tf_op jit(solution)/shard_map/ppermute | solution.py:296
  74.8 4.6 %collective-permute-start.10 = (f32[520,128]{1,0:T(8,128)S(1)}, f32[520,128]{1,0:T(8,128)S(1)}, u32[]{:S(2)}, u32[]{:S(2)}) collective-permute-start(f32[520,128]{1,0:T(8,128)S(1)} %stats.4.mine.refs_12_), channel_id=1, source_target_pairs={{0,4},{4,0},{8,12},{12,8},{16,20},{20,16},{24,28},{28,24},{32,36},... | collective-permute-start | bytes 798728 | tf_op jit(solution)/shard_map/ppermute | solution.py:305
  77.3 20.3 %collective-permute-start.11 = (f32[520,128]{1,0:T(8,128)S(1)}, f32[520,128]{1,0:T(8,128)S(1)}, u32[]{:S(2)}, u32[]{:S(2)}) collective-permute-start(f32[520,128]{1,0:T(8,128)S(1)} %stats.4.mine.refs_12_), channel_id=1, source_target_pairs={{4,8},{8,4},{12,16},{16,12},{20,24},{24,20},{28,32},{32,28},{36,40... | collective-permute-start | bytes 798728 | tf_op jit(solution)/shard_map/ppermute | solution.py:301
  99.9 6.5 %collective-permute-start.13 = (f32[4,128,128]{2,1,0:T(8,128)S(1)}, f32[4,128,128]{2,1,0:T(8,128)S(1)}, u32[]{:S(2)}, u32[]{:S(2)}) collective-permute-start(f32[4,128,128]{2,1,0:T(8,128)S(1)} %get-tuple-element.71), channel_id=1, source_target_pairs={{0,1},{1,0},{2,3},{3,2},{4,7},{5,6},{6,5},{7,4},{8,9},{9,8},{10,11... | collective-permute-start | bytes 786440 | tf_op jit(solution)/shard_map/ppermute | solution.py:296
  102.9 6.5 %collective-permute-start.12 = (f32[4,128,128]{2,1,0:T(8,128)S(1)}, f32[4,128,128]{2,1,0:T(8,128)S(1)}, u32[]{:S(2)}, u32[]{:S(2)}) collective-permute-start(f32[4,128,128]{2,1,0:T(8,128)S(1)} %direct.7.after), channel_id=1, source_target_pairs={{0,1},{1,0},{2,3},{3,2},{4,7},{5,6},{6,5},{7,4},{8,9},{9,8},{10,11... | collective-permute-start | bytes 786440 | tf_op jit(solution)/shard_map/ppermute | solution.py:296
  106.5 6.8 %collective-permute-start.14 = (f32[4,128,128]{2,1,0:T(8,128)S(1)}, f32[4,128,128]{2,1,0:T(8,128)S(1)}, u32[]{:S(2)}, u32[]{:S(2)}) collective-permute-start(f32[4,128,128]{2,1,0:T(8,128)S(1)} %relay.7), channel_id=1, source_target_pairs={{0,3},{1,2},{2,1},{3,0},{4,5},{5,4},{6,7},{7,6},{8,11},{9,10},{10,... | collective-permute-start | bytes 786440 | tf_op jit(solution)/shard_map/ppermute | solution.py:296
  113.5 4.5 %collective-permute-start.15 = (f32[520,128]{1,0:T(8,128)S(1)}, f32[520,128]{1,0:T(8,128)S(1)}, u32[]{:S(2)}, u32[]{:S(2)}) collective-permute-start(f32[520,128]{1,0:T(8,128)S(1)} %stats.5.mine.refs_12_), channel_id=1, source_target_pairs={{0,4},{4,0},{8,12},{12,8},{16,20},{20,16},{24,28},{28,24},{32,36},... | collective-permute-start | bytes 798728 | tf_op jit(solution)/shard_map/ppermute | solution.py:305
  115.9 20.3 %collective-permute-start.16 = (f32[520,128]{1,0:T(8,128)S(1)}, f32[520,128]{1,0:T(8,128)S(1)}, u32[]{:S(2)}, u32[]{:S(2)}) collective-permute-start(f32[520,128]{1,0:T(8,128)S(1)} %stats.5.mine.refs_12_), channel_id=1, source_target_pairs={{4,8},{8,4},{12,16},{16,12},{20,24},{24,20},{28,32},{32,28},{36,40... | collective-permute-start | bytes 798728 | tf_op jit(solution)/shard_map/ppermute | solution.py:301
  138.6 6.7 %collective-permute-start.18 = (f32[4,128,128]{2,1,0:T(8,128)S(1)}, f32[4,128,128]{2,1,0:T(8,128)S(1)}, u32[]{:S(2)}, u32[]{:S(2)}) collective-permute-start(f32[4,128,128]{2,1,0:T(8,128)S(1)} %get-tuple-element.82), channel_id=1, source_target_pairs={{0,1},{1,0},{2,3},{3,2},{4,7},{5,6},{6,5},{7,4},{8,9},{9,8},{10,11... | collective-permute-start | bytes 786440 | tf_op jit(solution)/shard_map/ppermute | solution.py:296
  141.8 6.5 %collective-permute-start.17 = (f32[4,128,128]{2,1,0:T(8,128)S(1)}, f32[4,128,128]{2,1,0:T(8,128)S(1)}, u32[]{:S(2)}, u32[]{:S(2)}) collective-permute-start(f32[4,128,128]{2,1,0:T(8,128)S(1)} %direct.8.after), channel_id=1, source_target_pairs={{0,1},{1,0},{2,3},{3,2},{4,7},{5,6},{6,5},{7,4},{8,9},{9,8},{10,11... | collective-permute-start | bytes 786440 | tf_op jit(solution)/shard_map/ppermute | solution.py:296
  145.3 6.9 %collective-permute-start.19 = (f32[4,128,128]{2,1,0:T(8,128)S(1)}, f32[4,128,128]{2,1,0:T(8,128)S(1)}, u32[]{:S(2)}, u32[]{:S(2)}) collective-permute-start(f32[4,128,128]{2,1,0:T(8,128)S(1)} %relay.8), channel_id=1, source_target_pairs={{0,3},{1,2},{2,1},{3,0},{4,5},{5,4},{6,7},{7,6},{8,11},{9,10},{10,... | collective-permute-start | bytes 786440 | tf_op jit(solution)/shard_map/ppermute | solution.py:296
  152.5 4.5 %collective-permute-start.20 = (f32[520,128]{1,0:T(8,128)S(1)}, f32[520,128]{1,0:T(8,128)S(1)}, u32[]{:S(2)}, u32[]{:S(2)}) collective-permute-start(f32[520,128]{1,0:T(8,128)S(1)} %stats.6.mine.refs_12_), channel_id=1, source_target_pairs={{0,4},{4,0},{8,12},{12,8},{16,20},{20,16},{24,28},{28,24},{32,36},... | collective-permute-start | bytes 798728 | tf_op jit(solution)/shard_map/ppermute | solution.py:305
  154.8 20.3 %collective-permute-start.21 = (f32[520,128]{1,0:T(8,128)S(1)}, f32[520,128]{1,0:T(8,128)S(1)}, u32[]{:S(2)}, u32[]{:S(2)}) collective-permute-start(f32[520,128]{1,0:T(8,128)S(1)} %stats.6.mine.refs_12_), channel_id=1, source_target_pairs={{4,8},{8,4},{12,16},{16,12},{20,24},{24,20},{28,32},{32,28},{36,40... | collective-permute-start | bytes 798728 | tf_op jit(solution)/shard_map/ppermute | solution.py:301
  177.5 6.5 %collective-permute-start.23 = (f32[4,128,128]{2,1,0:T(8,128)S(1)}, f32[4,128,128]{2,1,0:T(8,128)S(1)}, u32[]{:S(2)}, u32[]{:S(2)}) collective-permute-start(f32[4,128,128]{2,1,0:T(8,128)S(1)} %get-tuple-element.93), channel_id=1, source_target_pairs={{0,1},{1,0},{2,3},{3,2},{4,7},{5,6},{6,5},{7,4},{8,9},{9,8},{10,11... | collective-permute-start | bytes 786440 | tf_op jit(solution)/shard_map/ppermute | solution.py:296
  180.5 6.5 %collective-permute-start.22 = (f32[4,128,128]{2,1,0:T(8,128)S(1)}, f32[4,128,128]{2,1,0:T(8,128)S(1)}, u32[]{:S(2)}, u32[]{:S(2)}) collective-permute-start(f32[4,128,128]{2,1,0:T(8,128)S(1)} %direct.9.after), channel_id=1, source_target_pairs={{0,1},{1,0},{2,3},{3,2},{4,7},{5,6},{6,5},{7,4},{8,9},{9,8},{10,11... | collective-permute-start | bytes 786440 | tf_op jit(solution)/shard_map/ppermute | solution.py:296
  184.0 6.9 %collective-permute-start.24 = (f32[4,128,128]{2,1,0:T(8,128)S(1)}, f32[4,128,128]{2,1,0:T(8,128)S(1)}, u32[]{:S(2)}, u32[]{:S(2)}) collective-permute-start(f32[4,128,128]{2,1,0:T(8,128)S(1)} %relay.9), channel_id=1, source_target_pairs={{0,3},{1,2},{2,1},{3,0},{4,5},{5,4},{6,7},{7,6},{8,11},{9,10},{10,... | collective-permute-start | bytes 786440 | tf_op jit(solution)/shard_map/ppermute | solution.py:296
  191.1 3.2 %collective-permute-start.25 = (f32[8,128]{1,0:T(8,128)S(1)}, f32[8,128]{1,0:T(8,128)S(1)}, u32[]{:S(2)}, u32[]{:S(2)}) collective-permute-start(f32[8,128]{1,0:T(8,128)S(1)} %stats.7.mine), channel_id=1, source_target_pairs={{0,4},{4,0},{8,12},{12,8},{16,20},{20,16},{24,28},{28,24},{32,36},... | collective-permute-start | bytes 12296 | tf_op jit(solution)/shard_map/ppermute | solution.py:305
